TPU v7x, 32 devices: a whole 2x2x4 slice. The times are simulated.
32 devices in a mesh: leaf: 8 (over z, y), grp: 4 (over x, core).
Axes of the slice: x: 2, y: 2, z: 4, core: 2. Of those that a mesh axis runs over, the one named last changes fastest.
Arguments:
- vectors: bfloat16 [32, 65536], P(None, ('leaf', 'grp')), may hold values from -6 to 6
- leaf_basis: bfloat16 [256, 64, 256], P(('leaf', 'grp')), may hold values from -0.375 to 0.375
- transfer: float32 [2, 64, 64], replicated, may hold values from -0.625 to 0.625
- sibling_coupling: float32 [2, 64, 64], replicated, may hold values from -0.75 to 0.75
- list_coupling: float32 [8, 64, 64], replicated, may hold values from -0.4375 to 0.4375
- near_tiles: bfloat16 [512, 256, 256], P(('leaf', 'grp')), may hold values from -0.375 to 0.375
- tile_target: int32 [512], P(('leaf', 'grp')), may hold values from 0 to 7
- tile_source: int32 [512], P(('leaf', 'grp')), may hold values from 0 to 23, as said below
- tile_count: int32 [32], P(('leaf', 'grp')), may hold values from 8 to 16, as said below
- couple_offset: int32 [32, 3], P(('leaf', 'grp')), may hold values from -2 to 2, as said below
- couple_class: int32 [32, 3], P(('leaf', 'grp')), may hold values from 0 to 7
Outputs:
- field: float32 [32, 65536], P(None, ('leaf', 'grp'))
Inputs may be any that keep to these rules, and one draw needn't show every extreme that they name: Only a device's first tile_count slots hold live tiles; some device uses all 16 slots. `tile_source`: over all 16 slots of a device, live or not, the sources in the window's first 8 boxes name at most 4 distinct boxes, and so do those in its last 8 boxes; on every device the live tiles name 4 boxes on both sides. `couple_offset`: never zero.
All inputs are finite; a program needn't handle non-finite values.
Results may differ from a plain program's by a relative error of at most 0.0024.
Values may be sent and summed in bfloat16 or wider, within the bound.
No kernel may reach another device: no remote copies, remote signals or barrier semaphores. Data moves between devices by JAX's collectives and lax.ppermute only.
A program may use at most 64 MiB of HBM per device.

v0:
```python
import functools

import jax
import jax.numpy as jnp
from jax import lax
from jax.experimental import pallas as pl
from jax.experimental.pallas import tpu as pltpu
from jax.sharding import PartitionSpec as P

AXES = ("leaf", "grp")
F32 = jnp.float32
BF16 = jnp.bfloat16
NN = (((1,), (0,)), ((), ()))
NT = (((1,), (1,)), ((), ()))
CHUNK = 512
VMEM_LIMIT = 48 * 2**20


def split(x):
    high = x.astype(BF16)
    return high, (x - high.astype(F32)).astype(BF16)


def dot(a, b, dims=NN):
    return lax.dot_general(a, b, dims, preferred_element_type=F32)


def dot3(a, b, dims=NN):
    a_high, a_low = split(a)
    b_high, b_low = split(b)
    return dot(a_high, b_high, dims) + (dot(a_low, b_high, dims) + dot(a_high, b_low, dims))


def rounds_of(bits):
    rounds = []
    top = bits
    while top > 0:
        wide = 2 if top > 1 else 1
        rounds.append((top - wide, wide))
        top -= wide
    return rounds


def masks_of(bits):
    masks = [0]
    for low, wide in rounds_of(bits):
        masks = [mask ^ (step << low) for step in range(2**wide) for mask in masks]
    return masks


def place_of(mask, bits):
    place, shift = 0, 0
    for low, wide in rounds_of(bits):
        place = place | (((mask >> low) & (2**wide - 1)) << shift)
        shift += wide
    return place


def up(blocks, transfer):
    left = jnp.concatenate(blocks[0::2], axis=0)
    right = jnp.concatenate(blocks[1::2], axis=0)
    rows = blocks[0].shape[0]
    total = dot3(left, transfer[0]) + dot3(right, transfer[1])
    return [total[i * rows : (i + 1) * rows] for i in range(len(blocks) // 2)]


def leaf_kernel(vectors, basis, transfer, send, leaf):
    boxes, _, points = basis.shape
    level = []
    for b in range(boxes):
        level.append(dot(vectors[:, b * points : (b + 1) * points], basis[b], NT))
        leaf[b] = level[b]
    pair = (transfer[0], transfer[1])
    while len(level) > 1:
        level = up(level, pair)
    send[0] = jnp.concatenate(split(level[0]), axis=1)


def map_kernel(bits, device, offsets, classes, leaf, transfer, sibling, coupling, maps, spread, local, stack):
    boxes, columns, rank = leaf.shape
    me = device[0]
    count = 2**bits
    places = {mask: k for k, mask in enumerate(masks_of(bits))}
    t0, t1 = transfer[0], transfer[1]
    s0, s1 = sibling[0], sibling[1]

    def put(at, block):
        both = jnp.concatenate(split(block), axis=1)
        maps[pl.ds(at, rank)] = both
        maps[pl.ds(at + rank, rank)] = both

    put(0, jnp.zeros((rank, rank), F32))
    for height in range(bits):
        mine = (me >> height) & 1
        rows = 2**height * rank
        if height == 0:
            put(places[1] * 2 * rank, sibling[mine])
            stack[0:rank] = transfer[mine]
            stack[rank : 2 * rank] = transfer[1 - mine]
            continue
        bridge = dot3(sibling[mine], stack[0:rank], NT)
        near, far = transfer[mine], transfer[1 - mine]
        for start in range(0, rows, CHUNK):
            size = min(CHUNK, rows - start)
            part = stack[start : start + size]
            block = dot3(part, bridge)
            for i in range(size // rank):
                at = places[2**height + start // rank + i] * 2 * rank
                put(at, block[i * rank : (i + 1) * rank])
            if height + 1 < bits:
                stack[rows + start : rows + start + size] = dot3(part, far)
                stack[start : start + size] = dot3(part, near)
    for i in range(offsets.shape[1]):
        mask = ((me + offsets[0, i] + count) & (count - 1)) ^ me
        at = pl.multiple_of(place_of(mask, bits) * 2 * rank, 2 * rank)
        both = maps[pl.ds(at, rank)].astype(F32)
        put(at, both[:, :rank] + both[:, rank:] + coupling[classes[0, i]])

    levels = [[leaf[b] for b in range(boxes)]]
    while len(levels[-1]) > 2:
        levels.append(up(levels[-1], (t0, t1)))
    down = None
    paths = [None]
    for level in reversed(levels):
        across0 = dot3(jnp.concatenate(level[1::2], axis=0), s0)
        across1 = dot3(jnp.concatenate(level[0::2], axis=0), s1)
        if down is not None:
            parents = jnp.concatenate(down, axis=0)
            across0 = across0 + dot3(parents, t0, NT)
            across1 = across1 + dot3(parents, t1, NT)
        down = []
        for i in range(len(level) // 2):
            down.append(across0[i * columns : (i + 1) * columns])
            down.append(across1[i * columns : (i + 1) * columns])
        if paths[0] is None:
            paths = [t0.T, t1.T]
        else:
            tall = jnp.concatenate(paths, axis=0)
            left, right = dot3(tall, t0, NT), dot3(tall, t1, NT)
            paths = []
            for i in range(len(level) // 2):
                paths.append(left[i * rank : (i + 1) * rank])
                paths.append(right[i * rank : (i + 1) * rank])
    for b in range(boxes):
        local[:, b * rank : (b + 1) * rank] = down[b]
        high, low = split(paths[b])
        for half in range(2):
            rows = slice(half * rank, (half + 1) * rank)
            spread[rows, b * rank : (b + 1) * rank] = high
            spread[rows, (boxes + b) * rank : (boxes + b + 1) * rank] = low


def near_kernel(live, targets, sources, before, own, after, tiles, near, window):
    slots, points, _ = tiles.shape
    boxes = near.shape[0]
    for i, part in enumerate((before, own, after)):
        for b in range(boxes):
            window[i * boxes + b] = part[:, b * points : (b + 1) * points]
    near[...] = jnp.zeros_like(near)
    for slot in range(slots):
        source = window[sources[slot]]
        source = jnp.where(slot < live[0], source, jnp.zeros_like(source))
        target = targets[slot]
        near[target] = near[target] + dot(source, tiles[slot])


def field_kernel(gathered, maps, spread, local, basis, near, field):
    count = gathered.shape[0]
    boxes, rank, points = basis.shape
    pairs = count // 2
    wide = 4 * rank

    def step(k):
        coeffs = jnp.concatenate([gathered[2 * k], gathered[2 * k + 1]], axis=1)
        return dot(coeffs, maps[pl.ds(k * wide, wide)])

    if pairs <= 32:
        both = step(0)
        for k in range(1, pairs):
            both = both + step(k)
    else:
        both = lax.fori_loop(1, pairs, lambda k, sums: sums + step(k), step(0))
    summit = both[:, :rank] + both[:, rank:]
    doubled = dot(jnp.concatenate(split(summit), axis=1), spread[...])
    half = boxes * rank
    rounded = (doubled[:, :half] + doubled[:, half:] + local[...]).astype(BF16)
    for b in range(boxes):
        far = dot(rounded[:, b * rank : (b + 1) * rank], basis[b])
        field[:, b * points : (b + 1) * points] = near[b] + far


def call(kernel, name, outs, kinds, args, scratch=(), flops=0):
    spaces = {"v": pltpu.VMEM, "s": pltpu.SMEM}
    moved = sum(x.size * x.dtype.itemsize for x in args)
    return pl.pallas_call(
        kernel,
        name=name,
        out_shape=outs,
        in_specs=[pl.BlockSpec(memory_space=spaces[kind]) for kind in kinds],
        out_specs=jax.tree.map(lambda _: pl.BlockSpec(memory_space=pltpu.VMEM), outs),
        scratch_shapes=list(scratch),
        compiler_params=pltpu.CompilerParams(vmem_limit_bytes=VMEM_LIMIT),
        cost_estimate=pl.CostEstimate(flops=flops, bytes_accessed=moved, transcendentals=0),
    )(*args)


def body(
    vectors,
    leaf_basis,
    transfer,
    sibling_coupling,
    list_coupling,
    near_tiles,
    tile_target,
    tile_source,
    tile_count,
    couple_offset,
    couple_class,
):
    columns, width = vectors.shape
    boxes, rank, points = leaf_basis.shape
    count = lax.axis_size(AXES)
    bits = count.bit_length() - 1
    shape = jax.ShapeDtypeStruct

    def send(x, target):
        return lax.ppermute(x, AXES, [(i, target(i)) for i in range(count)])

    coeffs, leaf = call(
        leaf_kernel,
        "leaf",
        (shape((1, columns, 2 * rank), BF16), shape((boxes, columns, rank), F32)),
        "vvv",
        (vectors, leaf_basis, transfer),
    )
    before = send(vectors, lambda i: (i + 1) % count)
    after = send(vectors, lambda i: (i - 1) % count)
    device = lax.axis_index(AXES).astype(jnp.int32).reshape(1)
    maps, spread, local = call(
        functools.partial(map_kernel, bits),
        "maps",
        (
            shape((count * 2 * rank, 2 * rank), BF16),
            shape((2 * rank, 2 * boxes * rank), BF16),
            shape((columns, boxes * rank), F32),
        ),
        "sssvvvv",
        (device, couple_offset, couple_class, leaf, transfer, sibling_coupling, list_coupling),
        scratch=(pltpu.VMEM((count // 2 * rank, rank), F32),),
    )
    near = call(
        near_kernel,
        "near",
        shape((boxes, columns, points), F32),
        "sssvvvv",
        (tile_count, tile_target, tile_source, before, vectors, after, near_tiles),
        scratch=(pltpu.VMEM((3 * boxes, columns, points), BF16),),
    )
    gathered = coeffs
    for low, wide in rounds_of(bits):
        parts = [gathered]
        for step in range(1, 2**wide):
            parts.append(send(gathered, lambda i, mask=step << low: i ^ mask))
        gathered = jnp.concatenate(parts, axis=0)
    return call(
        field_kernel,
        "field",
        shape((columns, width), F32),
        "vvvvvv",
        (gathered, maps, spread, local, leaf_basis, near),
    )


def solution(mesh):
    in_specs = (
        P(None, AXES),
        P(AXES, None, None),
        P(),
        P(),
        P(),
        P(AXES, None, None),
        P(AXES),
        P(AXES),
        P(AXES),
        P(AXES, None),
        P(AXES, None),
    )
    return jax.shard_map(body, mesh=mesh, in_specs=in_specs, out_specs=P(None, AXES), check_vma=False)
```

profile of v0, /device:TPU:0, one launch (start us, length us, event | category | flops | bytes accessed | tf_op | source)
XLA Modules:
  0.0 39.0 jit_solution(6440174722350413604)
XLA Ops:
  0.0 0.0 copy-start.1
  0.0 0.9 %copy-done.1 = bf16[8,64,256]{2,1,0:T(8,128)(2,1)S(1)} copy-done((bf16[8,64,256]{2,1,0:T(8,128)(2,1)S(1)}, bf16[8,64,256]{2,1,0:T(8,128)(2,1)}, u32[]{:S(2)}) %copy-start.1) | copy-done | bytes 262168
  1.0 0.0 copy-start.3
  1.0 0.8 %copy-done.3 = f32[2,64,64]{2,1,0:T(8,128)S(1)} copy-done((f32[2,64,64]{2,1,0:T(8,128)S(1)}, f32[2,64,64]{2,1,0:T(8,128)}, u32[]{:S(2)}) %copy-start.3) | copy-done | bytes 32792
  1.8 1.7 %leaf.1 = (bf16[1,32,128]{2,1,0:T(8,128)(2,1)S(1)}, f32[8,32,64]{2,1,0:T(8,128)S(1)}) custom-call(bf16[32,2048]{1,0:T(8,128)(2,1)} %own.1, bf16[8,64,256]{2,1,0:T(8,128)(2,1)S(1)} %copy-done.1, f32[2,64,64]{2,1,0:T(8,128)S(1)} %copy-done.3), custom_call_target="tpu_custom_call" | custom-call | bytes 425984 | tf_op jit(solution)/shard_map/leaf/pallas_call | solution.py:195
  3.5 0.0 copy-start.2
  3.5 5.1 %collective-permute-start.2 = (bf16[1,32,128]{2,1,0:T(8,128)(2,1)S(1)}, bf16[1,32,128]{2,1,0:T(8,128)(2,1)S(1)}, u32[]{:S(2)}, u32[]{:S(2)}) collective-permute-start(bf16[1,32,128]{2,1,0:T(8,128)(2,1)S(1)} %get-tuple-element.10), channel_id=1, source_target_pairs={{0,24},{1,25},{2,26},{3,27},{4,28},{5,29},{6,30},{7,31},{8,16},{9,... | collective-permute-start | bytes 24584 | tf_op jit(solution)/shard_map/ppermute | solution.py:227
  8.5 0.0 collective-permute-start.1
  8.5 0.6 %collective-permute-start = (bf16[1,32,128]{2,1,0:T(8,128)(2,1)S(1)}, bf16[1,32,128]{2,1,0:T(8,128)(2,1)S(1)}, u32[]{:S(2)}, u32[]{:S(2)}) collective-permute-start(bf16[1,32,128]{2,1,0:T(8,128)(2,1)S(1)} %get-tuple-element.10), channel_id=1, source_target_pairs={{0,8},{1,9},{2,10},{3,11},{4,12},{5,13},{6,14},{7,15},{8,0},{9,1},... | collective-permute-start | bytes 24584 | tf_op jit(solution)/shard_map/ppermute | solution.py:227
  9.2 3.0 %collective-permute-done = bf16[1,32,128]{2,1,0:T(8,128)(2,1)S(1)} collective-permute-done((bf16[1,32,128]{2,1,0:T(8,128)(2,1)S(1)}, bf16[1,32,128]{2,1,0:T(8,128)(2,1)S(1)}, u32[]{:S(2)}, u32[]{:S(2)}) %collective-permute-start) | collective-permute-done | bytes 8224 | tf_op jit(solution)/shard_map/ppermute | solution.py:227
  12.2 0.9 %collective-permute-done.1 = bf16[1,32,128]{2,1,0:T(8,128)(2,1)S(1)} collective-permute-done((bf16[1,32,128]{2,1,0:T(8,128)(2,1)S(1)}, bf16[1,32,128]{2,1,0:T(8,128)(2,1)S(1)}, u32[]{:S(2)}, u32[]{:S(2)}) %collective-permute-start.1) | collective-permute-done | bytes 8224 | tf_op jit(solution)/shard_map/ppermute | solution.py:227
  13.1 0.0 collective-permute-done.2
  13.1 1.6 %collective-permute-start.3 = (bf16[4,32,128]{2,1,0:T(8,128)(2,1)S(1)}, bf16[4,32,128]{2,1,0:T(8,128)(2,1)S(1)}, u32[]{:S(2)}, u32[]{:S(2)}) collective-permute-start(bf16[4,32,128]{2,1,0:T(8,128)(2,1)S(1)} %get-tuple-element.23), channel_id=1, source_target_pairs={{0,2},{1,3},{2,0},{3,1},{4,6},{5,7},{6,4},{7,5},{8,10},{9,11},{10,... | collective-permute-start | bytes 98312 | tf_op jit(solution)/shard_map/ppermute | solution.py:227
  14.7 0.0 collective-permute-start.7
  14.7 5.3 %collective-permute-start.8 = (bf16[32,2048]{1,0:T(8,128)(2,1)}, bf16[32,2048]{1,0:T(8,128)(2,1)S(1)}, u32[]{:S(2)}, u32[]{:S(2)}) collective-permute-start(bf16[32,2048]{1,0:T(8,128)(2,1)} %own.1), channel_id=1, source_target_pairs={{0,31},{1,0},{2,1},{3,2},{4,3},{5,4},{6,5},{7,6},{8,7},{9,8},{10,9... | collective-permute-start | bytes 393224 | tf_op jit(solution)/shard_map/ppermute | solution.py:227
  20.0 0.0 collective-permute-start.5
  20.0 0.0 collective-permute-start.4
  20.0 0.0 collective-permute-done.3
  20.1 3.9 %collective-permute-done.4 = bf16[4,32,128]{2,1,0:T(8,128)(2,1)S(1)} collective-permute-done((bf16[4,32,128]{2,1,0:T(8,128)(2,1)S(1)}, bf16[4,32,128]{2,1,0:T(8,128)(2,1)S(1)}, u32[]{:S(2)}, u32[]{:S(2)}) %collective-permute-start.4) | collective-permute-done | bytes 32800 | tf_op jit(solution)/shard_map/ppermute | solution.py:227
  24.0 0.9 %collective-permute-done.5 = bf16[4,32,128]{2,1,0:T(8,128)(2,1)S(1)} collective-permute-done((bf16[4,32,128]{2,1,0:T(8,128)(2,1)S(1)}, bf16[4,32,128]{2,1,0:T(8,128)(2,1)S(1)}, u32[]{:S(2)}, u32[]{:S(2)}) %collective-permute-start.5) | collective-permute-done | bytes 32800 | tf_op jit(solution)/shard_map/ppermute | solution.py:227
  24.9 0.1 collective-permute-start.6
  25.6 0.0 copy-start.4
  25.6 0.8 %copy-done.4 = f32[2,64,64]{2,1,0:T(8,128)S(1)} copy-done((f32[2,64,64]{2,1,0:T(8,128)S(1)}, f32[2,64,64]{2,1,0:T(8,128)}, u32[]{:S(2)}) %copy-start.4) | copy-done | bytes 32792
  26.4 0.0 copy-start.5
  26.4 0.9 %copy-done.5 = f32[8,64,64]{2,1,0:T(8,128)S(1)} copy-done((f32[8,64,64]{2,1,0:T(8,128)S(1)}, f32[8,64,64]{2,1,0:T(8,128)}, u32[]{:S(2)}) %copy-start.5) | copy-done | bytes 131096
  27.4 0.0 copy-start.6
  27.4 0.8 %copy-done.6 = f32[2,64,64]{2,1,0:T(8,128)S(1)} copy-done((f32[2,64,64]{2,1,0:T(8,128)S(1)}, f32[2,64,64]{2,1,0:T(8,128)}, u32[]{:S(2)}) %copy-start.6) | copy-done | bytes 32792
  28.2 0.0 copy-start.7
  28.2 0.7 %copy-done.7 = s32[1,3]{1,0:T(1,128)S(1)} copy-done((s32[1,3]{1,0:T(1,128)S(1)}, s32[1,3]{1,0:T(1,128)}, u32[]{:S(2)}) %copy-start.7) | copy-done | bytes 36
  28.9 0.0 copy-start.8
  28.9 0.7 %copy-done.8 = s32[1,3]{1,0:T(1,128)S(1)} copy-done((s32[1,3]{1,0:T(1,128)S(1)}, s32[1,3]{1,0:T(1,128)}, u32[]{:S(2)}) %copy-start.8) | copy-done | bytes 36
  29.5 3.6 %maps.1 = (bf16[4096,128]{1,0:T(8,128)(2,1)S(1)}, bf16[128,1024]{1,0:T(8,128)(2,1)S(1)}, f32[32,512]{1,0:T(8,128)S(1)}) custom-call(s32[1]{0:T(128)} %bitcast.device, s32[1,3]{1,0:T(1,128)S(1)} %copy-done.7, s32[1,3]{1,0:T(1,128)S(1)} %copy-done.8, f32[8,32,64]{2,1,0:T(8,128)S(1)} %get-tuple-element.11.leaf, f32[2,64,64]{2,1,0:T(8,128)S(1)} %copy-done.4, ...), custom_call_target="tpu_custom_call" | custom-call | bytes 262172 | tf_op jit(solution)/shard_map/maps/pallas_call | solution.py:195
  33.1 0.0 collective-permute-done.7.before
  33.1 0.0 collective-permute-done.8.after
  33.1 0.0 copy-start
  33.1 1.6 %copy-done = bf16[16,256,256]{2,1,0:T(8,128)(2,1)S(1)} copy-done((bf16[16,256,256]{2,1,0:T(8,128)(2,1)S(1)}, bf16[16,256,256]{2,1,0:T(8,128)(2,1)}, u32[]{:S(2)}) %copy-start) | copy-done | bytes 2097176
  34.7 0.0 copy-start.9
  34.7 0.7 %copy-done.9 = s32[16]{0:T(128)S(1)} copy-done((s32[16]{0:T(128)S(1)}, s32[16]{0:T(128)}, u32[]{:S(2)}) %copy-start.9) | copy-done | bytes 88
  35.4 0.0 copy-start.10
  35.4 0.7 %copy-done.10 = s32[16]{0:T(128)S(1)} copy-done((s32[16]{0:T(128)S(1)}, s32[16]{0:T(128)}, u32[]{:S(2)}) %copy-start.10) | copy-done | bytes 88
  36.0 1.4 %near.1 = f32[8,32,256]{2,1,0:T(8,128)S(1)} custom-call(s32[1]{0:T(128)S(6)} %copy.28.live, s32[16]{0:T(128)S(1)} %copy-done.9, s32[16]{0:T(128)S(1)} %copy-done.10, bf16[32,2048]{1,0:T(8,128)(2,1)S(1)} %collective-permute-done.7.before, bf16[32,2048]{1,0:T(8,128)(2,1)} %own.1, bf16[32,2048]{1,0:T(8,128)(2,1)S(1)} %collective-permute-done.8.after, ...), custom_call_target="tpu_custom_call" | custom-call | bytes 2490500 | tf_op jit(solution)/shard_map/near/pallas_call | solution.py:195
  37.4 0.0 collective-permute-done.6
  37.5 0.0 copy-done.2
  37.5 1.5 %field.1 = f32[32,2048]{1,0:T(8,128)} custom-call(bf16[32,32,128]{2,1,0:T(8,128)(2,1)S(1)} %constant_dynamic-update-slice_fusion.11.gathered, bf16[4096,128]{1,0:T(8,128)(2,1)S(1)} %get-tuple-element.12.maps, bf16[128,1024]{1,0:T(8,128)(2,1)S(1)} %get-tuple-element.13.spread, f32[32,512]{1,0:T(8,128)S(1)} %get-tuple-element.14.local, ...), custom_call_target="tpu_custom_call" | custom-call | bytes 2162688 | tf_op jit(solution)/shard_map/field/pallas_call | solution.py:195
  (8 shorter events, 0.1 us)
Async XLA Ops:
  0.0 0.9 %copy-start.1 = (bf16[8,64,256]{2,1,0:T(8,128)(2,1)S(1)}, bf16[8,64,256]{2,1,0:T(8,128)(2,1)}, u32[]{:S(2)}) copy-start(bf16[8,64,256]{2,1,0:T(8,128)(2,1)} %basis.3) | copy-start | bytes 786436
  1.0 0.8 %copy-start.3 = (f32[2,64,64]{2,1,0:T(8,128)S(1)}, f32[2,64,64]{2,1,0:T(8,128)}, u32[]{:S(2)}) copy-start(f32[2,64,64]{2,1,0:T(8,128)} %transfer.3) | copy-start | bytes 98308
  3.5 34.0 %copy-start.2 = (bf16[8,64,256]{2,1,0:T(8,128)(2,1)S(1)}, bf16[8,64,256]{2,1,0:T(8,128)(2,1)}, u32[]{:S(2)}) copy-start(bf16[8,64,256]{2,1,0:T(8,128)(2,1)} %basis.3) | copy-start | bytes 786436
  3.5 9.6 %collective-permute-start.2 = (bf16[1,32,128]{2,1,0:T(8,128)(2,1)S(1)}, bf16[1,32,128]{2,1,0:T(8,128)(2,1)S(1)}, u32[]{:S(2)}, u32[]{:S(2)}) collective-permute-start(bf16[1,32,128]{2,1,0:T(8,128)(2,1)S(1)} %get-tuple-element.10), channel_id=1, source_target_pairs={{0,24},{1,25},{2,26},{3,27},{4,28},{5,29},{6,30},{7,31},{8,16},{9,... | collective-permute-start | bytes 24584 | tf_op jit(solution)/shard_map/ppermute | solution.py:227
  8.5 4.5 %collective-permute-start.1 = (bf16[1,32,128]{2,1,0:T(8,128)(2,1)S(1)}, bf16[1,32,128]{2,1,0:T(8,128)(2,1)S(1)}, u32[]{:S(2)}, u32[]{:S(2)}) collective-permute-start(bf16[1,32,128]{2,1,0:T(8,128)(2,1)S(1)} %get-tuple-element.10), channel_id=1, source_target_pairs={{0,16},{1,17},{2,18},{3,19},{4,20},{5,21},{6,22},{7,23},{8,24},{9,... | collective-permute-start | bytes 24584 | tf_op jit(solution)/shard_map/ppermute | solution.py:227
  8.5 3.7 %collective-permute-start = (bf16[1,32,128]{2,1,0:T(8,128)(2,1)S(1)}, bf16[1,32,128]{2,1,0:T(8,128)(2,1)S(1)}, u32[]{:S(2)}, u32[]{:S(2)}) collective-permute-start(bf16[1,32,128]{2,1,0:T(8,128)(2,1)S(1)} %get-tuple-element.10), channel_id=1, source_target_pairs={{0,8},{1,9},{2,10},{3,11},{4,12},{5,13},{6,14},{7,15},{8,0},{9,1},... | collective-permute-start | bytes 24584 | tf_op jit(solution)/shard_map/ppermute | solution.py:227
  13.1 6.9 %collective-permute-start.3 = (bf16[4,32,128]{2,1,0:T(8,128)(2,1)S(1)}, bf16[4,32,128]{2,1,0:T(8,128)(2,1)S(1)}, u32[]{:S(2)}, u32[]{:S(2)}) collective-permute-start(bf16[4,32,128]{2,1,0:T(8,128)(2,1)S(1)} %get-tuple-element.23), channel_id=1, source_target_pairs={{0,2},{1,3},{2,0},{3,1},{4,6},{5,7},{6,4},{7,5},{8,10},{9,11},{10,... | collective-permute-start | bytes 98312 | tf_op jit(solution)/shard_map/ppermute | solution.py:227
  14.7 18.4 %collective-permute-start.7 = (bf16[32,2048]{1,0:T(8,128)(2,1)}, bf16[32,2048]{1,0:T(8,128)(2,1)S(1)}, u32[]{:S(2)}, u32[]{:S(2)}) collective-permute-start(bf16[32,2048]{1,0:T(8,128)(2,1)} %own.1), channel_id=1, source_target_pairs={{0,1},{1,2},{2,3},{3,4},{4,5},{5,6},{6,7},{7,8},{8,9},{9,10},{10,1... | collective-permute-start | bytes 393224 | tf_op jit(solution)/shard_map/ppermute | solution.py:227
  14.7 18.5 %collective-permute-start.8 = (bf16[32,2048]{1,0:T(8,128)(2,1)}, bf16[32,2048]{1,0:T(8,128)(2,1)S(1)}, u32[]{:S(2)}, u32[]{:S(2)}) collective-permute-start(bf16[32,2048]{1,0:T(8,128)(2,1)} %own.1), channel_id=1, source_target_pairs={{0,31},{1,0},{2,1},{3,2},{4,3},{5,4},{6,5},{7,6},{8,7},{9,8},{10,9... | collective-permute-start | bytes 393224 | tf_op jit(solution)/shard_map/ppermute | solution.py:227
  20.0 4.8 %collective-permute-start.5 = (bf16[4,32,128]{2,1,0:T(8,128)(2,1)S(1)}, bf16[4,32,128]{2,1,0:T(8,128)(2,1)S(1)}, u32[]{:S(2)}, u32[]{:S(2)}) collective-permute-start(bf16[4,32,128]{2,1,0:T(8,128)(2,1)S(1)} %get-tuple-element.23), channel_id=1, source_target_pairs={{0,6},{1,7},{2,4},{3,5},{4,2},{5,3},{6,0},{7,1},{8,14},{9,15},{10,... | collective-permute-start | bytes 98312 | tf_op jit(solution)/shard_map/ppermute | solution.py:227
  20.0 3.9 %collective-permute-start.4 = (bf16[4,32,128]{2,1,0:T(8,128)(2,1)S(1)}, bf16[4,32,128]{2,1,0:T(8,128)(2,1)S(1)}, u32[]{:S(2)}, u32[]{:S(2)}) collective-permute-start(bf16[4,32,128]{2,1,0:T(8,128)(2,1)S(1)} %get-tuple-element.23), channel_id=1, source_target_pairs={{0,4},{1,5},{2,6},{3,7},{4,0},{5,1},{6,2},{7,3},{8,12},{9,13},{10,... | collective-permute-start | bytes 98312 | tf_op jit(solution)/shard_map/ppermute | solution.py:227
  24.9 12.6 %collective-permute-start.6 = (bf16[16,32,128]{2,1,0:T(8,128)(2,1)S(1)}, bf16[16,32,128]{2,1,0:T(8,128)(2,1)S(1)}, u32[]{:S(2)}, u32[]{:S(2)}) collective-permute-start(bf16[16,32,128]{2,1,0:T(8,128)(2,1)S(1)} %get-tuple-element.15), channel_id=1, source_target_pairs={{0,1},{1,0},{2,3},{3,2},{4,5},{5,4},{6,7},{7,6},{8,9},{9,8},{10,11... | collective-permute-start | bytes 393224 | tf_op jit(solution)/shard_map/ppermute | solution.py:227
  25.6 0.8 %copy-start.4 = (f32[2,64,64]{2,1,0:T(8,128)S(1)}, f32[2,64,64]{2,1,0:T(8,128)}, u32[]{:S(2)}) copy-start(f32[2,64,64]{2,1,0:T(8,128)} %transfer.3) | copy-start | bytes 98308
  26.4 0.9 %copy-start.5 = (f32[8,64,64]{2,1,0:T(8,128)S(1)}, f32[8,64,64]{2,1,0:T(8,128)}, u32[]{:S(2)}) copy-start(f32[8,64,64]{2,1,0:T(8,128)} %coupling.1) | copy-start | bytes 393220
  27.4 0.8 %copy-start.6 = (f32[2,64,64]{2,1,0:T(8,128)S(1)}, f32[2,64,64]{2,1,0:T(8,128)}, u32[]{:S(2)}) copy-start(f32[2,64,64]{2,1,0:T(8,128)} %sibling.1) | copy-start | bytes 98308
  28.2 0.7 %copy-start.7 = (s32[1,3]{1,0:T(1,128)S(1)}, s32[1,3]{1,0:T(1,128)}, u32[]{:S(2)}) copy-start(s32[1,3]{1,0:T(1,128)} %offsets.1) | copy-start | bytes 40
  28.9 0.7 %copy-start.8 = (s32[1,3]{1,0:T(1,128)S(1)}, s32[1,3]{1,0:T(1,128)}, u32[]{:S(2)}) copy-start(s32[1,3]{1,0:T(1,128)} %classes.1) | copy-start | bytes 40
  33.1 1.6 %copy-start = (bf16[16,256,256]{2,1,0:T(8,128)(2,1)S(1)}, bf16[16,256,256]{2,1,0:T(8,128)(2,1)}, u32[]{:S(2)}) copy-start(bf16[16,256,256]{2,1,0:T(8,128)(2,1)} %tiles.1) | copy-start | bytes 6291460
  34.7 0.7 %copy-start.9 = (s32[16]{0:T(128)S(1)}, s32[16]{0:T(128)}, u32[]{:S(2)}) copy-start(s32[16]{0:T(128)} %targets.1) | copy-start | bytes 196
  35.4 0.7 %copy-start.10 = (s32[16]{0:T(128)S(1)}, s32[16]{0:T(128)}, u32[]{:S(2)}) copy-start(s32[16]{0:T(128)} %sources.1) | copy-start | bytes 196
where the time goes:
time: 39.5 us; the launch traced here: 39 us
  starting transfers between devices  12.7 us (32%)
  local copies, waits for them, and re-layouts  8.73 us (22%)
  waiting for transfers between devices  8.66 us (22%)
  Pallas kernels  8.14 us (21%)
  between operations  0.77 us (2%)
    ppermute x9, starting transfers between devices, send(): return lax.ppermute(x, AXES, [(i, target(i)) for i in range(count)])  12.7 us
    unnamed x28, local copies, waits for them, and re-layouts  8.69 us
    ppermute x9, waiting for transfers between devices, send(): return lax.ppermute(x, AXES, [(i, target(i)) for i in range(count)])  8.66 us
    pallas_call x4, Pallas kernels, call(): pl.pallas_call(kernel, name=name, out_shape=outs, in_specs=[pl.BlockSpec(...  8.14 us
  transfers between devices with their start and end apart: 9, of which 4 were waited for; matrix products, arithmetic and copies ran while one was open for 0% of the time, Pallas kernels for 13%

commit v1 on v0

v1 whole, which is shorter than its diff:
```python
import functools

import jax
import jax.numpy as jnp
from jax import lax
from jax.experimental import pallas as pl
from jax.experimental.pallas import tpu as pltpu
from jax.sharding import PartitionSpec as P

AXES = ("leaf", "grp")
F32 = jnp.float32
BF16 = jnp.bfloat16
NN = (((1,), (0,)), ((), ()))
NT = (((1,), (1,)), ((), ()))
CHUNK = 512
VMEM_LIMIT = 48 * 2**20


def split(x):
    high = x.astype(BF16)
    return high, (x - high.astype(F32)).astype(BF16)


def dot(a, b, dims=NN):
    return lax.dot_general(a, b, dims, preferred_element_type=F32)


def dot3(a, b, dims=NN):
    a_high, a_low = split(a)
    b_high, b_low = split(b)
    return dot(a_high, b_high, dims) + (dot(a_low, b_high, dims) + dot(a_high, b_low, dims))


def rounds_of(bits):
    rounds = []
    top = bits
    while top > 0:
        wide = 2 if top > 1 else 1
        rounds.append((top - wide, wide))
        top -= wide
    return rounds


def masks_of(bits):
    masks = [0]
    for low, wide in rounds_of(bits):
        masks = [mask ^ (step << low) for step in range(2**wide) for mask in masks]
    return masks


def place_of(mask, bits):
    place, shift = 0, 0
    for low, wide in rounds_of(bits):
        place = place | (((mask >> low) & (2**wide - 1)) << shift)
        shift += wide
    return place


def up(blocks, transfer):
    left = jnp.concatenate(blocks[0::2], axis=0)
    right = jnp.concatenate(blocks[1::2], axis=0)
    rows = blocks[0].shape[0]
    total = dot3(left, transfer[0]) + dot3(right, transfer[1])
    return [total[i * rows : (i + 1) * rows] for i in range(len(blocks) // 2)]


def high_low(double):
    high, low = split(double)
    lane = lax.broadcasted_iota(jnp.int32, double.shape, 1)
    return jnp.where(lane < double.shape[1] // 2, high, low)


def leaf_kernel(vectors_hbm, basis_hbm, transfer_hbm, send, leaf, basis, paths, vectors, transfer, sems):
    boxes, rank, points = basis.shape
    columns = vectors.shape[0]
    steps = boxes.bit_length() - 1
    copies = [
        pltpu.make_async_copy(transfer_hbm, transfer, sems.at[0]),
        pltpu.make_async_copy(vectors_hbm, vectors, sems.at[1]),
        pltpu.make_async_copy(basis_hbm, basis, sems.at[2]),
    ]
    for copy in copies:
        copy.start()
    copies[0].wait()
    t0, t1 = transfer[0], transfer[1]
    stack = jnp.concatenate([t0, t1], axis=0)
    for height in range(1, steps):
        paths[height - 1, : 2**height * rank, :rank] = stack
        stack = jnp.concatenate([dot3(stack, t0), dot3(stack, t1)], axis=0)
    double = jnp.concatenate([stack, stack], axis=1)
    paths[steps - 1] = double
    weights, rest = split(double)
    copies[1].wait()
    copies[2].wait()
    high, low = [], []
    for b in range(boxes):
        coeffs = dot(vectors[:, b * points : (b + 1) * points], basis[b], NT)
        leaf[b] = coeffs
        one, other = split(coeffs)
        high.append(one)
        low.append(other)
    high = jnp.concatenate(high, axis=1)
    low = jnp.concatenate(low, axis=1)
    send[0] = high_low(dot(high, weights) + (dot(low, weights) + dot(high, rest)))


def map_kernel(
    bits,
    device,
    offsets_hbm,
    classes_hbm,
    targets_hbm,
    sources_hbm,
    live_hbm,
    transfer_hbm,
    sibling_hbm,
    coupling_hbm,
    tiles_hbm,
    coeffs,
    leaf,
    paths,
    maps,
    spread,
    local,
    tiles,
    passed,
    targets,
    sources,
    live,
    offsets,
    classes,
    transfer,
    sibling,
    coupling,
    sems,
):
    boxes, columns, rank = leaf.shape
    pairs = (
        (transfer_hbm, transfer),
        (sibling_hbm, sibling),
        (offsets_hbm, offsets),
        (classes_hbm, classes),
        (coupling_hbm, coupling),
        (targets_hbm, targets),
        (sources_hbm, sources),
        (live_hbm, live),
        (tiles_hbm, tiles),
    )
    copies = [pltpu.make_async_copy(a, b, sems.at[i]) for i, (a, b) in enumerate(pairs)]
    for copy in copies:
        copy.start()
    passed[...] = coeffs[...]
    me = device[0]
    count = 2**bits
    steps = boxes.bit_length() - 1
    copies[0].wait()
    copies[1].wait()
    t0, t1 = transfer[0], transfer[1]
    s0, s1 = sibling[0], sibling[1]

    def put(at, double):
        both = high_low(double)
        at = pl.multiple_of(at * 2 * rank, 2 * rank)
        maps[pl.ds(at, rank)] = both
        maps[pl.ds(at + rank, rank)] = both

    def twice(x):
        return jnp.concatenate([x, x], axis=1)

    def place(height, low):
        return place_of((1 << height) | (low ^ (me & ((1 << height) - 1))), bits)

    def path(height):
        if height <= steps:
            at = pl.multiple_of((me & ((1 << height) - 1)) * rank, rank)
            return paths[height - 1, pl.ds(at, rank), :rank]
        return dot3(path(height - 1), transfer[(me >> (height - 1)) & 1])

    put(0, jnp.zeros((rank, 2 * rank), F32))
    for height in range(bits):
        mine = sibling[(me >> height) & 1]
        if height == 0:
            put(place(0, 0), twice(mine))
            continue
        bridge = twice(dot3(mine, path(height), NT))
        base = min(height, steps)
        fans = [bridge]
        for step in range(height - 1, base - 1, -1):
            fans = [dot3(t, fan) for fan in fans for t in (t0, t1)]
        rows = 2**base * rank
        for j, fan in enumerate(fans):
            block = dot3(paths[base - 1, :rows, :rank], fan)
            for i in range(2**base):
                put(place(height, (j << base) + i), block[i * rank : (i + 1) * rank])
    copies[2].wait()
    copies[3].wait()
    copies[4].wait()
    for i in range(offsets.shape[1]):
        mask = ((me + offsets[0, i] + count) & (count - 1)) ^ me
        at = place_of(mask, bits)
        both = maps[pl.ds(pl.multiple_of(at * 2 * rank, 2 * rank), rank)].astype(F32)
        put(at, twice(both[:, :rank] + both[:, rank:] + coupling[classes[0, i]]))

    half = boxes * rank
    high, low = split(paths[steps - 1])
    spread[:half] = high
    spread[half:] = low
    levels = [[leaf[b] for b in range(boxes)]]
    while len(levels[-1]) > 2:
        levels.append(up(levels[-1], (t0, t1)))
    down = None
    for level in reversed(levels):
        across0 = dot3(jnp.concatenate(level[1::2], axis=0), s0)
        across1 = dot3(jnp.concatenate(level[0::2], axis=0), s1)
        if down is not None:
            parents = jnp.concatenate(down, axis=0)
            across0 = across0 + dot3(parents, t0, NT)
            across1 = across1 + dot3(parents, t1, NT)
        down = []
        for i in range(len(level) // 2):
            down.append(across0[i * columns : (i + 1) * columns])
            down.append(across1[i * columns : (i + 1) * columns])
    for b in range(boxes):
        local[:, b * rank : (b + 1) * rank] = down[b]
    for copy in copies[5:]:
        copy.wait()


def near_kernel(live, targets, sources, before, own, after, tiles, near, window):
    slots, points, _ = tiles.shape
    boxes = near.shape[0]
    for i, part in enumerate((before, own, after)):
        for b in range(boxes):
            window[i * boxes + b] = part[:, b * points : (b + 1) * points]
    near[...] = jnp.zeros_like(near)
    for slot in range(slots):
        source = window[sources[slot]]
        source = jnp.where(slot < live[0], source, jnp.zeros_like(source))
        target = targets[slot]
        near[target] = near[target] + dot(source, tiles[slot])


def field_kernel(gathered, maps, spread, local, basis, near, field):
    count = gathered.shape[0]
    boxes, rank, points = basis.shape
    pairs = count // 2
    wide = 4 * rank

    def step(k):
        coeffs = jnp.concatenate([gathered[2 * k], gathered[2 * k + 1]], axis=1)
        return dot(coeffs, maps[pl.ds(k * wide, wide)])

    if pairs <= 32:
        both = step(0)
        for k in range(1, pairs):
            both = both + step(k)
    else:
        both = lax.fori_loop(1, pairs, lambda k, sums: sums + step(k), step(0))
    summit = both[:, :rank] + both[:, rank:]
    doubled = dot(jnp.concatenate(split(summit), axis=1), spread[...], NT)
    half = boxes * rank
    rounded = (doubled[:, :half] + doubled[:, half:] + local[...]).astype(BF16)
    for b in range(boxes):
        far = dot(rounded[:, b * rank : (b + 1) * rank], basis[b])
        field[:, b * points : (b + 1) * points] = near[b] + far


SPACES = {"v": pltpu.VMEM, "s": pltpu.SMEM, "h": pltpu.HBM}


def call(kernel, name, kinds, args, outs, scratch=(), flops=0):
    moved = sum(x.size * x.dtype.itemsize for x in args)
    return pl.pallas_call(
        kernel,
        name=name,
        out_shape=[jax.ShapeDtypeStruct(shape, kind) for _, shape, kind in outs],
        in_specs=[pl.BlockSpec(memory_space=SPACES[kind]) for kind in kinds],
        out_specs=[pl.BlockSpec(memory_space=SPACES[space]) for space, _, _ in outs],
        scratch_shapes=list(scratch),
        compiler_params=pltpu.CompilerParams(vmem_limit_bytes=VMEM_LIMIT),
        cost_estimate=pl.CostEstimate(flops=flops, bytes_accessed=moved, transcendentals=0),
    )(*args)


def body(
    vectors,
    leaf_basis,
    transfer,
    sibling_coupling,
    list_coupling,
    near_tiles,
    tile_target,
    tile_source,
    tile_count,
    couple_offset,
    couple_class,
):
    columns, width = vectors.shape
    boxes, rank, points = leaf_basis.shape
    count = lax.axis_size(AXES)
    bits = count.bit_length() - 1
    steps = boxes.bit_length() - 1
    double = 2 * rank
    dma = pltpu.SemaphoreType.DMA

    def send(x, target):
        return lax.ppermute(x, AXES, [(i, target(i)) for i in range(count)])

    def swap(x, mask):
        return send(x, lambda i: i ^ mask)

    before = send(vectors, lambda i: (i + 1) % count)
    coeffs, leaf, basis, paths = call(
        leaf_kernel,
        "leaf",
        "hhh",
        (vectors, leaf_basis, transfer),
        (
            ("v", (1, columns, double), BF16),
            ("v", (boxes, columns, rank), F32),
            ("v", leaf_basis.shape, BF16),
            ("v", (steps, boxes * rank, double), F32),
        ),
        scratch=(pltpu.VMEM(vectors.shape, BF16), pltpu.VMEM(transfer.shape, F32), dma((3,))),
    )
    device = lax.axis_index(AXES).astype(jnp.int32).reshape(1)
    ints = jnp.int32
    maps, spread, local, tiles, passed, targets, sources, live = call(
        functools.partial(map_kernel, bits),
        "maps",
        "shhhhhhhhhvvv",
        (
            device,
            couple_offset,
            couple_class,
            tile_target,
            tile_source,
            tile_count,
            transfer,
            sibling_coupling,
            list_coupling,
            near_tiles,
            coeffs,
            leaf,
            paths,
        ),
        (
            ("v", (count * double, double), BF16),
            ("v", (2 * boxes * rank, double), BF16),
            ("v", (columns, boxes * rank), F32),
            ("v", near_tiles.shape, BF16),
            ("v", coeffs.shape, BF16),
            ("s", tile_target.shape, ints),
            ("s", tile_source.shape, ints),
            ("s", tile_count.shape, ints),
        ),
        scratch=(
            pltpu.SMEM(couple_offset.shape, ints),
            pltpu.SMEM(couple_class.shape, ints),
            pltpu.VMEM(transfer.shape, F32),
            pltpu.VMEM(sibling_coupling.shape, F32),
            pltpu.VMEM(list_coupling.shape, F32),
            dma((9,)),
        ),
    )
    gathered = coeffs
    after = None
    for index, (low, wide) in enumerate(rounds_of(bits)):
        parts = [passed if index == 0 else gathered]
        for step in range(1, 2**wide):
            parts.append(swap(gathered, step << low))
        gathered = jnp.concatenate(parts, axis=0)
        if index == 0:
            gathered, late = lax.optimization_barrier((gathered, vectors))
            after = send(late, lambda i: (i - 1) % count)
    (near,) = call(
        near_kernel,
        "near",
        "sssvvvv",
        (live, targets, sources, before, vectors, after, tiles),
        (("v", (boxes, columns, points), F32),),
        scratch=(pltpu.VMEM((3 * boxes, columns, points), BF16),),
    )
    (field,) = call(
        field_kernel,
        "field",
        "vvvvvv",
        (gathered, maps, spread, local, basis, near),
        (("v", (columns, width), F32),),
    )
    return field


def solution(mesh):
    in_specs = (
        P(None, AXES),
        P(AXES, None, None),
        P(),
        P(),
        P(),
        P(AXES, None, None),
        P(AXES),
        P(AXES),
        P(AXES),
        P(AXES, None),
        P(AXES, None),
    )
    return jax.shard_map(body, mesh=mesh, in_specs=in_specs, out_specs=P(None, AXES), check_vma=False)
```

time: 39.5 us -> 33.7 us (0.85)
  waiting for transfers between devices: 8.66 us -> 2.68 us
  local copies, waits for them, and re-layouts: 8.73 us -> 7.08 us
  starting transfers between devices: 12.7 us -> 14.2 us
    ppermute x9, waiting for transfers between devices: 8.66 us -> 2.68 us  [send(): return lax.ppermute(x, AXES, [(i, target(i)) for i in range(count)])]
    unnamed x28 -> x22, local copies, waits for them, and re-layouts: 8.69 us -> 7.07 us
    ppermute x9, starting transfers between devices: 12.7 us -> 14.2 us  [send(): return lax.ppermute(x, AXES, [(i, target(i)) for i in range(count)])]
  transfers between devices with their start and end apart: 9 -> 9, of which waited for: 4 -> 1; matrix products, arithmetic and copies ran while one was open for 0% -> 0% of each run, Pallas kernels for 13% -> 17%
where the time goes in v1:
time: 33.7 us; the launch traced here: 33.3 us
  starting transfers between devices  14.2 us (42%)
  Pallas kernels  8.43 us (25%)
  local copies, waits for them, and re-layouts  7.08 us (21%)
  waiting for transfers between devices  2.68 us (8%)
  between operations  0.79 us (2%)
    ppermute x9, starting transfers between devices, send(): return lax.ppermute(x, AXES, [(i, target(i)) for i in range(count)])  14.2 us
    pallas_call x4, Pallas kernels, call(): pl.pallas_call(kernel, name=name, out_shape=[jax.ShapeDtypeStruct(shape,...  8.43 us
    unnamed x22, local copies, waits for them, and re-layouts  7.07 us
    ppermute x9, waiting for transfers between devices, send(): return lax.ppermute(x, AXES, [(i, target(i)) for i in range(count)])  2.68 us
  transfers between devices with their start and end apart: 9, of which 1 were waited for; matrix products, arithmetic and copies ran while one was open for 0% of the time, Pallas kernels for 17%

profile of v1, /device:TPU:0, one launch (start us, length us, event | category | flops | bytes accessed | tf_op | source)
XLA Modules:
  0.0 33.3 jit_solution(6688540075706681038)
XLA Ops:
  0.0 0.0 copy-start
  0.0 0.8 %copy-done = f32[2,64,64]{2,1,0:T(8,128)S(1)} copy-done((f32[2,64,64]{2,1,0:T(8,128)S(1)}, f32[2,64,64]{2,1,0:T(8,128)}, u32[]{:S(2)}) %copy-start) | copy-done | bytes 32792
  0.8 0.0 copy-start.2
  0.8 0.9 %copy-done.2 = bf16[8,64,256]{2,1,0:T(8,128)(2,1)S(1)} copy-done((bf16[8,64,256]{2,1,0:T(8,128)(2,1)S(1)}, bf16[8,64,256]{2,1,0:T(8,128)(2,1)}, u32[]{:S(2)}) %copy-start.2) | copy-done | bytes 262168
  1.8 1.4 %leaf.1 = (bf16[1,32,128]{2,1,0:T(8,128)(2,1)S(1)}, f32[8,32,64]{2,1,0:T(8,128)S(1)}, bf16[8,64,256]{2,1,0:T(8,128)(2,1)S(1)}, f32[3,512,128]{2,1,0:T(8,128)S(1)}) custom-call(bf16[32,2048]{1,0:T(8,128)(2,1)} %own.1, bf16[8,64,256]{2,1,0:T(8,128)(2,1)S(1)} %copy-done.2, f32[2,64,64]{2,1,0:T(8,128)S(1)} %copy-done), custom_call_target="tpu_custom_call" | custom-call | bytes 425984 | tf_op jit(solution)/shard_map/leaf/pallas_call | solution.py:273
  3.2 3.1 %collective-permute-start = (bf16[1,32,128]{2,1,0:T(8,128)(2,1)S(1)}, bf16[1,32,128]{2,1,0:T(8,128)(2,1)S(1)}, u32[]{:S(2)}, u32[]{:S(2)}) collective-permute-start(bf16[1,32,128]{2,1,0:T(8,128)(2,1)S(1)} %get-tuple-element.19.coeffs), channel_id=1, source_target_pairs={{0,8},{1,9},{2,10},{3,11},{4,12},{5,13},{6,14},{7,15},{8,0},{9,1},... | collective-permute-start | bytes 24584 | tf_op jit(solution)/shard_map/ppermute | solution.py:307
  6.3 2.6 %collective-permute-start.1 = (bf16[1,32,128]{2,1,0:T(8,128)(2,1)S(1)}, bf16[1,32,128]{2,1,0:T(8,128)(2,1)S(1)}, u32[]{:S(2)}, u32[]{:S(2)}) collective-permute-start(bf16[1,32,128]{2,1,0:T(8,128)(2,1)S(1)} %get-tuple-element.19.coeffs), channel_id=1, source_target_pairs={{0,16},{1,17},{2,18},{3,19},{4,20},{5,21},{6,22},{7,23},{8,24},{9,... | collective-permute-start | bytes 24584 | tf_op jit(solution)/shard_map/ppermute | solution.py:307
  8.9 0.0 collective-permute-start.2
  8.9 0.0 collective-permute-start.7
  9.5 0.0 copy-start.1
  9.6 0.8 %copy-done.1 = f32[2,64,64]{2,1,0:T(8,128)S(1)} copy-done((f32[2,64,64]{2,1,0:T(8,128)S(1)}, f32[2,64,64]{2,1,0:T(8,128)}, u32[]{:S(2)}) %copy-start.1) | copy-done | bytes 32792
  10.4 0.0 copy-start.3
  10.4 0.9 %copy-done.3 = f32[8,64,64]{2,1,0:T(8,128)S(1)} copy-done((f32[8,64,64]{2,1,0:T(8,128)S(1)}, f32[8,64,64]{2,1,0:T(8,128)}, u32[]{:S(2)}) %copy-start.3) | copy-done | bytes 131096
  11.3 0.0 copy-start.4
  11.3 0.8 %copy-done.4 = f32[2,64,64]{2,1,0:T(8,128)S(1)} copy-done((f32[2,64,64]{2,1,0:T(8,128)S(1)}, f32[2,64,64]{2,1,0:T(8,128)}, u32[]{:S(2)}) %copy-start.4) | copy-done | bytes 32792
  12.2 0.0 copy-start.5
  12.2 0.7 %copy-done.5 = s32[1,3]{1,0:T(1,128)S(1)} copy-done((s32[1,3]{1,0:T(1,128)S(1)}, s32[1,3]{1,0:T(1,128)}, u32[]{:S(2)}) %copy-start.5) | copy-done | bytes 36
  12.8 0.0 copy-start.6
  12.8 0.7 %copy-done.6 = s32[1,3]{1,0:T(1,128)S(1)} copy-done((s32[1,3]{1,0:T(1,128)S(1)}, s32[1,3]{1,0:T(1,128)}, u32[]{:S(2)}) %copy-start.6) | copy-done | bytes 36
  13.5 0.0 copy-start.7
  13.5 0.7 %copy-done.7 = s32[16]{0:T(128)S(1)} copy-done((s32[16]{0:T(128)S(1)}, s32[16]{0:T(128)}, u32[]{:S(2)}) %copy-start.7) | copy-done | bytes 88
  14.1 0.0 copy-start.8
  14.1 0.7 %copy-done.8 = s32[16]{0:T(128)S(1)} copy-done((s32[16]{0:T(128)S(1)}, s32[16]{0:T(128)}, u32[]{:S(2)}) %copy-start.8) | copy-done | bytes 88
  14.8 3.4 %maps.1 = (bf16[4096,128]{1,0:T(8,128)(2,1)S(1)}, bf16[1024,128]{1,0:T(8,128)(2,1)S(1)}, f32[32,512]{1,0:T(8,128)S(1)}, bf16[16,256,256]{2,1,0:T(8,128)(2,1)S(1)...) custom-call(s32[1]{0:T(128)} %bitcast.device, s32[1,3]{1,0:T(1,128)S(1)} %copy-done.5, ...), custom_call_target="tpu_custom_call" | custom-call | bytes 3154080 | tf_op jit(solution)/shard_map/maps/pallas_call | solution.py:273
  18.2 0.0 collective-permute-done
  18.3 0.0 collective-permute-done.1
  18.3 0.0 collective-permute-done.2
  18.3 1.8 %collective-permute-start.3 = (bf16[4,32,128]{2,1,0:T(8,128)(2,1)S(1)}, bf16[4,32,128]{2,1,0:T(8,128)(2,1)S(1)}, u32[]{:S(2)}, u32[]{:S(2)}) collective-permute-start(bf16[4,32,128]{2,1,0:T(8,128)(2,1)S(1)} %pad_maximum_fusion.1), channel_id=1, source_target_pairs={{0,2},{1,3},{2,0},{3,1},{4,6},{5,7},{6,4},{7,5},{8,10},{9,11},{10,... | collective-permute-start | bytes 98312 | tf_op jit(solution)/shard_map/ppermute | solution.py:307
  20.1 1.5 %collective-permute-start.4 = (bf16[4,32,128]{2,1,0:T(8,128)(2,1)S(1)}, bf16[4,32,128]{2,1,0:T(8,128)(2,1)S(1)}, u32[]{:S(2)}, u32[]{:S(2)}) collective-permute-start(bf16[4,32,128]{2,1,0:T(8,128)(2,1)S(1)} %pad_maximum_fusion.1), channel_id=1, source_target_pairs={{0,4},{1,5},{2,6},{3,7},{4,0},{5,1},{6,2},{7,3},{8,12},{9,13},{10,... | collective-permute-start | bytes 98312 | tf_op jit(solution)/shard_map/ppermute | solution.py:307
  21.6 0.3 collective-permute-start.5
  21.8 4.9 %collective-permute-start.8 = (bf16[32,2048]{1,0:T(8,128)(2,1)}, bf16[32,2048]{1,0:T(8,128)(2,1)S(1)}, u32[]{:S(2)}, u32[]{:S(2)}) collective-permute-start(bf16[32,2048]{1,0:T(8,128)(2,1)} %own.1), channel_id=1, source_target_pairs={{0,31},{1,0},{2,1},{3,2},{4,3},{5,4},{6,5},{7,6},{8,7},{9,8},{10,9... | collective-permute-start | bytes 393224 | tf_op jit(solution)/shard_map/ppermute | solution.py:307
  26.8 0.0 collective-permute-done.3
  26.8 0.0 collective-permute-done.4
  26.8 0.0 collective-permute-done.5
  26.8 0.1 collective-permute-start.6
  26.9 0.0 collective-permute-done.7.before
  27.0 2.7 %collective-permute-done.8.after = bf16[32,2048]{1,0:T(8,128)(2,1)S(1)} collective-permute-done((bf16[32,2048]{1,0:T(8,128)(2,1)}, bf16[32,2048]{1,0:T(8,128)(2,1)S(1)}, u32[]{:S(2)}, u32[]{:S(2)}) %collective-permute-start.8) | collective-permute-done | bytes 131104 | tf_op jit(solution)/shard_map/ppermute | solution.py:307
  29.6 2.1 %near.1 = f32[8,32,256]{2,1,0:T(8,128)S(1)} custom-call(s32[1]{0:T(128)} %get-tuple-element.28.live, s32[16]{0:T(128)S(1)} %get-tuple-element.29.targets, s32[16]{0:T(128)S(1)} %get-tuple-element.30.sources, bf16[32,2048]{1,0:T(8,128)(2,1)S(1)} %collective-permute-done.7.before, bf16[32,2048]{1,0:T(8,128)(2,1)} %own.1, ...), custom_call_target="tpu_custom_call" | custom-call | bytes 2490500 | tf_op jit(solution)/shard_map/near/pallas_call | solution.py:273
  31.7 0.0 collective-permute-done.6
  31.7 1.5 %field.1 = f32[32,2048]{1,0:T(8,128)} custom-call(bf16[32,32,128]{2,1,0:T(8,128)(2,1)S(1)} %constant_dynamic-update-slice_fusion.gathered, bf16[4096,128]{1,0:T(8,128)(2,1)S(1)} %get-tuple-element.24.maps, bf16[1024,128]{1,0:T(8,128)(2,1)S(1)} %get-tuple-element.25.spread, f32[32,512]{1,0:T(8,128)S(1)} %get-tuple-element.26.local, ...), custom_call_target="tpu_custom_call" | custom-call | bytes 2162688 | tf_op jit(solution)/shard_map/field/pallas_call | solution.py:273
  (7 shorter events, 0.1 us)
Async XLA Ops:
  0.0 0.8 %copy-start = (f32[2,64,64]{2,1,0:T(8,128)S(1)}, f32[2,64,64]{2,1,0:T(8,128)}, u32[]{:S(2)}) copy-start(f32[2,64,64]{2,1,0:T(8,128)} %transfer_hbm.3) | copy-start | bytes 98308
  0.8 0.9 %copy-start.2 = (bf16[8,64,256]{2,1,0:T(8,128)(2,1)S(1)}, bf16[8,64,256]{2,1,0:T(8,128)(2,1)}, u32[]{:S(2)}) copy-start(bf16[8,64,256]{2,1,0:T(8,128)(2,1)} %basis_hbm.1) | copy-start | bytes 786436
  3.2 15.0 %collective-permute-start = (bf16[1,32,128]{2,1,0:T(8,128)(2,1)S(1)}, bf16[1,32,128]{2,1,0:T(8,128)(2,1)S(1)}, u32[]{:S(2)}, u32[]{:S(2)}) collective-permute-start(bf16[1,32,128]{2,1,0:T(8,128)(2,1)S(1)} %get-tuple-element.19.coeffs), channel_id=1, source_target_pairs={{0,8},{1,9},{2,10},{3,11},{4,12},{5,13},{6,14},{7,15},{8,0},{9,1},... | collective-permute-start | bytes 24584 | tf_op jit(solution)/shard_map/ppermute | solution.py:307
  6.3 12.0 %collective-permute-start.1 = (bf16[1,32,128]{2,1,0:T(8,128)(2,1)S(1)}, bf16[1,32,128]{2,1,0:T(8,128)(2,1)S(1)}, u32[]{:S(2)}, u32[]{:S(2)}) collective-permute-start(bf16[1,32,128]{2,1,0:T(8,128)(2,1)S(1)} %get-tuple-element.19.coeffs), channel_id=1, source_target_pairs={{0,16},{1,17},{2,18},{3,19},{4,20},{5,21},{6,22},{7,23},{8,24},{9,... | collective-permute-start | bytes 24584 | tf_op jit(solution)/shard_map/ppermute | solution.py:307
  8.9 9.4 %collective-permute-start.2 = (bf16[1,32,128]{2,1,0:T(8,128)(2,1)S(1)}, bf16[1,32,128]{2,1,0:T(8,128)(2,1)S(1)}, u32[]{:S(2)}, u32[]{:S(2)}) collective-permute-start(bf16[1,32,128]{2,1,0:T(8,128)(2,1)S(1)} %get-tuple-element.19.coeffs), channel_id=1, source_target_pairs={{0,24},{1,25},{2,26},{3,27},{4,28},{5,29},{6,30},{7,31},{8,16},{9,... | collective-permute-start | bytes 24584 | tf_op jit(solution)/shard_map/ppermute | solution.py:307
  8.9 18.1 %collective-permute-start.7 = (bf16[32,2048]{1,0:T(8,128)(2,1)}, bf16[32,2048]{1,0:T(8,128)(2,1)S(1)}, u32[]{:S(2)}, u32[]{:S(2)}) collective-permute-start(bf16[32,2048]{1,0:T(8,128)(2,1)} %own.1), channel_id=1, source_target_pairs={{0,1},{1,2},{2,3},{3,4},{4,5},{5,6},{6,7},{7,8},{8,9},{9,10},{10,1... | collective-permute-start | bytes 393224 | tf_op jit(solution)/shard_map/ppermute | solution.py:307
  9.5 0.8 %copy-start.1 = (f32[2,64,64]{2,1,0:T(8,128)S(1)}, f32[2,64,64]{2,1,0:T(8,128)}, u32[]{:S(2)}) copy-start(f32[2,64,64]{2,1,0:T(8,128)} %transfer_hbm.3) | copy-start | bytes 98308
  10.4 0.9 %copy-start.3 = (f32[8,64,64]{2,1,0:T(8,128)S(1)}, f32[8,64,64]{2,1,0:T(8,128)}, u32[]{:S(2)}) copy-start(f32[8,64,64]{2,1,0:T(8,128)} %coupling_hbm.1) | copy-start | bytes 393220
  11.3 0.8 %copy-start.4 = (f32[2,64,64]{2,1,0:T(8,128)S(1)}, f32[2,64,64]{2,1,0:T(8,128)}, u32[]{:S(2)}) copy-start(f32[2,64,64]{2,1,0:T(8,128)} %sibling_hbm.1) | copy-start | bytes 98308
  12.2 0.7 %copy-start.5 = (s32[1,3]{1,0:T(1,128)S(1)}, s32[1,3]{1,0:T(1,128)}, u32[]{:S(2)}) copy-start(s32[1,3]{1,0:T(1,128)} %offsets_hbm.1) | copy-start | bytes 40
  12.8 0.7 %copy-start.6 = (s32[1,3]{1,0:T(1,128)S(1)}, s32[1,3]{1,0:T(1,128)}, u32[]{:S(2)}) copy-start(s32[1,3]{1,0:T(1,128)} %classes_hbm.1) | copy-start | bytes 40
  13.5 0.7 %copy-start.7 = (s32[16]{0:T(128)S(1)}, s32[16]{0:T(128)}, u32[]{:S(2)}) copy-start(s32[16]{0:T(128)} %targets_hbm.1) | copy-start | bytes 196
  14.1 0.7 %copy-start.8 = (s32[16]{0:T(128)S(1)}, s32[16]{0:T(128)}, u32[]{:S(2)}) copy-start(s32[16]{0:T(128)} %sources_hbm.1) | copy-start | bytes 196
  18.3 8.5 %collective-permute-start.3 = (bf16[4,32,128]{2,1,0:T(8,128)(2,1)S(1)}, bf16[4,32,128]{2,1,0:T(8,128)(2,1)S(1)}, u32[]{:S(2)}, u32[]{:S(2)}) collective-permute-start(bf16[4,32,128]{2,1,0:T(8,128)(2,1)S(1)} %pad_maximum_fusion.1), channel_id=1, source_target_pairs={{0,2},{1,3},{2,0},{3,1},{4,6},{5,7},{6,4},{7,5},{8,10},{9,11},{10,... | collective-permute-start | bytes 98312 | tf_op jit(solution)/shard_map/ppermute | solution.py:307
  20.1 6.7 %collective-permute-start.4 = (bf16[4,32,128]{2,1,0:T(8,128)(2,1)S(1)}, bf16[4,32,128]{2,1,0:T(8,128)(2,1)S(1)}, u32[]{:S(2)}, u32[]{:S(2)}) collective-permute-start(bf16[4,32,128]{2,1,0:T(8,128)(2,1)S(1)} %pad_maximum_fusion.1), channel_id=1, source_target_pairs={{0,4},{1,5},{2,6},{3,7},{4,0},{5,1},{6,2},{7,3},{8,12},{9,13},{10,... | collective-permute-start | bytes 98312 | tf_op jit(solution)/shard_map/ppermute | solution.py:307
  21.6 5.2 %collective-permute-start.5 = (bf16[4,32,128]{2,1,0:T(8,128)(2,1)S(1)}, bf16[4,32,128]{2,1,0:T(8,128)(2,1)S(1)}, u32[]{:S(2)}, u32[]{:S(2)}) collective-permute-start(bf16[4,32,128]{2,1,0:T(8,128)(2,1)S(1)} %pad_maximum_fusion.1), channel_id=1, source_target_pairs={{0,6},{1,7},{2,4},{3,5},{4,2},{5,3},{6,0},{7,1},{8,14},{9,15},{10,... | collective-permute-start | bytes 98312 | tf_op jit(solution)/shard_map/ppermute | solution.py:307
  21.8 7.8 %collective-permute-start.8 = (bf16[32,2048]{1,0:T(8,128)(2,1)}, bf16[32,2048]{1,0:T(8,128)(2,1)S(1)}, u32[]{:S(2)}, u32[]{:S(2)}) collective-permute-start(bf16[32,2048]{1,0:T(8,128)(2,1)} %own.1), channel_id=1, source_target_pairs={{0,31},{1,0},{2,1},{3,2},{4,3},{5,4},{6,5},{7,6},{8,7},{9,8},{10,9... | collective-permute-start | bytes 393224 | tf_op jit(solution)/shard_map/ppermute | solution.py:307
  26.8 4.9 %collective-permute-start.6 = (bf16[16,32,128]{2,1,0:T(8,128)(2,1)S(1)}, bf16[16,32,128]{2,1,0:T(8,128)(2,1)S(1)}, u32[]{:S(2)}, u32[]{:S(2)}) collective-permute-start(bf16[16,32,128]{2,1,0:T(8,128)(2,1)S(1)} %pad_maximum_fusion), channel_id=1, source_target_pairs={{0,1},{1,0},{2,3},{3,2},{4,5},{5,4},{6,7},{7,6},{8,9},{9,8},{10,11... | collective-permute-start | bytes 393224 | tf_op jit(solution)/shard_map/ppermute | solution.py:307

commit v2 on v1

--- a/solution.py
+++ b/solution.py
@@ -111,7 +111,6 @@
     classes_hbm,
     targets_hbm,
     sources_hbm,
-    live_hbm,
     transfer_hbm,
     sibling_hbm,
     coupling_hbm,
@@ -126,7 +125,6 @@
     passed,
     targets,
     sources,
-    live,
     offsets,
     classes,
     transfer,
@@ -143,7 +141,6 @@
         (coupling_hbm, coupling),
         (targets_hbm, targets),
         (sources_hbm, sources),
-        (live_hbm, live),
         (tiles_hbm, tiles),
     )
     copies = [pltpu.make_async_copy(a, b, sems.at[i]) for i, (a, b) in enumerate(pairs)]
@@ -265,11 +262,15 @@
         field[:, b * points : (b + 1) * points] = near[b] + far
 
 
-SPACES = {"v": pltpu.VMEM, "s": pltpu.SMEM, "h": pltpu.HBM}
+SPACES = {"v": pltpu.VMEM, "s": pltpu.SMEM, "h": pl.ANY}
 
 
 def call(kernel, name, kinds, args, outs, scratch=(), flops=0):
     moved = sum(x.size * x.dtype.itemsize for x in args)
+    args = [
+        pltpu.with_memory_space_constraint(x, pltpu.HBM) if kind == "h" else x
+        for kind, x in zip(kinds, args)
+    ]
     return pl.pallas_call(
         kernel,
         name=name,
@@ -310,7 +311,7 @@
         return send(x, lambda i: i ^ mask)
 
     before = send(vectors, lambda i: (i + 1) % count)
-    coeffs, leaf, basis, paths = call(
+    coeffs, leaf, basis, paths, own = call(
         leaf_kernel,
         "leaf",
         "hhh",
@@ -320,22 +321,22 @@
             ("v", (boxes, columns, rank), F32),
             ("v", leaf_basis.shape, BF16),
             ("v", (steps, boxes * rank, double), F32),
+            ("v", vectors.shape, BF16),
         ),
-        scratch=(pltpu.VMEM(vectors.shape, BF16), pltpu.VMEM(transfer.shape, F32), dma((3,))),
+        scratch=(pltpu.VMEM(transfer.shape, F32), dma((3,))),
     )
     device = lax.axis_index(AXES).astype(jnp.int32).reshape(1)
     ints = jnp.int32
-    maps, spread, local, tiles, passed, targets, sources, live = call(
+    maps, spread, local, tiles, passed, targets, sources = call(
         functools.partial(map_kernel, bits),
         "maps",
-        "shhhhhhhhhvvv",
+        "shhhhhhhhvvv",
         (
             device,
             couple_offset,
             couple_class,
             tile_target,
             tile_source,
-            tile_count,
             transfer,
             sibling_coupling,
             list_coupling,
@@ -352,7 +353,6 @@
             ("v", coeffs.shape, BF16),
             ("s", tile_target.shape, ints),
             ("s", tile_source.shape, ints),
-            ("s", tile_count.shape, ints),
         ),
         scratch=(
             pltpu.SMEM(couple_offset.shape, ints),
@@ -360,7 +360,7 @@
             pltpu.VMEM(transfer.shape, F32),
             pltpu.VMEM(sibling_coupling.shape, F32),
             pltpu.VMEM(list_coupling.shape, F32),
-            dma((9,)),
+            dma((8,)),
         ),
     )
     gathered = coeffs
@@ -377,7 +377,7 @@
         near_kernel,
         "near",
         "sssvvvv",
-        (live, targets, sources, before, vectors, after, tiles),
+        (tile_count, targets, sources, before, own, after, tiles),
         (("v", (boxes, columns, points), F32),),
         scratch=(pltpu.VMEM((3 * boxes, columns, points), BF16),),
     )

time: 33.7 us -> 26.1 us (0.77)
  local copies, waits for them, and re-layouts: 7.08 us -> 0.06 us
  starting transfers between devices: 14.2 us -> 13.6 us
    unnamed x22 -> x6, local copies, waits for them, and re-layouts: 7.07 us -> 0.04 us
    ppermute x9, starting transfers between devices: 14.2 us -> 13.6 us  [send(): return lax.ppermute(x, AXES, [(i, target(i)) for i in range(count)])]
  transfers between devices with their start and end apart: 9 -> 9, of which waited for: 1 -> 2; matrix products, arithmetic and copies ran while one was open for 0% -> 0% of each run, Pallas kernels for 17% -> 20%
where the time goes in v2:
time: 26.1 us; the launch traced here: 26 us
  starting transfers between devices  13.6 us (52%)
  Pallas kernels  8.49 us (33%)
  waiting for transfers between devices  3.01 us (12%)
  between operations  0.75 us (3%)
    ppermute x9, starting transfers between devices, send(): return lax.ppermute(x, AXES, [(i, target(i)) for i in range(count)])  13.6 us
    pallas_call x4, Pallas kernels, call(): pl.pallas_call(kernel, name=name, out_shape=[jax.ShapeDtypeStruct(shape,...  8.49 us
    ppermute x9, waiting for transfers between devices, send(): return lax.ppermute(x, AXES, [(i, target(i)) for i in range(count)])  3.01 us
  transfers between devices with their start and end apart: 9, of which 2 were waited for; matrix products, arithmetic and copies ran while one was open for 0% of the time, Pallas kernels for 20%

profile of v2, /device:TPU:0, one launch (start us, length us, event | category | flops | bytes accessed | tf_op | source)
XLA Modules:
  0.0 26.0 jit_solution(4338797914135465942)
XLA Ops:
  0.0 0.0 copy-start
  0.0 1.8 %leaf.1 = (bf16[1,32,128]{2,1,0:T(8,128)(2,1)S(1)}, f32[8,32,64]{2,1,0:T(8,128)S(1)}, bf16[8,64,256]{2,1,0:T(8,128)(2,1)S(1)}, f32[3,512,128]{2,1,0:T(8,128)S(1)}, bf16[32,2048]{1,0:T(8,128)(2,1)S(1)}) custom-call(bf16[32,2048]{1,0:T(8,128)(2,1)} %vectors_hbm.1, bf16[8,64,256]{2,1,0:T(8,128)(2,1)} %basis_hbm.1, f32[2,64,64]{2,1,0:T(8,128)} %transfer_hbm.3), custom_call_target="tpu_custom_call" | custom-call | bytes 425984 | tf_op jit(solution)/shard_map/leaf/pallas_call | solution.py:274
  1.9 3.1 %collective-permute-start = (bf16[1,32,128]{2,1,0:T(8,128)(2,1)S(1)}, bf16[1,32,128]{2,1,0:T(8,128)(2,1)S(1)}, u32[]{:S(2)}, u32[]{:S(2)}) collective-permute-start(bf16[1,32,128]{2,1,0:T(8,128)(2,1)S(1)} %get-tuple-element.19.coeffs), channel_id=1, source_target_pairs={{0,8},{1,9},{2,10},{3,11},{4,12},{5,13},{6,14},{7,15},{8,0},{9,1},... | collective-permute-start | bytes 24584 | tf_op jit(solution)/shard_map/ppermute | solution.py:308
  4.9 2.6 %collective-permute-start.1 = (bf16[1,32,128]{2,1,0:T(8,128)(2,1)S(1)}, bf16[1,32,128]{2,1,0:T(8,128)(2,1)S(1)}, u32[]{:S(2)}, u32[]{:S(2)}) collective-permute-start(bf16[1,32,128]{2,1,0:T(8,128)(2,1)S(1)} %get-tuple-element.19.coeffs), channel_id=1, source_target_pairs={{0,16},{1,17},{2,18},{3,19},{4,20},{5,21},{6,22},{7,23},{8,24},{9,... | collective-permute-start | bytes 24584 | tf_op jit(solution)/shard_map/ppermute | solution.py:308
  7.5 0.0 collective-permute-start.2
  7.5 0.0 collective-permute-start.7
  8.2 4.1 %maps.1 = (bf16[4096,128]{1,0:T(8,128)(2,1)S(1)}, bf16[1024,128]{1,0:T(8,128)(2,1)S(1)}, f32[32,512]{1,0:T(8,128)S(1)}, bf16[16,256,256]{2,1,0:T(8,128)(2,1)S(1)...) custom-call(s32[1]{0:T(128)} %bitcast.device, s32[1,3]{1,0:T(1,128)} %offsets_hbm.1, ...), custom_call_target="tpu_custom_call" | custom-call | bytes 3154076 | tf_op jit(solution)/shard_map/maps/pallas_call | solution.py:274
  12.3 0.0 collective-permute-done
  12.3 0.0 collective-permute-done.1
  12.3 0.6 %collective-permute-done.2 = bf16[1,32,128]{2,1,0:T(8,128)(2,1)S(1)} collective-permute-done((bf16[1,32,128]{2,1,0:T(8,128)(2,1)S(1)}, bf16[1,32,128]{2,1,0:T(8,128)(2,1)S(1)}, u32[]{:S(2)}, u32[]{:S(2)}) %collective-permute-start.2) | collective-permute-done | bytes 8224 | tf_op jit(solution)/shard_map/ppermute | solution.py:308
  13.0 1.6 %collective-permute-start.3 = (bf16[4,32,128]{2,1,0:T(8,128)(2,1)S(1)}, bf16[4,32,128]{2,1,0:T(8,128)(2,1)S(1)}, u32[]{:S(2)}, u32[]{:S(2)}) collective-permute-start(bf16[4,32,128]{2,1,0:T(8,128)(2,1)S(1)} %pad_maximum_fusion.1), channel_id=1, source_target_pairs={{0,2},{1,3},{2,0},{3,1},{4,6},{5,7},{6,4},{7,5},{8,10},{9,11},{10,... | collective-permute-start | bytes 98312 | tf_op jit(solution)/shard_map/ppermute | solution.py:308
  14.5 1.5 %collective-permute-start.4 = (bf16[4,32,128]{2,1,0:T(8,128)(2,1)S(1)}, bf16[4,32,128]{2,1,0:T(8,128)(2,1)S(1)}, u32[]{:S(2)}, u32[]{:S(2)}) collective-permute-start(bf16[4,32,128]{2,1,0:T(8,128)(2,1)S(1)} %pad_maximum_fusion.1), channel_id=1, source_target_pairs={{0,4},{1,5},{2,6},{3,7},{4,0},{5,1},{6,2},{7,3},{8,12},{9,13},{10,... | collective-permute-start | bytes 98312 | tf_op jit(solution)/shard_map/ppermute | solution.py:308
  16.1 0.5 %collective-permute-start.5 = (bf16[4,32,128]{2,1,0:T(8,128)(2,1)S(1)}, bf16[4,32,128]{2,1,0:T(8,128)(2,1)S(1)}, u32[]{:S(2)}, u32[]{:S(2)}) collective-permute-start(bf16[4,32,128]{2,1,0:T(8,128)(2,1)S(1)} %pad_maximum_fusion.1), channel_id=1, source_target_pairs={{0,6},{1,7},{2,4},{3,5},{4,2},{5,3},{6,0},{7,1},{8,14},{9,15},{10,... | collective-permute-start | bytes 98312 | tf_op jit(solution)/shard_map/ppermute | solution.py:308
  16.5 0.0 copy-done
  16.5 4.3 %collective-permute-start.8 = (bf16[32,2048]{1,0:T(8,128)(2,1)S(1)}, bf16[32,2048]{1,0:T(8,128)(2,1)S(1)}, u32[]{:S(2)}, u32[]{:S(2)}) collective-permute-start(bf16[32,2048]{1,0:T(8,128)(2,1)S(1)} %copy-done), channel_id=1, source_target_pairs={{0,31},{1,0},{2,1},{3,2},{4,3},{5,4},{6,5},{7,6},{8,7},{9,8},{10,9... | collective-permute-start | bytes 393224 | tf_op jit(solution)/shard_map/ppermute | solution.py:308
  20.9 0.0 collective-permute-done.3
  20.9 0.0 collective-permute-done.4
  20.9 0.0 collective-permute-done.5
  20.9 0.1 collective-permute-start.6
  21.0 0.0 collective-permute-done.7.before
  21.0 2.3 %collective-permute-done.8.after = bf16[32,2048]{1,0:T(8,128)(2,1)S(1)} collective-permute-done((bf16[32,2048]{1,0:T(8,128)(2,1)S(1)}, bf16[32,2048]{1,0:T(8,128)(2,1)S(1)}, u32[]{:S(2)}, u32[]{:S(2)}) %collective-permute-start.8) | collective-permute-done | bytes 131104 | tf_op jit(solution)/shard_map/ppermute | solution.py:308
  23.4 1.0 %near.1 = f32[8,32,256]{2,1,0:T(8,128)S(1)} custom-call(s32[1]{0:T(128)S(6)} %copy.16.live, s32[16]{0:T(128)S(1)} %get-tuple-element.28.targets, s32[16]{0:T(128)S(1)} %get-tuple-element.29.sources, bf16[32,2048]{1,0:T(8,128)(2,1)S(1)} %collective-permute-done.7.before, bf16[32,2048]{1,0:T(8,128)(2,1)S(1)} %get-tuple-element.30.own, ...), custom_call_target="tpu_custom_call" | custom-call | bytes 2490500 | tf_op jit(solution)/shard_map/near/pallas_call | solution.py:274
  24.4 0.0 collective-permute-done.6
  24.5 1.5 %field.1 = f32[32,2048]{1,0:T(8,128)} custom-call(bf16[32,32,128]{2,1,0:T(8,128)(2,1)S(1)} %constant_dynamic-update-slice_fusion.gathered, bf16[4096,128]{1,0:T(8,128)(2,1)S(1)} %get-tuple-element.24.maps, bf16[1024,128]{1,0:T(8,128)(2,1)S(1)} %get-tuple-element.25.spread, f32[32,512]{1,0:T(8,128)S(1)} %get-tuple-element.26.local, ...), custom_call_target="tpu_custom_call" | custom-call | bytes 2162688 | tf_op jit(solution)/shard_map/field/pallas_call | solution.py:274
  (7 shorter events, 0.1 us)
Async XLA Ops:
  0.0 16.5 %copy-start = (bf16[32,2048]{1,0:T(8,128)(2,1)S(1)}, bf16[32,2048]{1,0:T(8,128)(2,1)}, u32[]{:S(2)}) copy-start(bf16[32,2048]{1,0:T(8,128)(2,1)} %vectors_hbm.1) | copy-start | bytes 393220
  1.9 10.5 %collective-permute-start = (bf16[1,32,128]{2,1,0:T(8,128)(2,1)S(1)}, bf16[1,32,128]{2,1,0:T(8,128)(2,1)S(1)}, u32[]{:S(2)}, u32[]{:S(2)}) collective-permute-start(bf16[1,32,128]{2,1,0:T(8,128)(2,1)S(1)} %get-tuple-element.19.coeffs), channel_id=1, source_target_pairs={{0,8},{1,9},{2,10},{3,11},{4,12},{5,13},{6,14},{7,15},{8,0},{9,1},... | collective-permute-start | bytes 24584 | tf_op jit(solution)/shard_map/ppermute | solution.py:308
  4.9 7.4 %collective-permute-start.1 = (bf16[1,32,128]{2,1,0:T(8,128)(2,1)S(1)}, bf16[1,32,128]{2,1,0:T(8,128)(2,1)S(1)}, u32[]{:S(2)}, u32[]{:S(2)}) collective-permute-start(bf16[1,32,128]{2,1,0:T(8,128)(2,1)S(1)} %get-tuple-element.19.coeffs), channel_id=1, source_target_pairs={{0,16},{1,17},{2,18},{3,19},{4,20},{5,21},{6,22},{7,23},{8,24},{9,... | collective-permute-start | bytes 24584 | tf_op jit(solution)/shard_map/ppermute | solution.py:308
  7.5 5.4 %collective-permute-start.2 = (bf16[1,32,128]{2,1,0:T(8,128)(2,1)S(1)}, bf16[1,32,128]{2,1,0:T(8,128)(2,1)S(1)}, u32[]{:S(2)}, u32[]{:S(2)}) collective-permute-start(bf16[1,32,128]{2,1,0:T(8,128)(2,1)S(1)} %get-tuple-element.19.coeffs), channel_id=1, source_target_pairs={{0,24},{1,25},{2,26},{3,27},{4,28},{5,29},{6,30},{7,31},{8,16},{9,... | collective-permute-start | bytes 24584 | tf_op jit(solution)/shard_map/ppermute | solution.py:308
  7.5 13.5 %collective-permute-start.7 = (bf16[32,2048]{1,0:T(8,128)(2,1)}, bf16[32,2048]{1,0:T(8,128)(2,1)S(1)}, u32[]{:S(2)}, u32[]{:S(2)}) collective-permute-start(bf16[32,2048]{1,0:T(8,128)(2,1)} %vectors_hbm.1), channel_id=1, source_target_pairs={{0,1},{1,2},{2,3},{3,4},{4,5},{5,6},{6,7},{7,8},{8,9},{9,10},{10,1... | collective-permute-start | bytes 393224 | tf_op jit(solution)/shard_map/ppermute | solution.py:308
  13.0 7.9 %collective-permute-start.3 = (bf16[4,32,128]{2,1,0:T(8,128)(2,1)S(1)}, bf16[4,32,128]{2,1,0:T(8,128)(2,1)S(1)}, u32[]{:S(2)}, u32[]{:S(2)}) collective-permute-start(bf16[4,32,128]{2,1,0:T(8,128)(2,1)S(1)} %pad_maximum_fusion.1), channel_id=1, source_target_pairs={{0,2},{1,3},{2,0},{3,1},{4,6},{5,7},{6,4},{7,5},{8,10},{9,11},{10,... | collective-permute-start | bytes 98312 | tf_op jit(solution)/shard_map/ppermute | solution.py:308
  14.5 6.3 %collective-permute-start.4 = (bf16[4,32,128]{2,1,0:T(8,128)(2,1)S(1)}, bf16[4,32,128]{2,1,0:T(8,128)(2,1)S(1)}, u32[]{:S(2)}, u32[]{:S(2)}) collective-permute-start(bf16[4,32,128]{2,1,0:T(8,128)(2,1)S(1)} %pad_maximum_fusion.1), channel_id=1, source_target_pairs={{0,4},{1,5},{2,6},{3,7},{4,0},{5,1},{6,2},{7,3},{8,12},{9,13},{10,... | collective-permute-start | bytes 98312 | tf_op jit(solution)/shard_map/ppermute | solution.py:308
  16.1 4.8 %collective-permute-start.5 = (bf16[4,32,128]{2,1,0:T(8,128)(2,1)S(1)}, bf16[4,32,128]{2,1,0:T(8,128)(2,1)S(1)}, u32[]{:S(2)}, u32[]{:S(2)}) collective-permute-start(bf16[4,32,128]{2,1,0:T(8,128)(2,1)S(1)} %pad_maximum_fusion.1), channel_id=1, source_target_pairs={{0,6},{1,7},{2,4},{3,5},{4,2},{5,3},{6,0},{7,1},{8,14},{9,15},{10,... | collective-permute-start | bytes 98312 | tf_op jit(solution)/shard_map/ppermute | solution.py:308
  16.5 6.8 %collective-permute-start.8 = (bf16[32,2048]{1,0:T(8,128)(2,1)S(1)}, bf16[32,2048]{1,0:T(8,128)(2,1)S(1)}, u32[]{:S(2)}, u32[]{:S(2)}) collective-permute-start(bf16[32,2048]{1,0:T(8,128)(2,1)S(1)} %copy-done), channel_id=1, source_target_pairs={{0,31},{1,0},{2,1},{3,2},{4,3},{5,4},{6,5},{7,6},{8,7},{9,8},{10,9... | collective-permute-start | bytes 393224 | tf_op jit(solution)/shard_map/ppermute | solution.py:308
  20.9 3.5 %collective-permute-start.6 = (bf16[16,32,128]{2,1,0:T(8,128)(2,1)S(1)}, bf16[16,32,128]{2,1,0:T(8,128)(2,1)S(1)}, u32[]{:S(2)}, u32[]{:S(2)}) collective-permute-start(bf16[16,32,128]{2,1,0:T(8,128)(2,1)S(1)} %pad_maximum_fusion), channel_id=1, source_target_pairs={{0,1},{1,0},{2,3},{3,2},{4,5},{5,4},{6,7},{7,6},{8,9},{9,8},{10,11... | collective-permute-start | bytes 393224 | tf_op jit(solution)/shard_map/ppermute | solution.py:308

commit v3 on v2

v3 whole, which is shorter than its diff:
```python
import functools

import jax
import jax.numpy as jnp
from jax import lax
from jax.experimental import pallas as pl
from jax.experimental.pallas import tpu as pltpu
from jax.sharding import PartitionSpec as P

AXES = ("leaf", "grp")
F32 = jnp.float32
BF16 = jnp.bfloat16
NN = (((1,), (0,)), ((), ()))
NT = (((1,), (1,)), ((), ()))
CHUNK = 512
STACK = 6 * 2**20


def split(x):
    high = x.astype(BF16)
    return high, (x - high.astype(F32)).astype(BF16)


def dot(a, b, dims=NN):
    return lax.dot_general(a, b, dims, preferred_element_type=F32)


def dot3(a, b, dims=NN):
    a_high, a_low = split(a)
    b_high, b_low = split(b)
    return dot(a_high, b_high, dims) + (dot(a_low, b_high, dims) + dot(a_high, b_low, dims))


def rounds_of(bits):
    rounds = []
    top = bits
    while top > 0:
        wide = 2 if top > 1 else 1
        rounds.append((top - wide, wide))
        top -= wide
    return rounds


def masks_of(bits):
    masks = [0]
    for low, wide in rounds_of(bits):
        masks = [mask ^ (step << low) for step in range(2**wide) for mask in masks]
    return masks


def place_of(mask, bits):
    place, shift = 0, 0
    for low, wide in rounds_of(bits):
        place = place | (((mask >> low) & (2**wide - 1)) << shift)
        shift += wide
    return place


def up(blocks, transfer):
    left = jnp.concatenate(blocks[0::2], axis=0)
    right = jnp.concatenate(blocks[1::2], axis=0)
    rows = blocks[0].shape[0]
    total = dot3(left, transfer[0]) + dot3(right, transfer[1])
    return [total[i * rows : (i + 1) * rows] for i in range(len(blocks) // 2)]


def high_low(double):
    high, low = split(double)
    lane = lax.broadcasted_iota(jnp.int32, double.shape, 1)
    return jnp.where(lane < double.shape[1] // 2, high, low)


def start_copies(pairs, sems):
    copies = [pltpu.make_async_copy(a, b, sems.at[i]) for i, (a, b) in enumerate(pairs)]
    for copy in copies:
        copy.start()
    return copies


def leaf_kernel(transfer_hbm, vectors_hbm, sibling_hbm, basis_hbm, transfer, vectors, sibling, send, leaf, *refs):
    *paths, basis, sems = refs
    boxes, rank, points = basis.shape
    steps = boxes.bit_length() - 1
    pairs = ((transfer_hbm, transfer), (vectors_hbm, vectors), (basis_hbm, basis), (sibling_hbm, sibling))
    copies = start_copies(pairs, sems)
    copies[0].wait()
    t0, t1 = transfer[0], transfer[1]
    stack = jnp.concatenate([t0, t1], axis=0)
    for height in range(1, steps):
        paths[height - 1][...] = jnp.concatenate([stack, stack], axis=1)
        stack = jnp.concatenate([dot3(stack, t0), dot3(stack, t1)], axis=0)
    double = jnp.concatenate([stack, stack], axis=1)
    paths[steps - 1][...] = double
    weights, rest = split(double)
    copies[1].wait()
    copies[2].wait()
    high, low = [], []
    for b in range(boxes):
        coeffs = dot(vectors[:, b * points : (b + 1) * points], basis[b], NT)
        leaf[b] = coeffs
        one, other = split(coeffs)
        high.append(one)
        low.append(other)
    high = jnp.concatenate(high, axis=1)
    low = jnp.concatenate(low, axis=1)
    send[0] = high_low(dot(high, weights) + (dot(low, weights) + dot(high, rest)))
    copies[3].wait()


def down_kernel(coeffs, leaf, paths, transfer, sibling, before, spread, local, passed):
    boxes, columns, rank = leaf.shape
    half = boxes * rank
    passed[...] = coeffs[...]
    high, low = split(paths[...])
    spread[:half] = high
    spread[half:] = low
    t0, t1 = transfer[0], transfer[1]
    levels = [[leaf[b] for b in range(boxes)]]
    while len(levels[-1]) > 2:
        levels.append(up(levels[-1], (t0, t1)))
    s0, s1 = sibling[0], sibling[1]
    down = None
    for level in reversed(levels):
        across0 = dot3(jnp.concatenate(level[1::2], axis=0), s0)
        across1 = dot3(jnp.concatenate(level[0::2], axis=0), s1)
        if down is not None:
            parents = jnp.concatenate(down, axis=0)
            across0 = across0 + dot3(parents, t0, NT)
            across1 = across1 + dot3(parents, t1, NT)
        down = []
        for i in range(len(level) // 2):
            down.append(across0[i * columns : (i + 1) * columns])
            down.append(across1[i * columns : (i + 1) * columns])
    for b in range(boxes):
        local[:, b * rank : (b + 1) * rank] = down[b]


def map_kernel(bits, device, *refs):
    hbm, (gathered, transfer, sibling), paths = refs[:5], refs[5:8], refs[8:-9]
    maps, passed, places, *here, sems = refs[-9:]
    copies = start_copies(zip(hbm, here), sems)
    _, _, offsets, classes, coupling = here
    rank = transfer.shape[1]
    passed[...] = gathered[...]
    me = device[0]
    count = 2**bits
    steps = len(paths)
    boxes = 2**steps

    def put(at, double):
        both = high_low(double)
        if not isinstance(at, int):
            at = pl.multiple_of(at * 2 * rank, 2 * rank)
        else:
            at = at * 2 * rank
        maps[pl.ds(at, rank)] = both
        maps[pl.ds(at + rank, rank)] = both

    def twice(x):
        return jnp.concatenate([x, x], axis=1)

    def place(height, low):
        return place_of((1 << height) | (low ^ (me & ((1 << height) - 1))), bits)

    sides = []
    for height in range(1, steps + 1):
        tall = paths[height - 1][...]
        sides.append(jnp.concatenate([high_low(tall), tall.astype(BF16)], axis=1))

    def climb(height, fan):
        fan_high, fan_low = split(fan)
        weights = jnp.concatenate([fan_high, fan_high, fan_low, jnp.zeros_like(fan_low)], axis=0)
        return dot(sides[height - 1], weights)

    t0, t1 = transfer[0], transfer[1]

    def path(height):
        if height <= steps:
            at = pl.multiple_of((me & ((1 << height) - 1)) * rank, rank)
            return paths[height - 1][pl.ds(at, rank), :rank]
        return dot3(path(height - 1), transfer[(me >> (height - 1)) & 1])

    wide = []
    for height in range(1, bits):
        mine = sibling[(me >> height) & 1]
        bridge = twice(dot3(mine, path(height), NT))
        fans = [bridge]
        for step in range(height - 1, steps - 1, -1):
            fans = [dot3(t, fan) for fan in fans for t in (t0, t1)]
        if height < steps:
            block = climb(height, bridge)
            for i in range(2**height):
                put(place(height, i), block[i * rank : (i + 1) * rank])
        else:
            wide += [(height, j, fan) for j, fan in enumerate(fans)]
    for start in range(0, len(wide), 4):
        part = wide[start : start + 4]
        block = climb(steps, jnp.concatenate([fan for _, _, fan in part], axis=1))
        for k, (height, j, _) in enumerate(part):
            for i in range(boxes):
                one = block[i * rank : (i + 1) * rank, k * 2 * rank : (k + 1) * 2 * rank]
                put(place(height, (j << steps) + i), one)
    put(0, jnp.zeros((rank, 2 * rank), F32))
    put(place(0, 0), twice(sibling[me & 1]))
    for copy in copies:
        copy.wait()
    lane = lax.broadcasted_iota(jnp.int32, offsets.shape, 1)
    for i in range(offsets.shape[1]):
        offset = jnp.sum(jnp.where(lane == i, offsets[...], 0))
        kind = jnp.sum(jnp.where(lane == i, classes[...], 0))
        link = place_of(((me + offset + count) & (count - 1)) ^ me, bits)
        places[i] = jnp.full(places.shape[1:], link, jnp.int32)
        put(count + i, twice(coupling[kind]))


def near_kernel(live, targets, sources, before, own, after, tiles, gathered, near, window):
    slots, points, _ = tiles.shape
    boxes = near.shape[0]
    for i, part in enumerate((before, own, after)):
        for b in range(boxes):
            window[i * boxes + b] = part[:, b * points : (b + 1) * points]
    near[...] = jnp.zeros_like(near)
    for slot in range(slots):
        source = window[sources[slot]]
        source = jnp.where(slot < live[0], source, jnp.zeros_like(source))
        target = targets[slot]
        near[target] = near[target] + dot(source, tiles[slot])


def field_kernel(places, gathered, maps, spread, local, basis, near, field):
    count = gathered.shape[0]
    boxes, rank, points = basis.shape
    pairs = count // 2
    wide = 4 * rank

    def step(k):
        coeffs = jnp.concatenate([gathered[2 * k], gathered[2 * k + 1]], axis=1)
        return dot(coeffs, maps[pl.ds(k * wide, wide)])

    if pairs <= 32:
        both = step(0)
        for k in range(1, pairs):
            both = both + step(k)
    else:
        both = lax.fori_loop(1, pairs, lambda k, sums: sums + step(k), step(0))
    for i in range(places.shape[0]):
        rows = slice((count + i) * 2 * rank, (count + i + 1) * 2 * rank)
        both = both + dot(gathered[jnp.max(places[i])], maps[rows])
    summit = both[:, :rank] + both[:, rank:]
    doubled = dot(jnp.concatenate(split(summit), axis=1), spread[...], NT)
    half = boxes * rank
    rounded = (doubled[:, :half] + doubled[:, half:] + local[...]).astype(BF16)
    for b in range(boxes):
        far = dot(rounded[:, b * rank : (b + 1) * rank], basis[b])
        field[:, b * points : (b + 1) * points] = near[b] + far


SPACES = {"v": pltpu.VMEM, "s": pltpu.SMEM, "h": pl.ANY}


def call(kernel, name, kinds, args, outs, scratch=(), flops=0):
    moved = sum(x.size * x.dtype.itemsize for x in args)
    held = [x for x, kind in zip(args, kinds) if kind == "v"]
    held += [jax.ShapeDtypeStruct(shape, kind) for space, shape, kind in outs if space == "v"]
    limit = STACK + sum(x.size // x.shape[-1] * max(x.shape[-1], 128) * x.dtype.itemsize for x in held)
    args = [
        pltpu.with_memory_space_constraint(x, pltpu.HBM) if kind == "h" else x
        for kind, x in zip(kinds, args)
    ]
    return pl.pallas_call(
        kernel,
        name=name,
        out_shape=[jax.ShapeDtypeStruct(shape, kind) for _, shape, kind in outs],
        in_specs=[pl.BlockSpec(memory_space=SPACES[kind]) for kind in kinds],
        out_specs=[pl.BlockSpec(memory_space=SPACES[space]) for space, _, _ in outs],
        scratch_shapes=list(scratch),
        compiler_params=pltpu.CompilerParams(vmem_limit_bytes=limit),
        cost_estimate=pl.CostEstimate(flops=flops, bytes_accessed=moved, transcendentals=0),
    )(*args)


def body(
    vectors,
    leaf_basis,
    transfer,
    sibling_coupling,
    list_coupling,
    near_tiles,
    tile_target,
    tile_source,
    tile_count,
    couple_offset,
    couple_class,
):
    columns, width = vectors.shape
    boxes, rank, points = leaf_basis.shape
    count = lax.axis_size(AXES)
    bits = count.bit_length() - 1
    steps = boxes.bit_length() - 1
    double = 2 * rank
    dma = pltpu.SemaphoreType.DMA

    def send(x, target):
        return lax.ppermute(x, AXES, [(i, target(i)) for i in range(count)])

    def swap(x, mask):
        return send(x, lambda i: i ^ mask)

    before = send(vectors, lambda i: (i + 1) % count)
    ints = jnp.int32
    plain = (transfer, vectors, sibling_coupling)
    transfer, own, sibling, coeffs, leaf, *paths = call(
        leaf_kernel,
        "leaf",
        "hhhh",
        (*plain, leaf_basis),
        (
            *(("v", x.shape, x.dtype) for x in plain),
            ("v", (1, columns, double), BF16),
            ("v", (boxes, columns, rank), F32),
            *(("v", (2**height * rank, double), F32) for height in range(1, steps + 1)),
        ),
        scratch=(pltpu.VMEM(leaf_basis.shape, BF16), dma((4,))),
    )
    device = lax.axis_index(AXES).astype(ints).reshape(1)
    spread, local, passed = call(
        down_kernel,
        "down",
        "vvvvvv",
        (coeffs, leaf, paths[-1], transfer, sibling, before),
        (
            ("v", (2 * boxes * rank, double), BF16),
            ("v", (columns, boxes * rank), F32),
            ("v", coeffs.shape, BF16),
        ),
    )
    lists = (tile_target, tile_source, couple_offset, couple_class)
    gathered = held = coeffs
    after = send(own, lambda i: (i - 1) % count)
    for index, (low, wide) in enumerate(rounds_of(bits)):
        held = gathered
        kept = passed if index == 0 else gathered
        if index == 1:
            links = couple_offset.shape[1]
            maps, kept, places, targets, sources = call(
                functools.partial(map_kernel, bits),
                "maps",
                "shhhhhvvv" + "v" * steps,
                (device, *lists, list_coupling, gathered, transfer, sibling, *paths),
                (
                    ("v", ((count + links) * double, double), BF16),
                    ("v", gathered.shape, BF16),
                    ("v", (links, 8, 128), ints),
                    ("v", tile_target.shape, ints),
                    ("v", tile_source.shape, ints),
                ),
                scratch=(
                    pltpu.VMEM(couple_offset.shape, ints),
                    pltpu.VMEM(couple_class.shape, ints),
                    pltpu.VMEM(list_coupling.shape, F32),
                    dma((5,)),
                ),
            )
        parts = {0: kept}
        for step in range(2**wide - 1, 0, -1):
            parts[step] = swap(gathered, step << low)
        gathered = jnp.concatenate([parts[step] for step in range(2**wide)], axis=0)
    (near,) = call(
        near_kernel,
        "near",
        "sssvvvvv",
        (tile_count, targets, sources, before, own, after, near_tiles, held),
        (("v", (boxes, columns, points), F32),),
        scratch=(pltpu.VMEM((3 * boxes, columns, points), BF16),),
    )
    (field,) = call(
        field_kernel,
        "field",
        "vvvvvvv",
        (places, gathered, maps, spread, local, leaf_basis, near),
        (("v", (columns, width), F32),),
    )
    return field


def solution(mesh):
    in_specs = (
        P(None, AXES),
        P(AXES, None, None),
        P(),
        P(),
        P(),
        P(AXES, None, None),
        P(AXES),
        P(AXES),
        P(AXES),
        P(AXES, None),
        P(AXES, None),
    )
    return jax.shard_map(body, mesh=mesh, in_specs=in_specs, out_specs=P(None, AXES), check_vma=False)
```

time: 26.1 us -> 24.6 us (0.943)
  waiting for transfers between devices: 3.01 us -> 1.21 us
  starting transfers between devices: 13.6 us -> 14 us
    ppermute x9, waiting for transfers between devices: 3.01 us -> 1.21 us  [send(): return lax.ppermute(x, AXES, [(i, target(i)) for i in range(count)])]
    ppermute x9, starting transfers between devices: 13.6 us -> 14 us  [send(): return lax.ppermute(x, AXES, [(i, target(i)) for i in range(count)])]
    pallas_call x4 -> x5, Pallas kernels: 8.49 us -> 8.3 us  [call(): pl.pallas_call(kernel, name=name, out_shape=[jax.ShapeDtypeStruct(shape,...]
  transfers between devices with their start and end apart: 9 -> 9, of which waited for: 2 -> 1; matrix products, arithmetic and copies ran while one was open for 0% -> 0% of each run, Pallas kernels for 20% -> 27%
where the time goes in v3:
time: 24.6 us; the launch traced here: 24.4 us
  starting transfers between devices  14 us (57%)
  Pallas kernels  8.3 us (34%)
  waiting for transfers between devices  1.21 us (5%)
  between operations  0.81 us (3%)
    ppermute x9, starting transfers between devices, send(): return lax.ppermute(x, AXES, [(i, target(i)) for i in range(count)])  14 us
    pallas_call x5, Pallas kernels, call(): pl.pallas_call(kernel, name=name, out_shape=[jax.ShapeDtypeStruct(shape,...  8.3 us
    ppermute x9, waiting for transfers between devices, send(): return lax.ppermute(x, AXES, [(i, target(i)) for i in range(count)])  1.21 us
  transfers between devices with their start and end apart: 9, of which 1 were waited for; matrix products, arithmetic and copies ran while one was open for 0% of the time, Pallas kernels for 27%

profile of v3, /device:TPU:0, one launch (start us, length us, event | category | flops | bytes accessed | tf_op | source)
XLA Modules:
  0.0 24.4 jit_solution(1577599278699544833)
XLA Ops:
  0.0 0.0 copy-start
  0.0 0.5 %collective-permute-start = (bf16[32,2048]{1,0:T(8,128)(2,1)}, bf16[32,2048]{1,0:T(8,128)(2,1)S(1)}, u32[]{:S(2)}, u32[]{:S(2)}) collective-permute-start(bf16[32,2048]{1,0:T(8,128)(2,1)} %vectors_hbm.1), channel_id=1, source_target_pairs={{0,1},{1,2},{2,3},{3,4},{4,5},{5,6},{6,7},{7,8},{8,9},{9,10},{10,1... | collective-permute-start | bytes 393224 | tf_op jit(solution)/shard_map/ppermute | solution.py:304
  0.5 2.0 %leaf.1 = (f32[2,64,64]{2,1,0:T(8,128)S(1)}, bf16[32,2048]{1,0:T(8,128)(2,1)S(1)}, f32[2,64,64]{2,1,0:T(8,128)S(1)}, bf16[1,32,128]{2,1,0:T(8,128)(2,1)S(1)}, f3...) custom-call(f32[2,64,64]{2,1,0:T(8,128)} %transfer_hbm.1, ...), custom_call_target="tpu_custom_call" | custom-call | bytes 458752 | tf_op jit(solution)/shard_map/leaf/pallas_call | solution.py:270
  2.5 2.6 %collective-permute-start.1 = (bf16[1,32,128]{2,1,0:T(8,128)(2,1)S(1)}, bf16[1,32,128]{2,1,0:T(8,128)(2,1)S(1)}, u32[]{:S(2)}, u32[]{:S(2)}) collective-permute-start(bf16[1,32,128]{2,1,0:T(8,128)(2,1)S(1)} %get-tuple-element.21.coeffs), channel_id=1, source_target_pairs={{0,8},{1,9},{2,10},{3,11},{4,12},{5,13},{6,14},{7,15},{8,0},{9,1},... | collective-permute-start | bytes 24584 | tf_op jit(solution)/shard_map/ppermute | solution.py:304
  5.1 2.6 %collective-permute-start.2 = (bf16[1,32,128]{2,1,0:T(8,128)(2,1)S(1)}, bf16[1,32,128]{2,1,0:T(8,128)(2,1)S(1)}, u32[]{:S(2)}, u32[]{:S(2)}) collective-permute-start(bf16[1,32,128]{2,1,0:T(8,128)(2,1)S(1)} %get-tuple-element.21.coeffs), channel_id=1, source_target_pairs={{0,16},{1,17},{2,18},{3,19},{4,20},{5,21},{6,22},{7,23},{8,24},{9,... | collective-permute-start | bytes 24584 | tf_op jit(solution)/shard_map/ppermute | solution.py:304
  7.7 0.0 collective-permute-start.3
  7.7 4.7 %collective-permute-start.8 = (bf16[32,2048]{1,0:T(8,128)(2,1)S(1)}, bf16[32,2048]{1,0:T(8,128)(2,1)S(1)}, u32[]{:S(2)}, u32[]{:S(2)}) collective-permute-start(bf16[32,2048]{1,0:T(8,128)(2,1)S(1)} %get-tuple-element.36.own), channel_id=1, source_target_pairs={{0,31},{1,0},{2,1},{3,2},{4,3},{5,4},{6,5},{7,6},{8,7},{9,8},{10,9... | collective-permute-start | bytes 393224 | tf_op jit(solution)/shard_map/ppermute | solution.py:304
  12.4 0.0 collective-permute-done.before
  12.4 1.0 %down.1 = (bf16[1024,128]{1,0:T(8,128)(2,1)S(1)}, f32[32,512]{1,0:T(8,128)S(1)}, bf16[1,32,128]{2,1,0:T(8,128)(2,1)S(1)}) custom-call(bf16[1,32,128]{2,1,0:T(8,128)(2,1)S(1)} %get-tuple-element.21.coeffs, f32[8,32,64]{2,1,0:T(8,128)S(1)} %get-tuple-element.22.leaf, f32[512,128]{1,0:T(8,128)S(1)} %get-tuple-element.23.paths.refs_10_, ...), custom_call_target="tpu_custom_call" | custom-call | bytes 532480 | tf_op jit(solution)/shard_map/down/pallas_call | solution.py:270
  13.4 0.0 collective-permute-done.1
  13.4 0.0 collective-permute-done.2
  13.4 0.0 collective-permute-done.3
  13.4 1.2 %collective-permute-start.4 = (bf16[4,32,128]{2,1,0:T(8,128)(2,1)S(1)}, bf16[4,32,128]{2,1,0:T(8,128)(2,1)S(1)}, u32[]{:S(2)}, u32[]{:S(2)}) collective-permute-start(bf16[4,32,128]{2,1,0:T(8,128)(2,1)S(1)} %constant_dynamic-update-slice_fusion.refs_5_), channel_id=1, source_target_pairs={{0,2},{1,3},{2,0},{3,1},{4,6},{5,7},{6,4},{7,5},{8,10},{9,11},{10,... | collective-permute-start | bytes 98312 | tf_op jit(solution)/shard_map/ppermute | solution.py:304
  14.6 1.5 %collective-permute-start.5 = (bf16[4,32,128]{2,1,0:T(8,128)(2,1)S(1)}, bf16[4,32,128]{2,1,0:T(8,128)(2,1)S(1)}, u32[]{:S(2)}, u32[]{:S(2)}) collective-permute-start(bf16[4,32,128]{2,1,0:T(8,128)(2,1)S(1)} %constant_dynamic-update-slice_fusion.refs_5_), channel_id=1, source_target_pairs={{0,4},{1,5},{2,6},{3,7},{4,0},{5,1},{6,2},{7,3},{8,12},{9,13},{10,... | collective-permute-start | bytes 98312 | tf_op jit(solution)/shard_map/ppermute | solution.py:304
  16.1 0.9 %collective-permute-start.6 = (bf16[4,32,128]{2,1,0:T(8,128)(2,1)S(1)}, bf16[4,32,128]{2,1,0:T(8,128)(2,1)S(1)}, u32[]{:S(2)}, u32[]{:S(2)}) collective-permute-start(bf16[4,32,128]{2,1,0:T(8,128)(2,1)S(1)} %constant_dynamic-update-slice_fusion.refs_5_), channel_id=1, source_target_pairs={{0,6},{1,7},{2,4},{3,5},{4,2},{5,3},{6,0},{7,1},{8,14},{9,15},{10,... | collective-permute-start | bytes 98312 | tf_op jit(solution)/shard_map/ppermute | solution.py:304
  17.0 0.0 copy-start.1
  17.0 2.7 %maps.1 = (bf16[4480,128]{1,0:T(8,128)(2,1)S(1)}, bf16[4,32,128]{2,1,0:T(8,128)(2,1)S(1)}, s32[3,8,128]{2,1,0:T(8,128)S(1)}, s32[16]{0:T(128)S(1)}, s32[16]{0:T(128)S(1)}) custom-call(s32[1]{0:T(128)} %bitcast.device, s32[16]{0:T(128)} %refs_0_.1, s32[16]{0:T(128)} %refs_1_.1, s32[1,3]{1,0:T(1,128)} %refs_2_.1, s32[1,3]{1,0:T(1,128)} %refs_3_.1, ...), custom_call_target="tpu_custom_call" | custom-call | bytes 688284 | tf_op jit(solution)/shard_map/maps/pallas_call | solution.py:270
  19.7 0.0 collective-permute-done.4
  19.7 0.0 collective-permute-done.5
  19.8 1.2 %collective-permute-done.6 = bf16[4,32,128]{2,1,0:T(8,128)(2,1)S(1)} collective-permute-done((bf16[4,32,128]{2,1,0:T(8,128)(2,1)S(1)}, bf16[4,32,128]{2,1,0:T(8,128)(2,1)S(1)}, u32[]{:S(2)}, u32[]{:S(2)}) %collective-permute-start.6) | collective-permute-done | bytes 32800 | tf_op jit(solution)/shard_map/ppermute | solution.py:304
  21.0 0.1 collective-permute-start.7
  21.7 0.0 collective-permute-done.8.after
  21.7 0.0 copy-done
  21.7 1.0 %near.1 = f32[8,32,256]{2,1,0:T(8,128)S(1)} custom-call(s32[1]{0:T(128)S(6)} %copy.22.live, s32[16]{0:T(128)S(1)} %get-tuple-element.34.targets, s32[16]{0:T(128)S(1)} %get-tuple-element.35.sources, bf16[32,2048]{1,0:T(8,128)(2,1)S(1)} %collective-permute-done.before, bf16[32,2048]{1,0:T(8,128)(2,1)S(1)} %get-tuple-element.36.own, ...), custom_call_target="tpu_custom_call" | custom-call | bytes 2621572 | tf_op jit(solution)/shard_map/near/pallas_call | solution.py:270
  22.7 0.0 collective-permute-done.7
  22.8 0.0 copy-done.1
  22.8 1.6 %field.1 = f32[32,2048]{1,0:T(8,128)} custom-call(s32[3,8,128]{2,1,0:T(8,128)S(1)} %get-tuple-element.29.places, bf16[32,32,128]{2,1,0:T(8,128)(2,1)S(1)} %constant_dynamic-update-slice_fusion.8.gathered, bf16[4480,128]{1,0:T(8,128)(2,1)S(1)} %get-tuple-element.31.maps, bf16[1024,128]{1,0:T(8,128)(2,1)S(1)} %get-tuple-element.32.spread, ...), custom_call_target="tpu_custom_call" | custom-call | bytes 2273280 | tf_op jit(solution)/shard_map/field/pallas_call | solution.py:270
  (9 shorter events, 0.1 us)
Async XLA Ops:
  0.0 21.7 %copy-start = (bf16[16,256,256]{2,1,0:T(8,128)(2,1)S(1)}, bf16[16,256,256]{2,1,0:T(8,128)(2,1)}, u32[]{:S(2)}) copy-start(bf16[16,256,256]{2,1,0:T(8,128)(2,1)} %tiles.1) | copy-start | bytes 6291460
  0.0 12.4 %collective-permute-start = (bf16[32,2048]{1,0:T(8,128)(2,1)}, bf16[32,2048]{1,0:T(8,128)(2,1)S(1)}, u32[]{:S(2)}, u32[]{:S(2)}) collective-permute-start(bf16[32,2048]{1,0:T(8,128)(2,1)} %vectors_hbm.1), channel_id=1, source_target_pairs={{0,1},{1,2},{2,3},{3,4},{4,5},{5,6},{6,7},{7,8},{8,9},{9,10},{10,1... | collective-permute-start | bytes 393224 | tf_op jit(solution)/shard_map/ppermute | solution.py:304
  2.5 10.9 %collective-permute-start.1 = (bf16[1,32,128]{2,1,0:T(8,128)(2,1)S(1)}, bf16[1,32,128]{2,1,0:T(8,128)(2,1)S(1)}, u32[]{:S(2)}, u32[]{:S(2)}) collective-permute-start(bf16[1,32,128]{2,1,0:T(8,128)(2,1)S(1)} %get-tuple-element.21.coeffs), channel_id=1, source_target_pairs={{0,8},{1,9},{2,10},{3,11},{4,12},{5,13},{6,14},{7,15},{8,0},{9,1},... | collective-permute-start | bytes 24584 | tf_op jit(solution)/shard_map/ppermute | solution.py:304
  5.1 8.3 %collective-permute-start.2 = (bf16[1,32,128]{2,1,0:T(8,128)(2,1)S(1)}, bf16[1,32,128]{2,1,0:T(8,128)(2,1)S(1)}, u32[]{:S(2)}, u32[]{:S(2)}) collective-permute-start(bf16[1,32,128]{2,1,0:T(8,128)(2,1)S(1)} %get-tuple-element.21.coeffs), channel_id=1, source_target_pairs={{0,16},{1,17},{2,18},{3,19},{4,20},{5,21},{6,22},{7,23},{8,24},{9,... | collective-permute-start | bytes 24584 | tf_op jit(solution)/shard_map/ppermute | solution.py:304
  7.7 5.8 %collective-permute-start.3 = (bf16[1,32,128]{2,1,0:T(8,128)(2,1)S(1)}, bf16[1,32,128]{2,1,0:T(8,128)(2,1)S(1)}, u32[]{:S(2)}, u32[]{:S(2)}) collective-permute-start(bf16[1,32,128]{2,1,0:T(8,128)(2,1)S(1)} %get-tuple-element.21.coeffs), channel_id=1, source_target_pairs={{0,24},{1,25},{2,26},{3,27},{4,28},{5,29},{6,30},{7,31},{8,16},{9,... | collective-permute-start | bytes 24584 | tf_op jit(solution)/shard_map/ppermute | solution.py:304
  7.7 14.0 %collective-permute-start.8 = (bf16[32,2048]{1,0:T(8,128)(2,1)S(1)}, bf16[32,2048]{1,0:T(8,128)(2,1)S(1)}, u32[]{:S(2)}, u32[]{:S(2)}) collective-permute-start(bf16[32,2048]{1,0:T(8,128)(2,1)S(1)} %get-tuple-element.36.own), channel_id=1, source_target_pairs={{0,31},{1,0},{2,1},{3,2},{4,3},{5,4},{6,5},{7,6},{8,7},{9,8},{10,9... | collective-permute-start | bytes 393224 | tf_op jit(solution)/shard_map/ppermute | solution.py:304
  13.4 6.2 %collective-permute-start.4 = (bf16[4,32,128]{2,1,0:T(8,128)(2,1)S(1)}, bf16[4,32,128]{2,1,0:T(8,128)(2,1)S(1)}, u32[]{:S(2)}, u32[]{:S(2)}) collective-permute-start(bf16[4,32,128]{2,1,0:T(8,128)(2,1)S(1)} %constant_dynamic-update-slice_fusion.refs_5_), channel_id=1, source_target_pairs={{0,2},{1,3},{2,0},{3,1},{4,6},{5,7},{6,4},{7,5},{8,10},{9,11},{10,... | collective-permute-start | bytes 98312 | tf_op jit(solution)/shard_map/ppermute | solution.py:304
  14.6 5.1 %collective-permute-start.5 = (bf16[4,32,128]{2,1,0:T(8,128)(2,1)S(1)}, bf16[4,32,128]{2,1,0:T(8,128)(2,1)S(1)}, u32[]{:S(2)}, u32[]{:S(2)}) collective-permute-start(bf16[4,32,128]{2,1,0:T(8,128)(2,1)S(1)} %constant_dynamic-update-slice_fusion.refs_5_), channel_id=1, source_target_pairs={{0,4},{1,5},{2,6},{3,7},{4,0},{5,1},{6,2},{7,3},{8,12},{9,13},{10,... | collective-permute-start | bytes 98312 | tf_op jit(solution)/shard_map/ppermute | solution.py:304
  16.1 4.8 %collective-permute-start.6 = (bf16[4,32,128]{2,1,0:T(8,128)(2,1)S(1)}, bf16[4,32,128]{2,1,0:T(8,128)(2,1)S(1)}, u32[]{:S(2)}, u32[]{:S(2)}) collective-permute-start(bf16[4,32,128]{2,1,0:T(8,128)(2,1)S(1)} %constant_dynamic-update-slice_fusion.refs_5_), channel_id=1, source_target_pairs={{0,6},{1,7},{2,4},{3,5},{4,2},{5,3},{6,0},{7,1},{8,14},{9,15},{10,... | collective-permute-start | bytes 98312 | tf_op jit(solution)/shard_map/ppermute | solution.py:304
  17.0 5.8 %copy-start.1 = (bf16[8,64,256]{2,1,0:T(8,128)(2,1)S(1)}, bf16[8,64,256]{2,1,0:T(8,128)(2,1)}, u32[]{:S(2)}) copy-start(bf16[8,64,256]{2,1,0:T(8,128)(2,1)} %basis.1) | copy-start | bytes 786436
  21.0 1.8 %collective-permute-start.7 = (bf16[16,32,128]{2,1,0:T(8,128)(2,1)S(1)}, bf16[16,32,128]{2,1,0:T(8,128)(2,1)S(1)}, u32[]{:S(2)}, u32[]{:S(2)}) collective-permute-start(bf16[16,32,128]{2,1,0:T(8,128)(2,1)S(1)} %get-tuple-element.37.gathered), channel_id=1, source_target_pairs={{0,1},{1,0},{2,3},{3,2},{4,5},{5,4},{6,7},{7,6},{8,9},{9,8},{10,11... | collective-permute-start | bytes 393224 | tf_op jit(solution)/shard_map/ppermute | solution.py:304

commit v4 on v3

v4 whole, which is shorter than its diff:
```python
import functools

import jax
import jax.numpy as jnp
from jax import lax
from jax.experimental import pallas as pl
from jax.experimental.pallas import tpu as pltpu
from jax.sharding import PartitionSpec as P

AXES = ("leaf", "grp")
F32 = jnp.float32
BF16 = jnp.bfloat16
NN = (((1,), (0,)), ((), ()))
NT = (((1,), (1,)), ((), ()))
CHUNK = 512
STACK = 6 * 2**20


def split(x):
    high = x.astype(BF16)
    return high, (x - high.astype(F32)).astype(BF16)


def dot(a, b, dims=NN):
    return lax.dot_general(a, b, dims, preferred_element_type=F32)


def dot3(a, b, dims=NN):
    a_high, a_low = split(a)
    b_high, b_low = split(b)
    return dot(a_high, b_high, dims) + (dot(a_low, b_high, dims) + dot(a_high, b_low, dims))


def rounds_of(bits):
    rounds = []
    top = bits
    while top > 0:
        wide = 2 if top > 1 else 1
        rounds.append((top - wide, wide))
        top -= wide
    return rounds


def place_of(mask, bits):
    place, shift = 0, 0
    for low, wide in rounds_of(bits):
        place = place | ((-(mask >> low) & (2**wide - 1)) << shift)
        shift += wide
    return place


def up(blocks, transfer):
    left = jnp.concatenate(blocks[0::2], axis=0)
    right = jnp.concatenate(blocks[1::2], axis=0)
    rows = blocks[0].shape[0]
    total = dot3(left, transfer[0]) + dot3(right, transfer[1])
    return [total[i * rows : (i + 1) * rows] for i in range(len(blocks) // 2)]


def high_low(double):
    high, low = split(double)
    lane = lax.broadcasted_iota(jnp.int32, double.shape, 1)
    return jnp.where(lane < double.shape[1] // 2, high, low)


def twice(x):
    return jnp.concatenate([x, x], axis=1)


def both_halves(x):
    return x + pltpu.roll(x, x.shape[1] // 2, 1)


def start_copies(pairs, sems):
    copies = [pltpu.make_async_copy(a, b, sems.at[i]) for i, (a, b) in enumerate(pairs)]
    for copy in copies:
        copy.start()
    return copies


def leaf_kernel(transfer_hbm, vectors_hbm, sibling_hbm, basis_hbm, transfer, vectors, sibling, send, leaf, *refs):
    *paths, basis, sems = refs
    boxes, rank, points = basis.shape
    steps = boxes.bit_length() - 1
    pairs = ((transfer_hbm, transfer), (vectors_hbm, vectors), (basis_hbm, basis), (sibling_hbm, sibling))
    copies = start_copies(pairs, sems)
    copies[0].wait()
    t0, t1 = transfer[0], transfer[1]
    stack = jnp.concatenate([t0, t1], axis=0)
    for height in range(1, steps + 1):
        if height > 1:
            stack = jnp.concatenate([dot3(stack, t0), dot3(stack, t1)], axis=0)
        double = twice(stack)
        paths[height - 1][...] = double.reshape(paths[height - 1].shape)
    weights, rest = split(double)
    copies[1].wait()
    copies[2].wait()
    high, low = [], []
    for b in range(boxes):
        coeffs = dot(vectors[:, b * points : (b + 1) * points], basis[b], NT)
        leaf[b] = coeffs
        one, other = split(coeffs)
        high.append(one)
        low.append(other)
    high = jnp.concatenate(high, axis=1)
    low = jnp.concatenate(low, axis=1)
    send[0] = high_low(dot(high, weights) + (dot(low, weights) + dot(high, rest)))
    copies[3].wait()


def window_kernel(coeffs, before, own, window, passed):
    passed[...] = coeffs[...]
    boxes = window.shape[0] // 2
    points = window.shape[2]
    for i, part in enumerate((before, own)):
        for b in range(boxes):
            window[i * boxes + b] = part[:, b * points : (b + 1) * points]


def map_kernel(bits, device, *refs):
    hbm, (gathered, transfer, sibling), paths = refs[:5], refs[5:8], refs[8:-11]
    maps, rest, places, codes, passed, *here, sems = refs[-11:]
    copies = start_copies(zip(hbm, here), sems)
    _, _, offsets, classes, coupling = here
    rank = transfer.shape[1]
    passed[...] = gathered[...]
    me = device[0]
    side = me & 1
    pair = me >> 1
    count = 2**bits
    steps = len(paths)

    def put(table, at, double):
        both = high_low(double)
        if isinstance(at, int):
            at = at * 2 * rank
        else:
            at = pl.multiple_of(at * 2 * rank, 2 * rank)
        table[pl.ds(at, rank)] = both
        table[pl.ds(at + rank, rank)] = both

    def place(height, low):
        return place_of((1 << height) | (low ^ (pair & ((1 << height) - 1))), bits - 1)

    sides = []
    for height in range(1, steps + 1):
        tall = paths[height - 1][:, side].reshape(2 ** (height - 1) * rank, 2 * rank)
        sides.append(jnp.concatenate([high_low(tall), tall.astype(BF16)], axis=1))

    def climb(height, fan):
        fan_high, fan_low = split(fan)
        weights = jnp.concatenate([fan_high, fan_high, fan_low, jnp.zeros_like(fan_low)], axis=0)
        return dot(sides[height - 1], weights)

    t0, t1 = transfer[0], transfer[1]

    def path(height):
        if height <= steps:
            low = pair & ((1 << height) - 1)
            return paths[height - 1][low >> 1, low & 1][:, :rank]
        return dot3(path(height - 1), transfer[(pair >> (height - 1)) & 1])

    put(maps, 0, jnp.zeros((rank, 2 * rank), F32))
    wide = []
    for height in range(1, bits):
        bridge = sibling[(me >> height) & 1]
        if height > 1:
            bridge = dot3(bridge, path(height - 1), NT)
        fans = [twice(bridge)]
        for _ in range(height - steps):
            fans = [dot3(t, fan) for fan in fans for t in (t0, t1)]
        if height < steps:
            block = climb(height, fans[0])
            for i in range(2 ** (height - 1)):
                put(maps, place(height - 1, i), block[i * rank : (i + 1) * rank])
        else:
            wide += [(height, j, fan) for j, fan in enumerate(fans)]
    for start in range(0, len(wide), 4):
        part = wide[start : start + 4]
        block = climb(steps, jnp.concatenate([fan for _, _, fan in part], axis=1))
        for k, (height, j, _) in enumerate(part):
            for i in range(2 ** (steps - 1)):
                one = block[i * rank : (i + 1) * rank, k * 2 * rank : (k + 1) * 2 * rank]
                put(maps, place(height - 1, (j << (steps - 1)) + i), one)
    put(rest, 0, twice(sibling[side]))
    for copy in copies:
        copy.wait()
    lane = lax.broadcasted_iota(jnp.int32, offsets.shape, 1)
    for i in range(offsets.shape[1]):
        offset = jnp.sum(jnp.where(lane == i, offsets[...], 0))
        kind = jnp.sum(jnp.where(lane == i, classes[...], 0))
        mask = ((me + offset + count) & (count - 1)) ^ me
        here_too = (mask & 1) == 0
        link = jnp.where(here_too, place_of(mask >> 1, bits - 1), 0)
        places[i] = jnp.full(places.shape[1:], link, jnp.int32)
        code = jnp.where(here_too, 0, jnp.where(mask == 1, 1, 2))
        codes[i] = jnp.full(codes.shape[1:], code, jnp.int32)
        put(rest, 1 + i, twice(coupling[kind]))


def near_kernel(live, targets, sources, window, after, tiles, blocks, gathered, places, near, links, right):
    for i in range(links.shape[0]):
        links[i] = gathered[jnp.max(places[i])]
    slots, points, _ = tiles.shape
    boxes = near.shape[0]
    for b in range(boxes):
        right[b] = after[:, b * points : (b + 1) * points]
    near[...] = jnp.zeros_like(near)
    for slot in range(slots):
        box = sources[slot]
        inner = window[jnp.minimum(box, 2 * boxes - 1)]
        outer = right[jnp.maximum(box - 2 * boxes, 0)]
        source = jnp.where(box < 2 * boxes, inner, outer)
        source = jnp.where(slot < live[0], source, jnp.zeros_like(source))
        target = targets[slot]
        near[target] = near[target] + dot(source, tiles[slot])


def half_kernel(bits, device, gathered, maps, send, total):
    count = gathered.shape[0]
    wide = 2 * maps.shape[1]
    me = device[0]

    def step(k):
        coeffs = jnp.concatenate([gathered[2 * k], gathered[2 * k + 1]], axis=1)
        return dot(coeffs, maps[pl.ds(k * wide, wide)])

    pairs = count // 2
    if pairs <= 32:
        both = step(0)
        for k in range(1, pairs):
            both = both + step(k)
    else:
        both = lax.fori_loop(1, pairs, lambda k, sums: sums + step(k), step(0))
    sums = both_halves(both)
    total[...] = sums
    across = me + jnp.where((me & 1) == 1, -2, 2)
    mask = (across & (2**bits - 1)) ^ me
    send[0] = gathered[0]
    send[1] = gathered[place_of(mask >> 1, bits - 1)]
    send[2] = high_low(sums)


def down_kernel(device, leaf, paths, transfer, sibling, gathered, spread, local, passed):
    boxes, columns, rank = leaf.shape
    half = boxes * rank
    passed[...] = gathered[...]
    t0, t1 = transfer[0], transfer[1]
    s0, s1 = sibling[0], sibling[1]
    tall = paths[...].reshape(half, 2 * rank)
    high, low = split(tall)
    spread[:half, 2 * rank :] = high
    spread[half:, 2 * rank :] = low
    mine_high, mine_low = split(twice(transfer[device[0] & 1]))
    weights = jnp.concatenate([mine_high, mine_high, mine_low, jnp.zeros_like(mine_low)], axis=0)
    high, low = split(dot(jnp.concatenate([high_low(tall), high], axis=1), weights))
    spread[:half, : 2 * rank] = high
    spread[half:, : 2 * rank] = low
    levels = [[leaf[b] for b in range(boxes)]]
    while len(levels[-1]) > 2:
        levels.append(up(levels[-1], (t0, t1)))
    down = None
    for level in reversed(levels):
        across0 = dot3(jnp.concatenate(level[1::2], axis=0), s0)
        across1 = dot3(jnp.concatenate(level[0::2], axis=0), s1)
        if down is not None:
            parents = jnp.concatenate(down, axis=0)
            across0 = across0 + dot3(parents, t0, NT)
            across1 = across1 + dot3(parents, t1, NT)
        down = []
        for i in range(len(level) // 2):
            down.append(across0[i * columns : (i + 1) * columns])
            down.append(across1[i * columns : (i + 1) * columns])
    for b in range(boxes):
        local[:, b * rank : (b + 1) * rank] = down[b]


def field_kernel(other, links, codes, rest, total, spread, local, basis, near, field):
    boxes, rank, points = basis.shape
    parts = [other[0]]
    for i in range(links.shape[0]):
        code = codes[i]
        elsewhere = jnp.where(code == 1, other[0].astype(F32), other[1].astype(F32))
        parts.append(jnp.where(code == 0, links[i].astype(F32), elsewhere).astype(BF16))
    mine = both_halves(dot(jnp.concatenate(parts, axis=1), rest[...]))
    pair = total[...] + both_halves(other[2].astype(F32))
    doubled = dot(jnp.concatenate([high_low(pair), high_low(mine)], axis=1), spread[...], NT)
    half = boxes * rank
    rounded = (doubled[:, :half] + doubled[:, half:] + local[...]).astype(BF16)
    for b in range(boxes):
        far = dot(rounded[:, b * rank : (b + 1) * rank], basis[b])
        field[:, b * points : (b + 1) * points] = near[b] + far


SPACES = {"v": pltpu.VMEM, "s": pltpu.SMEM, "h": pl.ANY}


def call(kernel, name, kinds, args, outs, scratch=(), flops=0):
    moved = sum(x.size * x.dtype.itemsize for x in args)
    held = [x for x, kind in zip(args, kinds) if kind == "v"]
    held += [jax.ShapeDtypeStruct(shape, kind) for space, shape, kind in outs if space == "v"]
    limit = STACK + sum(x.size // x.shape[-1] * max(x.shape[-1], 128) * x.dtype.itemsize for x in held)
    args = [
        pltpu.with_memory_space_constraint(x, pltpu.HBM) if kind == "h" else x
        for kind, x in zip(kinds, args)
    ]
    return pl.pallas_call(
        kernel,
        name=name,
        out_shape=[jax.ShapeDtypeStruct(shape, kind) for _, shape, kind in outs],
        in_specs=[pl.BlockSpec(memory_space=SPACES[kind]) for kind in kinds],
        out_specs=[pl.BlockSpec(memory_space=SPACES[space]) for space, _, _ in outs],
        scratch_shapes=list(scratch),
        compiler_params=pltpu.CompilerParams(vmem_limit_bytes=limit),
        cost_estimate=pl.CostEstimate(flops=flops, bytes_accessed=moved, transcendentals=0),
    )(*args)


def body(
    vectors,
    leaf_basis,
    transfer,
    sibling_coupling,
    list_coupling,
    near_tiles,
    tile_target,
    tile_source,
    tile_count,
    couple_offset,
    couple_class,
):
    columns, width = vectors.shape
    boxes, rank, points = leaf_basis.shape
    count = lax.axis_size(AXES)
    bits = count.bit_length() - 1
    steps = boxes.bit_length() - 1
    double = 2 * rank
    dma = pltpu.SemaphoreType.DMA

    def send(x, target):
        return lax.ppermute(x, AXES, [(i, target(i)) for i in range(count)])

    def swap(x, mask):
        return send(x, lambda i: i ^ mask)

    before = send(vectors, lambda i: (i + 1) % count)
    ints = jnp.int32
    plain = (transfer, vectors, sibling_coupling)
    path_shapes = [(2 ** (height - 1), 2, rank, double) for height in range(1, steps + 1)]
    transfer, own, sibling, coeffs, leaf, *paths = call(
        leaf_kernel,
        "leaf",
        "hhhh",
        (*plain, leaf_basis),
        (
            *(("v", x.shape, x.dtype) for x in plain),
            ("v", (1, columns, double), BF16),
            ("v", (boxes, columns, rank), F32),
            *(("v", shape, F32) for shape in path_shapes),
        ),
        scratch=(pltpu.VMEM(leaf_basis.shape, BF16), dma((4,))),
    )
    device = lax.axis_index(AXES).astype(ints).reshape(1)
    window, passed = call(
        window_kernel,
        "window",
        "vvv",
        (coeffs, before, own),
        (("v", (2 * boxes, columns, points), BF16), ("v", coeffs.shape, BF16)),
    )
    lists = (tile_target, tile_source, couple_offset, couple_class)
    links = couple_offset.shape[1]
    gathered = coeffs
    after = send(own, lambda i: (i - 1) % count)
    for index, (low, wide) in enumerate(rounds_of(bits - 1)):
        kept = passed if index == 0 else gathered
        if index == 1:
            maps, rest, places, codes, kept, targets, sources = call(
                functools.partial(map_kernel, bits),
                "maps",
                "shhhhhvvv" + "v" * steps,
                (device, *lists, list_coupling, gathered, transfer, sibling, *paths),
                (
                    ("v", (count // 2 * double, double), BF16),
                    ("v", ((1 + links) * double, double), BF16),
                    ("v", (links, 8, 128), ints),
                    ("v", (links, columns, double), ints),
                    ("v", gathered.shape, BF16),
                    ("v", tile_target.shape, ints),
                    ("v", tile_source.shape, ints),
                ),
                scratch=(
                    pltpu.VMEM(couple_offset.shape, ints),
                    pltpu.VMEM(couple_class.shape, ints),
                    pltpu.VMEM(list_coupling.shape, F32),
                    dma((5,)),
                ),
            )
            spread, local, kept = call(
                down_kernel,
                "down",
                "svvvvv",
                (device, leaf, paths[-1], transfer, sibling, kept),
                (
                    ("v", (2 * boxes * rank, 2 * double), BF16),
                    ("v", (columns, boxes * rank), F32),
                    ("v", gathered.shape, BF16),
                ),
            )
        parts = {0: kept}
        for step in range(2**wide - 1, 0, -1):
            parts[step] = swap(gathered, 2 * step << low)
        gathered = jnp.concatenate([parts[-step % 2**wide] for step in range(2**wide)], axis=0)
    blocks, total = call(
        functools.partial(half_kernel, bits),
        "half",
        "svv",
        (device, gathered, maps),
        (("v", (3, columns, double), BF16), ("v", (columns, double), F32)),
    )
    other = swap(blocks, 1)
    near, picked = call(
        near_kernel,
        "near",
        "sssvvvvvv",
        (tile_count, targets, sources, window, after, near_tiles, blocks, gathered, places),
        (("v", (boxes, columns, points), F32), ("v", (links, columns, double), BF16)),
        scratch=(pltpu.VMEM((boxes, columns, points), BF16),),
    )
    (field,) = call(
        field_kernel,
        "field",
        "v" * 9,
        (other, picked, codes, rest, total, spread, local, leaf_basis, near),
        (("v", (columns, width), F32),),
    )
    return field


def solution(mesh):
    in_specs = (
        P(None, AXES),
        P(AXES, None, None),
        P(),
        P(),
        P(),
        P(AXES, None, None),
        P(AXES),
        P(AXES),
        P(AXES),
        P(AXES, None),
        P(AXES, None),
    )
    return jax.shard_map(body, mesh=mesh, in_specs=in_specs, out_specs=P(None, AXES), check_vma=False)
```

time: 24.6 us -> 22.3 us (0.907)
  waiting for transfers between devices: 1.21 us -> 0.02 us
  Pallas kernels: 8.3 us -> 7.6 us
  starting transfers between devices: 14 us -> 13.6 us
    ppermute x9, waiting for transfers between devices: 1.21 us -> 0.02 us  [send(): return lax.ppermute(x, AXES, [(i, target(i)) for i in range(count)])]
    pallas_call x5 -> x7, Pallas kernels: 8.3 us -> 7.6 us  [call(): pl.pallas_call(kernel, name=name, out_shape=[jax.ShapeDtypeStruct(shape,...]
    ppermute x9, starting transfers between devices: 14 us -> 13.6 us  [send(): return lax.ppermute(x, AXES, [(i, target(i)) for i in range(count)])]
  transfers between devices with their start and end apart: 9 -> 9, of which waited for: 1 -> 0; matrix products, arithmetic and copies ran while one was open for 0% -> 0% of each run, Pallas kernels for 27% -> 28%
where the time goes in v4:
time: 22.3 us; the launch traced here: 22.1 us
  starting transfers between devices  13.6 us (61%)
  Pallas kernels  7.6 us (34%)
  between operations  0.83 us (4%)
    ppermute x9, starting transfers between devices, send(): return lax.ppermute(x, AXES, [(i, target(i)) for i in range(count)])  13.6 us
    pallas_call x7, Pallas kernels, call(): pl.pallas_call(kernel, name=name, out_shape=[jax.ShapeDtypeStruct(shape,...  7.6 us
  transfers between devices with their start and end apart: 9, of which 0 were waited for; matrix products, arithmetic and copies ran while one was open for 0% of the time, Pallas kernels for 28%

profile of v4, /device:TPU:0, one launch (start us, length us, event | category | flops | bytes accessed | tf_op | source)
XLA Modules:
  0.0 22.1 jit_solution(8476016162838737446)
XLA Ops:
  0.0 0.0 copy-start
  0.0 0.5 %collective-permute-start = (bf16[32,2048]{1,0:T(8,128)(2,1)}, bf16[32,2048]{1,0:T(8,128)(2,1)S(1)}, u32[]{:S(2)}, u32[]{:S(2)}) collective-permute-start(bf16[32,2048]{1,0:T(8,128)(2,1)} %vectors_hbm.1), channel_id=1, source_target_pairs={{0,1},{1,2},{2,3},{3,4},{4,5},{5,6},{6,7},{7,8},{8,9},{9,10},{10,1... | collective-permute-start | bytes 393224 | tf_op jit(solution)/shard_map/ppermute | solution.py:341
  0.5 2.0 %leaf.1 = (f32[2,64,64]{2,1,0:T(8,128)S(1)}, bf16[32,2048]{1,0:T(8,128)(2,1)S(1)}, f32[2,64,64]{2,1,0:T(8,128)S(1)}, bf16[1,32,128]{2,1,0:T(8,128)(2,1)S(1)}, f3...) custom-call(f32[2,64,64]{2,1,0:T(8,128)} %transfer_hbm.1, ...), custom_call_target="tpu_custom_call" | custom-call | bytes 458752 | tf_op jit(solution)/shard_map/leaf/pallas_call | solution.py:307
  2.5 4.6 %collective-permute-start.1 = (bf16[1,32,128]{2,1,0:T(8,128)(2,1)S(1)}, bf16[1,32,128]{2,1,0:T(8,128)(2,1)S(1)}, u32[]{:S(2)}, u32[]{:S(2)}) collective-permute-start(bf16[1,32,128]{2,1,0:T(8,128)(2,1)S(1)} %get-tuple-element.33.coeffs), channel_id=1, source_target_pairs={{0,24},{1,25},{2,26},{3,27},{4,28},{5,29},{6,30},{7,31},{8,16},{9,... | collective-permute-start | bytes 24584 | tf_op jit(solution)/shard_map/ppermute | solution.py:341
  7.1 0.0 collective-permute-start.2
  7.1 0.6 %collective-permute-start.3 = (bf16[1,32,128]{2,1,0:T(8,128)(2,1)S(1)}, bf16[1,32,128]{2,1,0:T(8,128)(2,1)S(1)}, u32[]{:S(2)}, u32[]{:S(2)}) collective-permute-start(bf16[1,32,128]{2,1,0:T(8,128)(2,1)S(1)} %get-tuple-element.33.coeffs), channel_id=1, source_target_pairs={{0,8},{1,9},{2,10},{3,11},{4,12},{5,13},{6,14},{7,15},{8,0},{9,1},... | collective-permute-start | bytes 24584 | tf_op jit(solution)/shard_map/ppermute | solution.py:341
  7.7 4.2 %collective-permute-start.8 = (bf16[32,2048]{1,0:T(8,128)(2,1)S(1)}, bf16[32,2048]{1,0:T(8,128)(2,1)S(1)}, u32[]{:S(2)}, u32[]{:S(2)}) collective-permute-start(bf16[32,2048]{1,0:T(8,128)(2,1)S(1)} %get-tuple-element.34.own), channel_id=1, source_target_pairs={{0,31},{1,0},{2,1},{3,2},{4,3},{5,4},{6,5},{7,6},{8,7},{9,8},{10,9... | collective-permute-start | bytes 393224 | tf_op jit(solution)/shard_map/ppermute | solution.py:341
  12.0 0.0 collective-permute-done.before
  12.0 0.0 collective-permute-done.1
  12.0 0.0 collective-permute-done.2
  12.1 0.0 collective-permute-done.3
  12.1 2.1 %collective-permute-start.4 = (bf16[4,32,128]{2,1,0:T(8,128)(2,1)S(1)}, bf16[4,32,128]{2,1,0:T(8,128)(2,1)S(1)}, u32[]{:S(2)}, u32[]{:S(2)}) collective-permute-start(bf16[4,32,128]{2,1,0:T(8,128)(2,1)S(1)} %constant_dynamic-update-slice_fusion.refs_5_), channel_id=1, source_target_pairs={{0,6},{1,7},{2,4},{3,5},{4,2},{5,3},{6,0},{7,1},{8,14},{9,15},{10,... | collective-permute-start | bytes 98312 | tf_op jit(solution)/shard_map/ppermute | solution.py:341
  14.2 0.5 %collective-permute-start.5 = (bf16[4,32,128]{2,1,0:T(8,128)(2,1)S(1)}, bf16[4,32,128]{2,1,0:T(8,128)(2,1)S(1)}, u32[]{:S(2)}, u32[]{:S(2)}) collective-permute-start(bf16[4,32,128]{2,1,0:T(8,128)(2,1)S(1)} %constant_dynamic-update-slice_fusion.refs_5_), channel_id=1, source_target_pairs={{0,4},{1,5},{2,6},{3,7},{4,0},{5,1},{6,2},{7,3},{8,12},{9,13},{10,... | collective-permute-start | bytes 98312 | tf_op jit(solution)/shard_map/ppermute | solution.py:341
  14.7 0.9 %collective-permute-start.6 = (bf16[4,32,128]{2,1,0:T(8,128)(2,1)S(1)}, bf16[4,32,128]{2,1,0:T(8,128)(2,1)S(1)}, u32[]{:S(2)}, u32[]{:S(2)}) collective-permute-start(bf16[4,32,128]{2,1,0:T(8,128)(2,1)S(1)} %constant_dynamic-update-slice_fusion.refs_5_), channel_id=1, source_target_pairs={{0,2},{1,3},{2,0},{3,1},{4,6},{5,7},{6,4},{7,5},{8,10},{9,11},{10,... | collective-permute-start | bytes 98312 | tf_op jit(solution)/shard_map/ppermute | solution.py:341
  15.6 2.0 %maps.1 = (bf16[2048,128]{1,0:T(8,128)(2,1)S(1)}, bf16[512,128]{1,0:T(8,128)(2,1)S(1)}, s32[3,8,128]{2,1,0:T(8,128)S(1)}, s32[3,32,128]{2,1,0:T(8,128)S(1)}, bf1...) custom-call(s32[1]{0:T(128)} %bitcast.device, s32[16]{0:T(128)} %refs_0_.1, s32[16]{0:T(128)} %refs_1_.1, ...), custom_call_target="tpu_custom_call" | custom-call | bytes 688284 | tf_op jit(solution)/shard_map/maps/pallas_call | solution.py:307
  17.7 0.0 copy-start.1
  17.7 0.9 %down.1 = (bf16[1024,256]{1,0:T(8,128)(2,1)S(1)}, f32[32,512]{1,0:T(8,128)S(1)}, bf16[4,32,128]{2,1,0:T(8,128)(2,1)S(1)}) custom-call(s32[1]{0:T(128)} %bitcast.device, f32[8,32,64]{2,1,0:T(8,128)S(1)} %get-tuple-element.29.leaf, f32[4,2,64,128]{3,2,1,0:T(8,128)S(1)} %get-tuple-element.30.refs_10_.paths, ...), custom_call_target="tpu_custom_call" | custom-call | bytes 425988 | tf_op jit(solution)/shard_map/down/pallas_call | solution.py:307
  18.6 0.0 collective-permute-done.4
  18.7 0.0 collective-permute-done.5
  18.7 0.0 collective-permute-done.6
  18.7 0.3 %half.1 = (bf16[3,32,128]{2,1,0:T(8,128)(2,1)S(1)}, f32[32,128]{1,0:T(8,128)S(1)}) custom-call(s32[1]{0:T(128)} %bitcast.device, bf16[16,32,128]{2,1,0:T(8,128)(2,1)S(1)} %constant_dynamic-update-slice_fusion.4.gathered, bf16[2048,128]{1,0:T(8,128)(2,1)S(1)} %get-tuple-element.40.maps), custom_call_target="tpu_custom_call" | custom-call | bytes 655364 | tf_op jit(solution)/shard_map/half/pallas_call | solution.py:307
  19.0 0.1 collective-permute-start.7
  19.7 0.0 collective-permute-done.8.after
  19.7 0.0 copy-done
  19.7 1.0 %near.1 = (f32[8,32,256]{2,1,0:T(8,128)S(1)}, bf16[3,32,128]{2,1,0:T(8,128)(2,1)S(1)}) custom-call(s32[1]{0:T(128)S(6)} %copy.18.live, s32[16]{0:T(128)S(1)} %get-tuple-element.42.targets, s32[16]{0:T(128)S(1)} %get-tuple-element.43.sources, bf16[16,32,256]{2,1,0:T(8,128)(2,1)S(1)} %get-tuple-element.44.window, ...), custom_call_target="tpu_custom_call" | custom-call | bytes 2658436 | tf_op jit(solution)/shard_map/near/pallas_call | solution.py:307
  20.8 0.0 collective-permute-done.7.other
  20.8 0.0 copy-done.1
  20.8 1.3 %field.1 = f32[32,2048]{1,0:T(8,128)} custom-call(bf16[3,32,128]{2,1,0:T(8,128)(2,1)S(1)} %collective-permute-done.7.other, bf16[3,32,128]{2,1,0:T(8,128)(2,1)S(1)} %get-tuple-element.46.links, s32[3,32,128]{2,1,0:T(8,128)S(1)} %get-tuple-element.47.codes, bf16[512,128]{1,0:T(8,128)(2,1)S(1)} %get-tuple-element.48.rest, ...), custom_call_target="tpu_custom_call" | custom-call | bytes 1359872 | tf_op jit(solution)/shard_map/field/pallas_call | solution.py:307
  (9 shorter events, 0.1 us)
Async XLA Ops:
  0.0 19.7 %copy-start = (bf16[16,256,256]{2,1,0:T(8,128)(2,1)S(1)}, bf16[16,256,256]{2,1,0:T(8,128)(2,1)}, u32[]{:S(2)}) copy-start(bf16[16,256,256]{2,1,0:T(8,128)(2,1)} %tiles.1) | copy-start | bytes 6291460
  0.0 12.0 %collective-permute-start = (bf16[32,2048]{1,0:T(8,128)(2,1)}, bf16[32,2048]{1,0:T(8,128)(2,1)S(1)}, u32[]{:S(2)}, u32[]{:S(2)}) collective-permute-start(bf16[32,2048]{1,0:T(8,128)(2,1)} %vectors_hbm.1), channel_id=1, source_target_pairs={{0,1},{1,2},{2,3},{3,4},{4,5},{5,6},{6,7},{7,8},{8,9},{9,10},{10,1... | collective-permute-start | bytes 393224 | tf_op jit(solution)/shard_map/ppermute | solution.py:341
  2.5 9.5 %collective-permute-start.1 = (bf16[1,32,128]{2,1,0:T(8,128)(2,1)S(1)}, bf16[1,32,128]{2,1,0:T(8,128)(2,1)S(1)}, u32[]{:S(2)}, u32[]{:S(2)}) collective-permute-start(bf16[1,32,128]{2,1,0:T(8,128)(2,1)S(1)} %get-tuple-element.33.coeffs), channel_id=1, source_target_pairs={{0,24},{1,25},{2,26},{3,27},{4,28},{5,29},{6,30},{7,31},{8,16},{9,... | collective-permute-start | bytes 24584 | tf_op jit(solution)/shard_map/ppermute | solution.py:341
  7.1 4.9 %collective-permute-start.2 = (bf16[1,32,128]{2,1,0:T(8,128)(2,1)S(1)}, bf16[1,32,128]{2,1,0:T(8,128)(2,1)S(1)}, u32[]{:S(2)}, u32[]{:S(2)}) collective-permute-start(bf16[1,32,128]{2,1,0:T(8,128)(2,1)S(1)} %get-tuple-element.33.coeffs), channel_id=1, source_target_pairs={{0,16},{1,17},{2,18},{3,19},{4,20},{5,21},{6,22},{7,23},{8,24},{9,... | collective-permute-start | bytes 24584 | tf_op jit(solution)/shard_map/ppermute | solution.py:341
  7.1 5.0 %collective-permute-start.3 = (bf16[1,32,128]{2,1,0:T(8,128)(2,1)S(1)}, bf16[1,32,128]{2,1,0:T(8,128)(2,1)S(1)}, u32[]{:S(2)}, u32[]{:S(2)}) collective-permute-start(bf16[1,32,128]{2,1,0:T(8,128)(2,1)S(1)} %get-tuple-element.33.coeffs), channel_id=1, source_target_pairs={{0,8},{1,9},{2,10},{3,11},{4,12},{5,13},{6,14},{7,15},{8,0},{9,1},... | collective-permute-start | bytes 24584 | tf_op jit(solution)/shard_map/ppermute | solution.py:341
  7.7 12.0 %collective-permute-start.8 = (bf16[32,2048]{1,0:T(8,128)(2,1)S(1)}, bf16[32,2048]{1,0:T(8,128)(2,1)S(1)}, u32[]{:S(2)}, u32[]{:S(2)}) collective-permute-start(bf16[32,2048]{1,0:T(8,128)(2,1)S(1)} %get-tuple-element.34.own), channel_id=1, source_target_pairs={{0,31},{1,0},{2,1},{3,2},{4,3},{5,4},{6,5},{7,6},{8,7},{9,8},{10,9... | collective-permute-start | bytes 393224 | tf_op jit(solution)/shard_map/ppermute | solution.py:341
  12.1 6.6 %collective-permute-start.4 = (bf16[4,32,128]{2,1,0:T(8,128)(2,1)S(1)}, bf16[4,32,128]{2,1,0:T(8,128)(2,1)S(1)}, u32[]{:S(2)}, u32[]{:S(2)}) collective-permute-start(bf16[4,32,128]{2,1,0:T(8,128)(2,1)S(1)} %constant_dynamic-update-slice_fusion.refs_5_), channel_id=1, source_target_pairs={{0,6},{1,7},{2,4},{3,5},{4,2},{5,3},{6,0},{7,1},{8,14},{9,15},{10,... | collective-permute-start | bytes 98312 | tf_op jit(solution)/shard_map/ppermute | solution.py:341
  14.2 4.5 %collective-permute-start.5 = (bf16[4,32,128]{2,1,0:T(8,128)(2,1)S(1)}, bf16[4,32,128]{2,1,0:T(8,128)(2,1)S(1)}, u32[]{:S(2)}, u32[]{:S(2)}) collective-permute-start(bf16[4,32,128]{2,1,0:T(8,128)(2,1)S(1)} %constant_dynamic-update-slice_fusion.refs_5_), channel_id=1, source_target_pairs={{0,4},{1,5},{2,6},{3,7},{4,0},{5,1},{6,2},{7,3},{8,12},{9,13},{10,... | collective-permute-start | bytes 98312 | tf_op jit(solution)/shard_map/ppermute | solution.py:341
  14.7 4.0 %collective-permute-start.6 = (bf16[4,32,128]{2,1,0:T(8,128)(2,1)S(1)}, bf16[4,32,128]{2,1,0:T(8,128)(2,1)S(1)}, u32[]{:S(2)}, u32[]{:S(2)}) collective-permute-start(bf16[4,32,128]{2,1,0:T(8,128)(2,1)S(1)} %constant_dynamic-update-slice_fusion.refs_5_), channel_id=1, source_target_pairs={{0,2},{1,3},{2,0},{3,1},{4,6},{5,7},{6,4},{7,5},{8,10},{9,11},{10,... | collective-permute-start | bytes 98312 | tf_op jit(solution)/shard_map/ppermute | solution.py:341
  17.7 3.1 %copy-start.1 = (bf16[8,64,256]{2,1,0:T(8,128)(2,1)S(1)}, bf16[8,64,256]{2,1,0:T(8,128)(2,1)}, u32[]{:S(2)}) copy-start(bf16[8,64,256]{2,1,0:T(8,128)(2,1)} %basis.1) | copy-start | bytes 786436
  19.0 1.8 %collective-permute-start.7 = (bf16[3,32,128]{2,1,0:T(8,128)(2,1)S(1)}, bf16[3,32,128]{2,1,0:T(8,128)(2,1)S(1)}, u32[]{:S(2)}, u32[]{:S(2)}) collective-permute-start(bf16[3,32,128]{2,1,0:T(8,128)(2,1)S(1)} %get-tuple-element.41.blocks), channel_id=1, source_target_pairs={{0,1},{1,0},{2,3},{3,2},{4,5},{5,4},{6,7},{7,6},{8,9},{9,8},{10,11... | collective-permute-start | bytes 73736 | tf_op jit(solution)/shard_map/ppermute | solution.py:341

commit v5 on v4

--- a/solution.py
+++ b/solution.py
@@ -41,10 +41,10 @@
     return rounds
 
 
-def place_of(mask, bits):
+def place_of(source, here, bits):
     place, shift = 0, 0
     for low, wide in rounds_of(bits):
-        place = place | ((-(mask >> low) & (2**wide - 1)) << shift)
+        place = place | ((((here >> low) - (source >> low)) & (2**wide - 1)) << shift)
         shift += wide
     return place
 
@@ -69,6 +69,17 @@
 
 def both_halves(x):
     return x + pltpu.roll(x, x.shape[1] // 2, 1)
+
+
+def packed(double):
+    high, low = split(double)
+    lane = lax.broadcasted_iota(jnp.int32, double.shape, 1)
+    return jnp.concatenate([jnp.where(lane < double.shape[1] // 2, high, low), high], axis=1)
+
+
+def packing(right):
+    high, low = split(right)
+    return jnp.concatenate([high, high, low, jnp.zeros_like(low)], axis=0)
 
 
 def start_copies(pairs, sems):
@@ -85,14 +96,15 @@
     pairs = ((transfer_hbm, transfer), (vectors_hbm, vectors), (basis_hbm, basis), (sibling_hbm, sibling))
     copies = start_copies(pairs, sems)
     copies[0].wait()
-    t0, t1 = transfer[0], transfer[1]
-    stack = jnp.concatenate([t0, t1], axis=0)
+    t0, t1 = twice(transfer[0]), twice(transfer[1])
+    double = jnp.concatenate([t0, t1], axis=0)
+    sides = packing(jnp.concatenate([t0, t1], axis=1))
     for height in range(1, steps + 1):
         if height > 1:
-            stack = jnp.concatenate([dot3(stack, t0), dot3(stack, t1)], axis=0)
-        double = twice(stack)
+            wide = dot(packed(double), sides)
+            double = jnp.concatenate([wide[:, : 2 * rank], wide[:, 2 * rank :]], axis=0)
         paths[height - 1][...] = double.reshape(paths[height - 1].shape)
-    weights, rest = split(double)
+    weights = jnp.concatenate(split(double), axis=1)
     copies[1].wait()
     copies[2].wait()
     high, low = [], []
@@ -104,7 +116,9 @@
         low.append(other)
     high = jnp.concatenate(high, axis=1)
     low = jnp.concatenate(low, axis=1)
-    send[0] = high_low(dot(high, weights) + (dot(low, weights) + dot(high, rest)))
+    sums = dot(high, weights)
+    sums = sums[:, : 2 * rank] + (sums[:, 2 * rank :] + dot(low, weights[:, : 2 * rank]))
+    send[0] = high_low(sums)
     copies[3].wait()
 
 
@@ -117,9 +131,40 @@
             window[i * boxes + b] = part[:, b * points : (b + 1) * points]
 
 
+def fill_down(me, leaf, paths, transfer, sibling, spread, local):
+    boxes, columns, rank = leaf.shape
+    half = boxes * rank
+    t0, t1 = transfer[0], transfer[1]
+    s0, s1 = sibling[0], sibling[1]
+    tall = paths[...].reshape(half, 2 * rank)
+    high, low = split(tall)
+    spread[:half, 2 * rank :] = high
+    spread[half:, 2 * rank :] = low
+    high, low = split(dot(packed(tall), packing(twice(transfer[me & 1]))))
+    spread[:half, : 2 * rank] = high
+    spread[half:, : 2 * rank] = low
+    levels = [[leaf[b] for b in range(boxes)]]
+    while len(levels[-1]) > 2:
+        levels.append(up(levels[-1], (t0, t1)))
+    down = None
+    for level in reversed(levels):
+        across0 = dot3(jnp.concatenate(level[1::2], axis=0), s0)
+        across1 = dot3(jnp.concatenate(level[0::2], axis=0), s1)
+        if down is not None:
+            parents = jnp.concatenate(down, axis=0)
+            across0 = across0 + dot3(parents, t0, NT)
+            across1 = across1 + dot3(parents, t1, NT)
+        down = []
+        for i in range(len(level) // 2):
+            down.append(across0[i * columns : (i + 1) * columns])
+            down.append(across1[i * columns : (i + 1) * columns])
+    for b in range(boxes):
+        local[:, b * rank : (b + 1) * rank] = down[b]
+
+
 def map_kernel(bits, device, *refs):
-    hbm, (gathered, transfer, sibling), paths = refs[:5], refs[5:8], refs[8:-11]
-    maps, rest, places, codes, passed, *here, sems = refs[-11:]
+    hbm, (gathered, transfer, sibling, leaf), paths = refs[:5], refs[5:9], refs[9:-13]
+    maps, rest, places, codes, passed, spread, local, *here, sems = refs[-13:]
     copies = start_copies(zip(hbm, here), sems)
     _, _, offsets, classes, coupling = here
     rank = transfer.shape[1]
@@ -140,17 +185,15 @@
         table[pl.ds(at + rank, rank)] = both
 
     def place(height, low):
-        return place_of((1 << height) | (low ^ (pair & ((1 << height) - 1))), bits - 1)
+        return place_of((((pair >> height) ^ 1) << height) | low, pair, bits - 1)
 
     sides = []
     for height in range(1, steps + 1):
         tall = paths[height - 1][:, side].reshape(2 ** (height - 1) * rank, 2 * rank)
-        sides.append(jnp.concatenate([high_low(tall), tall.astype(BF16)], axis=1))
+        sides.append(packed(tall))
 
     def climb(height, fan):
-        fan_high, fan_low = split(fan)
-        weights = jnp.concatenate([fan_high, fan_high, fan_low, jnp.zeros_like(fan_low)], axis=0)
-        return dot(sides[height - 1], weights)
+        return dot(sides[height - 1], packing(fan))
 
     t0, t1 = transfer[0], transfer[1]
 
@@ -183,17 +226,17 @@
                 one = block[i * rank : (i + 1) * rank, k * 2 * rank : (k + 1) * 2 * rank]
                 put(maps, place(height - 1, (j << (steps - 1)) + i), one)
     put(rest, 0, twice(sibling[side]))
+    fill_down(me, leaf, paths[-1], transfer, sibling, spread, local)
     for copy in copies:
         copy.wait()
-    lane = lax.broadcasted_iota(jnp.int32, offsets.shape, 1)
     for i in range(offsets.shape[1]):
-        offset = jnp.sum(jnp.where(lane == i, offsets[...], 0))
-        kind = jnp.sum(jnp.where(lane == i, classes[...], 0))
-        mask = ((me + offset + count) & (count - 1)) ^ me
-        here_too = (mask & 1) == 0
-        link = jnp.where(here_too, place_of(mask >> 1, bits - 1), 0)
+        offset = offsets[0, i]
+        kind = classes[0, i]
+        source = (me + offset + count) & (count - 1)
+        here_too = ((source ^ me) & 1) == 0
+        link = jnp.where(here_too, place_of(source >> 1, pair, bits - 1), 0)
         places[i] = jnp.full(places.shape[1:], link, jnp.int32)
-        code = jnp.where(here_too, 0, jnp.where(mask == 1, 1, 2))
+        code = jnp.where(here_too, 0, jnp.where(source == me ^ 1, 1, 2))
         codes[i] = jnp.full(codes.shape[1:], code, jnp.int32)
         put(rest, 1 + i, twice(coupling[kind]))
 
@@ -234,45 +277,10 @@
         both = lax.fori_loop(1, pairs, lambda k, sums: sums + step(k), step(0))
     sums = both_halves(both)
     total[...] = sums
-    across = me + jnp.where((me & 1) == 1, -2, 2)
-    mask = (across & (2**bits - 1)) ^ me
+    across = (me + jnp.where((me & 1) == 1, -2, 2)) & (2**bits - 1)
     send[0] = gathered[0]
-    send[1] = gathered[place_of(mask >> 1, bits - 1)]
+    send[1] = gathered[place_of(across >> 1, me >> 1, bits - 1)]
     send[2] = high_low(sums)
-
-
-def down_kernel(device, leaf, paths, transfer, sibling, gathered, spread, local, passed):
-    boxes, columns, rank = leaf.shape
-    half = boxes * rank
-    passed[...] = gathered[...]
-    t0, t1 = transfer[0], transfer[1]
-    s0, s1 = sibling[0], sibling[1]
-    tall = paths[...].reshape(half, 2 * rank)
-    high, low = split(tall)
-    spread[:half, 2 * rank :] = high
-    spread[half:, 2 * rank :] = low
-    mine_high, mine_low = split(twice(transfer[device[0] & 1]))
-    weights = jnp.concatenate([mine_high, mine_high, mine_low, jnp.zeros_like(mine_low)], axis=0)
-    high, low = split(dot(jnp.concatenate([high_low(tall), high], axis=1), weights))
-    spread[:half, : 2 * rank] = high
-    spread[half:, : 2 * rank] = low
-    levels = [[leaf[b] for b in range(boxes)]]
-    while len(levels[-1]) > 2:
-        levels.append(up(levels[-1], (t0, t1)))
-    down = None
-    for level in reversed(levels):
-        across0 = dot3(jnp.concatenate(level[1::2], axis=0), s0)
-        across1 = dot3(jnp.concatenate(level[0::2], axis=0), s1)
-        if down is not None:
-            parents = jnp.concatenate(down, axis=0)
-            across0 = across0 + dot3(parents, t0, NT)
-            across1 = across1 + dot3(parents, t1, NT)
-        down = []
-        for i in range(len(level) // 2):
-            down.append(across0[i * columns : (i + 1) * columns])
-            down.append(across1[i * columns : (i + 1) * columns])
-    for b in range(boxes):
-        local[:, b * rank : (b + 1) * rank] = down[b]
 
 
 def field_kernel(other, links, codes, rest, total, spread, local, basis, near, field):
@@ -340,8 +348,9 @@
     def send(x, target):
         return lax.ppermute(x, AXES, [(i, target(i)) for i in range(count)])
 
-    def swap(x, mask):
-        return send(x, lambda i: i ^ mask)
+    def turned(i, low, wide, step):
+        digit = (i >> low) % 2**wide
+        return i + (((digit + step) % 2**wide - digit) << low)
 
     before = send(vectors, lambda i: (i + 1) % count)
     ints = jnp.int32
@@ -375,42 +384,33 @@
     for index, (low, wide) in enumerate(rounds_of(bits - 1)):
         kept = passed if index == 0 else gathered
         if index == 1:
-            maps, rest, places, codes, kept, targets, sources = call(
+            maps, rest, places, codes, kept, spread, local, targets, sources = call(
                 functools.partial(map_kernel, bits),
                 "maps",
-                "shhhhhvvv" + "v" * steps,
-                (device, *lists, list_coupling, gathered, transfer, sibling, *paths),
+                "shhhhhvvvv" + "v" * steps,
+                (device, *lists, list_coupling, gathered, transfer, sibling, leaf, *paths),
                 (
                     ("v", (count // 2 * double, double), BF16),
                     ("v", ((1 + links) * double, double), BF16),
                     ("v", (links, 8, 128), ints),
                     ("v", (links, columns, double), ints),
                     ("v", gathered.shape, BF16),
+                    ("v", (2 * boxes * rank, 2 * double), BF16),
+                    ("v", (columns, boxes * rank), F32),
                     ("v", tile_target.shape, ints),
                     ("v", tile_source.shape, ints),
                 ),
                 scratch=(
-                    pltpu.VMEM(couple_offset.shape, ints),
-                    pltpu.VMEM(couple_class.shape, ints),
+                    pltpu.SMEM(couple_offset.shape, ints),
+                    pltpu.SMEM(couple_class.shape, ints),
                     pltpu.VMEM(list_coupling.shape, F32),
                     dma((5,)),
                 ),
             )
-            spread, local, kept = call(
-                down_kernel,
-                "down",
-                "svvvvv",
-                (device, leaf, paths[-1], transfer, sibling, kept),
-                (
-                    ("v", (2 * boxes * rank, 2 * double), BF16),
-                    ("v", (columns, boxes * rank), F32),
-                    ("v", gathered.shape, BF16),
-                ),
-            )
-        parts = {0: kept}
-        for step in range(2**wide - 1, 0, -1):
-            parts[step] = swap(gathered, 2 * step << low)
-        gathered = jnp.concatenate([parts[-step % 2**wide] for step in range(2**wide)], axis=0)
+        parts = [kept]
+        for step in range(1, 2**wide):
+            parts.append(send(gathered, lambda i, args=(low + 1, wide, step): turned(i, *args)))
+        gathered = jnp.concatenate(parts, axis=0)
     blocks, total = call(
         functools.partial(half_kernel, bits),
         "half",
@@ -418,7 +418,7 @@
         (device, gathered, maps),
         (("v", (3, columns, double), BF16), ("v", (columns, double), F32)),
     )
-    other = swap(blocks, 1)
+    other = send(blocks, lambda i: i ^ 1)
     near, picked = call(
         near_kernel,
         "near",

time: 22.3 us -> 21.7 us (0.973)
  Pallas kernels: 7.6 us -> 6.67 us
    pallas_call x7 -> x6, Pallas kernels: 7.6 us -> 6.67 us  [call(): pl.pallas_call(kernel, name=name, out_shape=[jax.ShapeDtypeStruct(shape,...]
  transfers between devices with their start and end apart: 9 -> 9, of which waited for: 0 -> 1; matrix products, arithmetic and copies ran while one was open for 0% -> 0% of each run, Pallas kernels for 28% -> 25%
where the time goes in v5:
time: 21.7 us; the launch traced here: 21.5 us
  starting transfers between devices  13.7 us (63%)
  Pallas kernels  6.67 us (31%)
  between operations  0.8 us (4%)
  waiting for transfers between devices  0.24 us (1%)
    ppermute x9, starting transfers between devices, send(): return lax.ppermute(x, AXES, [(i, target(i)) for i in range(count)])  13.7 us
    pallas_call x6, Pallas kernels, call(): pl.pallas_call(kernel, name=name, out_shape=[jax.ShapeDtypeStruct(shape,...  6.67 us
  transfers between devices with their start and end apart: 9, of which 1 were waited for; matrix products, arithmetic and copies ran while one was open for 0% of the time, Pallas kernels for 25%

profile of v5, /device:TPU:0, one launch (start us, length us, event | category | flops | bytes accessed | tf_op | source)
XLA Modules:
  0.0 21.5 jit_solution(3812207067251421160)
XLA Ops:
  0.0 0.0 copy-start
  0.0 0.5 %collective-permute-start = (bf16[32,2048]{1,0:T(8,128)(2,1)}, bf16[32,2048]{1,0:T(8,128)(2,1)S(1)}, u32[]{:S(2)}, u32[]{:S(2)}) collective-permute-start(bf16[32,2048]{1,0:T(8,128)(2,1)} %vectors_hbm.1), channel_id=1, source_target_pairs={{0,1},{1,2},{2,3},{3,4},{4,5},{5,6},{6,7},{7,8},{8,9},{9,10},{10,1... | collective-permute-start | bytes 393224 | tf_op jit(solution)/shard_map/ppermute | solution.py:349
  0.5 1.9 %leaf.1 = (f32[2,64,64]{2,1,0:T(8,128)S(1)}, bf16[32,2048]{1,0:T(8,128)(2,1)S(1)}, f32[2,64,64]{2,1,0:T(8,128)S(1)}, bf16[1,32,128]{2,1,0:T(8,128)(2,1)S(1)}, f3...) custom-call(f32[2,64,64]{2,1,0:T(8,128)} %transfer_hbm.1, ...), custom_call_target="tpu_custom_call" | custom-call | bytes 458752 | tf_op jit(solution)/shard_map/leaf/pallas_call | solution.py:315
  2.3 2.6 %collective-permute-start.1 = (bf16[1,32,128]{2,1,0:T(8,128)(2,1)S(1)}, bf16[1,32,128]{2,1,0:T(8,128)(2,1)S(1)}, u32[]{:S(2)}, u32[]{:S(2)}) collective-permute-start(bf16[1,32,128]{2,1,0:T(8,128)(2,1)S(1)} %get-tuple-element.28.coeffs), channel_id=1, source_target_pairs={{0,8},{1,9},{2,10},{3,11},{4,12},{5,13},{6,14},{7,15},{8,16},{9,17... | collective-permute-start | bytes 24584 | tf_op jit(solution)/shard_map/ppermute | solution.py:349
  4.9 2.6 %collective-permute-start.2 = (bf16[1,32,128]{2,1,0:T(8,128)(2,1)S(1)}, bf16[1,32,128]{2,1,0:T(8,128)(2,1)S(1)}, u32[]{:S(2)}, u32[]{:S(2)}) collective-permute-start(bf16[1,32,128]{2,1,0:T(8,128)(2,1)S(1)} %get-tuple-element.28.coeffs), channel_id=1, source_target_pairs={{0,16},{1,17},{2,18},{3,19},{4,20},{5,21},{6,22},{7,23},{8,24},{9,... | collective-permute-start | bytes 24584 | tf_op jit(solution)/shard_map/ppermute | solution.py:349
  7.5 1.3 %collective-permute-start.3 = (bf16[1,32,128]{2,1,0:T(8,128)(2,1)S(1)}, bf16[1,32,128]{2,1,0:T(8,128)(2,1)S(1)}, u32[]{:S(2)}, u32[]{:S(2)}) collective-permute-start(bf16[1,32,128]{2,1,0:T(8,128)(2,1)S(1)} %get-tuple-element.28.coeffs), channel_id=1, source_target_pairs={{0,24},{1,25},{2,26},{3,27},{4,28},{5,29},{6,30},{7,31},{8,0},{9,1... | collective-permute-start | bytes 24584 | tf_op jit(solution)/shard_map/ppermute | solution.py:349
  8.9 2.6 %collective-permute-start.8 = (bf16[32,2048]{1,0:T(8,128)(2,1)S(1)}, bf16[32,2048]{1,0:T(8,128)(2,1)S(1)}, u32[]{:S(2)}, u32[]{:S(2)}) collective-permute-start(bf16[32,2048]{1,0:T(8,128)(2,1)S(1)} %get-tuple-element.29.own), channel_id=1, source_target_pairs={{0,31},{1,0},{2,1},{3,2},{4,3},{5,4},{6,5},{7,6},{8,7},{9,8},{10,9... | collective-permute-start | bytes 393224 | tf_op jit(solution)/shard_map/ppermute | solution.py:349
  11.4 0.0 collective-permute-done.before
  11.5 0.0 collective-permute-done.1
  11.5 0.0 collective-permute-done.2
  11.5 0.0 collective-permute-done.3
  11.5 1.2 %collective-permute-start.4 = (bf16[4,32,128]{2,1,0:T(8,128)(2,1)S(1)}, bf16[4,32,128]{2,1,0:T(8,128)(2,1)S(1)}, u32[]{:S(2)}, u32[]{:S(2)}) collective-permute-start(bf16[4,32,128]{2,1,0:T(8,128)(2,1)S(1)} %constant_dynamic-update-slice_fusion.refs_5_), channel_id=1, source_target_pairs={{0,2},{1,3},{2,4},{3,5},{4,6},{5,7},{6,0},{7,1},{8,10},{9,11},{10,... | collective-permute-start | bytes 98312 | tf_op jit(solution)/shard_map/ppermute | solution.py:349
  12.7 1.5 %collective-permute-start.5 = (bf16[4,32,128]{2,1,0:T(8,128)(2,1)S(1)}, bf16[4,32,128]{2,1,0:T(8,128)(2,1)S(1)}, u32[]{:S(2)}, u32[]{:S(2)}) collective-permute-start(bf16[4,32,128]{2,1,0:T(8,128)(2,1)S(1)} %constant_dynamic-update-slice_fusion.refs_5_), channel_id=1, source_target_pairs={{0,4},{1,5},{2,6},{3,7},{4,0},{5,1},{6,2},{7,3},{8,12},{9,13},{10,... | collective-permute-start | bytes 98312 | tf_op jit(solution)/shard_map/ppermute | solution.py:349
  14.2 1.4 %collective-permute-start.6 = (bf16[4,32,128]{2,1,0:T(8,128)(2,1)S(1)}, bf16[4,32,128]{2,1,0:T(8,128)(2,1)S(1)}, u32[]{:S(2)}, u32[]{:S(2)}) collective-permute-start(bf16[4,32,128]{2,1,0:T(8,128)(2,1)S(1)} %constant_dynamic-update-slice_fusion.refs_5_), channel_id=1, source_target_pairs={{0,6},{1,7},{2,0},{3,1},{4,2},{5,3},{6,4},{7,5},{8,14},{9,15},{10,... | collective-permute-start | bytes 98312 | tf_op jit(solution)/shard_map/ppermute | solution.py:349
  15.6 0.0 copy-start.1
  15.6 2.2 %maps.1 = (bf16[2048,128]{1,0:T(8,128)(2,1)S(1)}, bf16[512,128]{1,0:T(8,128)(2,1)S(1)}, s32[3,8,128]{2,1,0:T(8,128)S(1)}, s32[3,32,128]{2,1,0:T(8,128)S(1)}, bf1...) custom-call(s32[1]{0:T(128)} %bitcast.device, ...), custom_call_target="tpu_custom_call" | custom-call | bytes 753820 | tf_op jit(solution)/shard_map/maps/pallas_call | solution.py:315
  17.8 0.0 collective-permute-done.4
  17.9 0.0 collective-permute-done.5
  17.9 0.2 %collective-permute-done.6 = bf16[4,32,128]{2,1,0:T(8,128)(2,1)S(1)} collective-permute-done((bf16[4,32,128]{2,1,0:T(8,128)(2,1)S(1)}, bf16[4,32,128]{2,1,0:T(8,128)(2,1)S(1)}, u32[]{:S(2)}, u32[]{:S(2)}) %collective-permute-start.6) | collective-permute-done | bytes 32800 | tf_op jit(solution)/shard_map/ppermute | solution.py:349
  18.1 0.3 %half.1 = (bf16[3,32,128]{2,1,0:T(8,128)(2,1)S(1)}, f32[32,128]{1,0:T(8,128)S(1)}) custom-call(s32[1]{0:T(128)} %bitcast.device, bf16[16,32,128]{2,1,0:T(8,128)(2,1)S(1)} %constant_dynamic-update-slice_fusion.4.gathered, bf16[2048,128]{1,0:T(8,128)(2,1)S(1)} %get-tuple-element.38.maps), custom_call_target="tpu_custom_call" | custom-call | bytes 655364 | tf_op jit(solution)/shard_map/half/pallas_call | solution.py:315
  18.4 0.1 collective-permute-start.7
  19.1 0.0 collective-permute-done.8.after
  19.1 0.0 copy-done
  19.1 1.0 %near.1 = (f32[8,32,256]{2,1,0:T(8,128)S(1)}, bf16[3,32,128]{2,1,0:T(8,128)(2,1)S(1)}) custom-call(s32[1]{0:T(128)S(6)} %copy.18.live, s32[16]{0:T(128)S(1)} %get-tuple-element.40.targets, s32[16]{0:T(128)S(1)} %get-tuple-element.41.sources, bf16[16,32,256]{2,1,0:T(8,128)(2,1)S(1)} %get-tuple-element.42.window, ...), custom_call_target="tpu_custom_call" | custom-call | bytes 2658436 | tf_op jit(solution)/shard_map/near/pallas_call | solution.py:315
  20.2 0.0 collective-permute-done.7.other
  20.2 0.0 copy-done.1
  20.2 1.3 %field.1 = f32[32,2048]{1,0:T(8,128)} custom-call(bf16[3,32,128]{2,1,0:T(8,128)(2,1)S(1)} %collective-permute-done.7.other, bf16[3,32,128]{2,1,0:T(8,128)(2,1)S(1)} %get-tuple-element.44.links, s32[3,32,128]{2,1,0:T(8,128)S(1)} %get-tuple-element.45.codes, bf16[512,128]{1,0:T(8,128)(2,1)S(1)} %get-tuple-element.46.rest, ...), custom_call_target="tpu_custom_call" | custom-call | bytes 1359872 | tf_op jit(solution)/shard_map/field/pallas_call | solution.py:315
  (9 shorter events, 0.1 us)
Async XLA Ops:
  0.0 19.1 %copy-start = (bf16[16,256,256]{2,1,0:T(8,128)(2,1)S(1)}, bf16[16,256,256]{2,1,0:T(8,128)(2,1)}, u32[]{:S(2)}) copy-start(bf16[16,256,256]{2,1,0:T(8,128)(2,1)} %tiles.1) | copy-start | bytes 6291460
  0.0 11.4 %collective-permute-start = (bf16[32,2048]{1,0:T(8,128)(2,1)}, bf16[32,2048]{1,0:T(8,128)(2,1)S(1)}, u32[]{:S(2)}, u32[]{:S(2)}) collective-permute-start(bf16[32,2048]{1,0:T(8,128)(2,1)} %vectors_hbm.1), channel_id=1, source_target_pairs={{0,1},{1,2},{2,3},{3,4},{4,5},{5,6},{6,7},{7,8},{8,9},{9,10},{10,1... | collective-permute-start | bytes 393224 | tf_op jit(solution)/shard_map/ppermute | solution.py:349
  2.3 9.1 %collective-permute-start.1 = (bf16[1,32,128]{2,1,0:T(8,128)(2,1)S(1)}, bf16[1,32,128]{2,1,0:T(8,128)(2,1)S(1)}, u32[]{:S(2)}, u32[]{:S(2)}) collective-permute-start(bf16[1,32,128]{2,1,0:T(8,128)(2,1)S(1)} %get-tuple-element.28.coeffs), channel_id=1, source_target_pairs={{0,8},{1,9},{2,10},{3,11},{4,12},{5,13},{6,14},{7,15},{8,16},{9,17... | collective-permute-start | bytes 24584 | tf_op jit(solution)/shard_map/ppermute | solution.py:349
  4.9 6.6 %collective-permute-start.2 = (bf16[1,32,128]{2,1,0:T(8,128)(2,1)S(1)}, bf16[1,32,128]{2,1,0:T(8,128)(2,1)S(1)}, u32[]{:S(2)}, u32[]{:S(2)}) collective-permute-start(bf16[1,32,128]{2,1,0:T(8,128)(2,1)S(1)} %get-tuple-element.28.coeffs), channel_id=1, source_target_pairs={{0,16},{1,17},{2,18},{3,19},{4,20},{5,21},{6,22},{7,23},{8,24},{9,... | collective-permute-start | bytes 24584 | tf_op jit(solution)/shard_map/ppermute | solution.py:349
  7.5 4.0 %collective-permute-start.3 = (bf16[1,32,128]{2,1,0:T(8,128)(2,1)S(1)}, bf16[1,32,128]{2,1,0:T(8,128)(2,1)S(1)}, u32[]{:S(2)}, u32[]{:S(2)}) collective-permute-start(bf16[1,32,128]{2,1,0:T(8,128)(2,1)S(1)} %get-tuple-element.28.coeffs), channel_id=1, source_target_pairs={{0,24},{1,25},{2,26},{3,27},{4,28},{5,29},{6,30},{7,31},{8,0},{9,1... | collective-permute-start | bytes 24584 | tf_op jit(solution)/shard_map/ppermute | solution.py:349
  8.9 10.3 %collective-permute-start.8 = (bf16[32,2048]{1,0:T(8,128)(2,1)S(1)}, bf16[32,2048]{1,0:T(8,128)(2,1)S(1)}, u32[]{:S(2)}, u32[]{:S(2)}) collective-permute-start(bf16[32,2048]{1,0:T(8,128)(2,1)S(1)} %get-tuple-element.29.own), channel_id=1, source_target_pairs={{0,31},{1,0},{2,1},{3,2},{4,3},{5,4},{6,5},{7,6},{8,7},{9,8},{10,9... | collective-permute-start | bytes 393224 | tf_op jit(solution)/shard_map/ppermute | solution.py:349
  11.5 6.3 %collective-permute-start.4 = (bf16[4,32,128]{2,1,0:T(8,128)(2,1)S(1)}, bf16[4,32,128]{2,1,0:T(8,128)(2,1)S(1)}, u32[]{:S(2)}, u32[]{:S(2)}) collective-permute-start(bf16[4,32,128]{2,1,0:T(8,128)(2,1)S(1)} %constant_dynamic-update-slice_fusion.refs_5_), channel_id=1, source_target_pairs={{0,2},{1,3},{2,4},{3,5},{4,6},{5,7},{6,0},{7,1},{8,10},{9,11},{10,... | collective-permute-start | bytes 98312 | tf_op jit(solution)/shard_map/ppermute | solution.py:349
  12.7 5.2 %collective-permute-start.5 = (bf16[4,32,128]{2,1,0:T(8,128)(2,1)S(1)}, bf16[4,32,128]{2,1,0:T(8,128)(2,1)S(1)}, u32[]{:S(2)}, u32[]{:S(2)}) collective-permute-start(bf16[4,32,128]{2,1,0:T(8,128)(2,1)S(1)} %constant_dynamic-update-slice_fusion.refs_5_), channel_id=1, source_target_pairs={{0,4},{1,5},{2,6},{3,7},{4,0},{5,1},{6,2},{7,3},{8,12},{9,13},{10,... | collective-permute-start | bytes 98312 | tf_op jit(solution)/shard_map/ppermute | solution.py:349
  14.2 3.9 %collective-permute-start.6 = (bf16[4,32,128]{2,1,0:T(8,128)(2,1)S(1)}, bf16[4,32,128]{2,1,0:T(8,128)(2,1)S(1)}, u32[]{:S(2)}, u32[]{:S(2)}) collective-permute-start(bf16[4,32,128]{2,1,0:T(8,128)(2,1)S(1)} %constant_dynamic-update-slice_fusion.refs_5_), channel_id=1, source_target_pairs={{0,6},{1,7},{2,0},{3,1},{4,2},{5,3},{6,4},{7,5},{8,14},{9,15},{10,... | collective-permute-start | bytes 98312 | tf_op jit(solution)/shard_map/ppermute | solution.py:349
  15.6 4.5 %copy-start.1 = (bf16[8,64,256]{2,1,0:T(8,128)(2,1)S(1)}, bf16[8,64,256]{2,1,0:T(8,128)(2,1)}, u32[]{:S(2)}) copy-start(bf16[8,64,256]{2,1,0:T(8,128)(2,1)} %basis.1) | copy-start | bytes 786436
  18.4 1.8 %collective-permute-start.7 = (bf16[3,32,128]{2,1,0:T(8,128)(2,1)S(1)}, bf16[3,32,128]{2,1,0:T(8,128)(2,1)S(1)}, u32[]{:S(2)}, u32[]{:S(2)}) collective-permute-start(bf16[3,32,128]{2,1,0:T(8,128)(2,1)S(1)} %get-tuple-element.39.blocks), channel_id=1, source_target_pairs={{0,1},{1,0},{2,3},{3,2},{4,5},{5,4},{6,7},{7,6},{8,9},{9,8},{10,11... | collective-permute-start | bytes 73736 | tf_op jit(solution)/shard_map/ppermute | solution.py:349

commit v6 on v5

--- a/solution.py
+++ b/solution.py
@@ -100,20 +100,21 @@
     double = jnp.concatenate([t0, t1], axis=0)
     sides = packing(jnp.concatenate([t0, t1], axis=1))
     for height in range(1, steps + 1):
+        if height == steps:
+            copies[1].wait()
+            copies[2].wait()
+            high, low = [], []
+            for b in range(boxes):
+                coeffs = dot(vectors[:, b * points : (b + 1) * points], basis[b], NT)
+                leaf[b] = coeffs
+                one, other = split(coeffs)
+                high.append(one)
+                low.append(other)
         if height > 1:
             wide = dot(packed(double), sides)
             double = jnp.concatenate([wide[:, : 2 * rank], wide[:, 2 * rank :]], axis=0)
         paths[height - 1][...] = double.reshape(paths[height - 1].shape)
     weights = jnp.concatenate(split(double), axis=1)
-    copies[1].wait()
-    copies[2].wait()
-    high, low = [], []
-    for b in range(boxes):
-        coeffs = dot(vectors[:, b * points : (b + 1) * points], basis[b], NT)
-        leaf[b] = coeffs
-        one, other = split(coeffs)
-        high.append(one)
-        low.append(other)
     high = jnp.concatenate(high, axis=1)
     low = jnp.concatenate(low, axis=1)
     sums = dot(high, weights)

time: 21.7 us -> 21.7 us (level)
  no operation moved by 1% of the time
where the time goes in v6:
time: 21.7 us; the launch traced here: 21.5 us
  starting transfers between devices  13.7 us (63%)
  Pallas kernels  6.61 us (30%)
  between operations  0.8 us (4%)
  waiting for transfers between devices  0.24 us (1%)
    ppermute x9, starting transfers between devices, send(): return lax.ppermute(x, AXES, [(i, target(i)) for i in range(count)])  13.7 us
    pallas_call x6, Pallas kernels, call(): pl.pallas_call(kernel, name=name, out_shape=[jax.ShapeDtypeStruct(shape,...  6.61 us
  transfers between devices with their start and end apart: 9, of which 1 were waited for; matrix products, arithmetic and copies ran while one was open for 0% of the time, Pallas kernels for 25%

profile of v6, /device:TPU:0, one launch (start us, length us, event | category | flops | bytes accessed | tf_op | source)
XLA Modules:
  0.0 21.5 jit_solution(10614753824785297553)
XLA Ops:
  0.0 0.0 copy-start
  0.0 0.5 %collective-permute-start = (bf16[32,2048]{1,0:T(8,128)(2,1)}, bf16[32,2048]{1,0:T(8,128)(2,1)S(1)}, u32[]{:S(2)}, u32[]{:S(2)}) collective-permute-start(bf16[32,2048]{1,0:T(8,128)(2,1)} %vectors_hbm.1), channel_id=1, source_target_pairs={{0,1},{1,2},{2,3},{3,4},{4,5},{5,6},{6,7},{7,8},{8,9},{9,10},{10,1... | collective-permute-start | bytes 393224 | tf_op jit(solution)/shard_map/ppermute | solution.py:350
  0.5 1.8 %leaf.1 = (f32[2,64,64]{2,1,0:T(8,128)S(1)}, bf16[32,2048]{1,0:T(8,128)(2,1)S(1)}, f32[2,64,64]{2,1,0:T(8,128)S(1)}, bf16[1,32,128]{2,1,0:T(8,128)(2,1)S(1)}, f3...) custom-call(f32[2,64,64]{2,1,0:T(8,128)} %transfer_hbm.1, ...), custom_call_target="tpu_custom_call" | custom-call | bytes 458752 | tf_op jit(solution)/shard_map/leaf/pallas_call | solution.py:316
  2.3 2.6 %collective-permute-start.1 = (bf16[1,32,128]{2,1,0:T(8,128)(2,1)S(1)}, bf16[1,32,128]{2,1,0:T(8,128)(2,1)S(1)}, u32[]{:S(2)}, u32[]{:S(2)}) collective-permute-start(bf16[1,32,128]{2,1,0:T(8,128)(2,1)S(1)} %get-tuple-element.28.coeffs), channel_id=1, source_target_pairs={{0,8},{1,9},{2,10},{3,11},{4,12},{5,13},{6,14},{7,15},{8,16},{9,17... | collective-permute-start | bytes 24584 | tf_op jit(solution)/shard_map/ppermute | solution.py:350
  4.9 2.6 %collective-permute-start.2 = (bf16[1,32,128]{2,1,0:T(8,128)(2,1)S(1)}, bf16[1,32,128]{2,1,0:T(8,128)(2,1)S(1)}, u32[]{:S(2)}, u32[]{:S(2)}) collective-permute-start(bf16[1,32,128]{2,1,0:T(8,128)(2,1)S(1)} %get-tuple-element.28.coeffs), channel_id=1, source_target_pairs={{0,16},{1,17},{2,18},{3,19},{4,20},{5,21},{6,22},{7,23},{8,24},{9,... | collective-permute-start | bytes 24584 | tf_op jit(solution)/shard_map/ppermute | solution.py:350
  7.5 1.3 %collective-permute-start.3 = (bf16[1,32,128]{2,1,0:T(8,128)(2,1)S(1)}, bf16[1,32,128]{2,1,0:T(8,128)(2,1)S(1)}, u32[]{:S(2)}, u32[]{:S(2)}) collective-permute-start(bf16[1,32,128]{2,1,0:T(8,128)(2,1)S(1)} %get-tuple-element.28.coeffs), channel_id=1, source_target_pairs={{0,24},{1,25},{2,26},{3,27},{4,28},{5,29},{6,30},{7,31},{8,0},{9,1... | collective-permute-start | bytes 24584 | tf_op jit(solution)/shard_map/ppermute | solution.py:350
  8.8 2.6 %collective-permute-start.8 = (bf16[32,2048]{1,0:T(8,128)(2,1)S(1)}, bf16[32,2048]{1,0:T(8,128)(2,1)S(1)}, u32[]{:S(2)}, u32[]{:S(2)}) collective-permute-start(bf16[32,2048]{1,0:T(8,128)(2,1)S(1)} %get-tuple-element.29.own), channel_id=1, source_target_pairs={{0,31},{1,0},{2,1},{3,2},{4,3},{5,4},{6,5},{7,6},{8,7},{9,8},{10,9... | collective-permute-start | bytes 393224 | tf_op jit(solution)/shard_map/ppermute | solution.py:350
  11.4 0.0 collective-permute-done.before
  11.4 0.0 collective-permute-done.1
  11.4 0.0 collective-permute-done.2
  11.4 0.0 collective-permute-done.3
  11.5 1.2 %collective-permute-start.4 = (bf16[4,32,128]{2,1,0:T(8,128)(2,1)S(1)}, bf16[4,32,128]{2,1,0:T(8,128)(2,1)S(1)}, u32[]{:S(2)}, u32[]{:S(2)}) collective-permute-start(bf16[4,32,128]{2,1,0:T(8,128)(2,1)S(1)} %constant_dynamic-update-slice_fusion.refs_5_), channel_id=1, source_target_pairs={{0,2},{1,3},{2,4},{3,5},{4,6},{5,7},{6,0},{7,1},{8,10},{9,11},{10,... | collective-permute-start | bytes 98312 | tf_op jit(solution)/shard_map/ppermute | solution.py:350
  12.6 1.5 %collective-permute-start.5 = (bf16[4,32,128]{2,1,0:T(8,128)(2,1)S(1)}, bf16[4,32,128]{2,1,0:T(8,128)(2,1)S(1)}, u32[]{:S(2)}, u32[]{:S(2)}) collective-permute-start(bf16[4,32,128]{2,1,0:T(8,128)(2,1)S(1)} %constant_dynamic-update-slice_fusion.refs_5_), channel_id=1, source_target_pairs={{0,4},{1,5},{2,6},{3,7},{4,0},{5,1},{6,2},{7,3},{8,12},{9,13},{10,... | collective-permute-start | bytes 98312 | tf_op jit(solution)/shard_map/ppermute | solution.py:350
  14.1 1.4 %collective-permute-start.6 = (bf16[4,32,128]{2,1,0:T(8,128)(2,1)S(1)}, bf16[4,32,128]{2,1,0:T(8,128)(2,1)S(1)}, u32[]{:S(2)}, u32[]{:S(2)}) collective-permute-start(bf16[4,32,128]{2,1,0:T(8,128)(2,1)S(1)} %constant_dynamic-update-slice_fusion.refs_5_), channel_id=1, source_target_pairs={{0,6},{1,7},{2,0},{3,1},{4,2},{5,3},{6,4},{7,5},{8,14},{9,15},{10,... | collective-permute-start | bytes 98312 | tf_op jit(solution)/shard_map/ppermute | solution.py:350
  15.6 0.0 copy-start.1
  15.6 2.2 %maps.1 = (bf16[2048,128]{1,0:T(8,128)(2,1)S(1)}, bf16[512,128]{1,0:T(8,128)(2,1)S(1)}, s32[3,8,128]{2,1,0:T(8,128)S(1)}, s32[3,32,128]{2,1,0:T(8,128)S(1)}, bf1...) custom-call(s32[1]{0:T(128)} %bitcast.device, ...), custom_call_target="tpu_custom_call" | custom-call | bytes 753820 | tf_op jit(solution)/shard_map/maps/pallas_call | solution.py:316
  17.8 0.0 collective-permute-done.4
  17.8 0.0 collective-permute-done.5
  17.8 0.2 %collective-permute-done.6 = bf16[4,32,128]{2,1,0:T(8,128)(2,1)S(1)} collective-permute-done((bf16[4,32,128]{2,1,0:T(8,128)(2,1)S(1)}, bf16[4,32,128]{2,1,0:T(8,128)(2,1)S(1)}, u32[]{:S(2)}, u32[]{:S(2)}) %collective-permute-start.6) | collective-permute-done | bytes 32800 | tf_op jit(solution)/shard_map/ppermute | solution.py:350
  18.1 0.3 %half.1 = (bf16[3,32,128]{2,1,0:T(8,128)(2,1)S(1)}, f32[32,128]{1,0:T(8,128)S(1)}) custom-call(s32[1]{0:T(128)} %bitcast.device, bf16[16,32,128]{2,1,0:T(8,128)(2,1)S(1)} %constant_dynamic-update-slice_fusion.4.gathered, bf16[2048,128]{1,0:T(8,128)(2,1)S(1)} %get-tuple-element.38.maps), custom_call_target="tpu_custom_call" | custom-call | bytes 655364 | tf_op jit(solution)/shard_map/half/pallas_call | solution.py:316
  18.3 0.1 collective-permute-start.7
  19.1 0.0 collective-permute-done.8.after
  19.1 0.0 copy-done
  19.1 1.0 %near.1 = (f32[8,32,256]{2,1,0:T(8,128)S(1)}, bf16[3,32,128]{2,1,0:T(8,128)(2,1)S(1)}) custom-call(s32[1]{0:T(128)S(6)} %copy.18.live, s32[16]{0:T(128)S(1)} %get-tuple-element.40.targets, s32[16]{0:T(128)S(1)} %get-tuple-element.41.sources, bf16[16,32,256]{2,1,0:T(8,128)(2,1)S(1)} %get-tuple-element.42.window, ...), custom_call_target="tpu_custom_call" | custom-call | bytes 2658436 | tf_op jit(solution)/shard_map/near/pallas_call | solution.py:316
  20.1 0.0 collective-permute-done.7.other
  20.1 0.0 copy-done.1
  20.1 1.3 %field.1 = f32[32,2048]{1,0:T(8,128)} custom-call(bf16[3,32,128]{2,1,0:T(8,128)(2,1)S(1)} %collective-permute-done.7.other, bf16[3,32,128]{2,1,0:T(8,128)(2,1)S(1)} %get-tuple-element.44.links, s32[3,32,128]{2,1,0:T(8,128)S(1)} %get-tuple-element.45.codes, bf16[512,128]{1,0:T(8,128)(2,1)S(1)} %get-tuple-element.46.rest, ...), custom_call_target="tpu_custom_call" | custom-call | bytes 1359872 | tf_op jit(solution)/shard_map/field/pallas_call | solution.py:316
  (9 shorter events, 0.1 us)
Async XLA Ops:
  0.0 19.1 %copy-start = (bf16[16,256,256]{2,1,0:T(8,128)(2,1)S(1)}, bf16[16,256,256]{2,1,0:T(8,128)(2,1)}, u32[]{:S(2)}) copy-start(bf16[16,256,256]{2,1,0:T(8,128)(2,1)} %tiles.1) | copy-start | bytes 6291460
  0.0 11.4 %collective-permute-start = (bf16[32,2048]{1,0:T(8,128)(2,1)}, bf16[32,2048]{1,0:T(8,128)(2,1)S(1)}, u32[]{:S(2)}, u32[]{:S(2)}) collective-permute-start(bf16[32,2048]{1,0:T(8,128)(2,1)} %vectors_hbm.1), channel_id=1, source_target_pairs={{0,1},{1,2},{2,3},{3,4},{4,5},{5,6},{6,7},{7,8},{8,9},{9,10},{10,1... | collective-permute-start | bytes 393224 | tf_op jit(solution)/shard_map/ppermute | solution.py:350
  2.3 9.1 %collective-permute-start.1 = (bf16[1,32,128]{2,1,0:T(8,128)(2,1)S(1)}, bf16[1,32,128]{2,1,0:T(8,128)(2,1)S(1)}, u32[]{:S(2)}, u32[]{:S(2)}) collective-permute-start(bf16[1,32,128]{2,1,0:T(8,128)(2,1)S(1)} %get-tuple-element.28.coeffs), channel_id=1, source_target_pairs={{0,8},{1,9},{2,10},{3,11},{4,12},{5,13},{6,14},{7,15},{8,16},{9,17... | collective-permute-start | bytes 24584 | tf_op jit(solution)/shard_map/ppermute | solution.py:350
  4.9 6.6 %collective-permute-start.2 = (bf16[1,32,128]{2,1,0:T(8,128)(2,1)S(1)}, bf16[1,32,128]{2,1,0:T(8,128)(2,1)S(1)}, u32[]{:S(2)}, u32[]{:S(2)}) collective-permute-start(bf16[1,32,128]{2,1,0:T(8,128)(2,1)S(1)} %get-tuple-element.28.coeffs), channel_id=1, source_target_pairs={{0,16},{1,17},{2,18},{3,19},{4,20},{5,21},{6,22},{7,23},{8,24},{9,... | collective-permute-start | bytes 24584 | tf_op jit(solution)/shard_map/ppermute | solution.py:350
  7.5 4.0 %collective-permute-start.3 = (bf16[1,32,128]{2,1,0:T(8,128)(2,1)S(1)}, bf16[1,32,128]{2,1,0:T(8,128)(2,1)S(1)}, u32[]{:S(2)}, u32[]{:S(2)}) collective-permute-start(bf16[1,32,128]{2,1,0:T(8,128)(2,1)S(1)} %get-tuple-element.28.coeffs), channel_id=1, source_target_pairs={{0,24},{1,25},{2,26},{3,27},{4,28},{5,29},{6,30},{7,31},{8,0},{9,1... | collective-permute-start | bytes 24584 | tf_op jit(solution)/shard_map/ppermute | solution.py:350
  8.8 10.3 %collective-permute-start.8 = (bf16[32,2048]{1,0:T(8,128)(2,1)S(1)}, bf16[32,2048]{1,0:T(8,128)(2,1)S(1)}, u32[]{:S(2)}, u32[]{:S(2)}) collective-permute-start(bf16[32,2048]{1,0:T(8,128)(2,1)S(1)} %get-tuple-element.29.own), channel_id=1, source_target_pairs={{0,31},{1,0},{2,1},{3,2},{4,3},{5,4},{6,5},{7,6},{8,7},{9,8},{10,9... | collective-permute-start | bytes 393224 | tf_op jit(solution)/shard_map/ppermute | solution.py:350
  11.5 6.3 %collective-permute-start.4 = (bf16[4,32,128]{2,1,0:T(8,128)(2,1)S(1)}, bf16[4,32,128]{2,1,0:T(8,128)(2,1)S(1)}, u32[]{:S(2)}, u32[]{:S(2)}) collective-permute-start(bf16[4,32,128]{2,1,0:T(8,128)(2,1)S(1)} %constant_dynamic-update-slice_fusion.refs_5_), channel_id=1, source_target_pairs={{0,2},{1,3},{2,4},{3,5},{4,6},{5,7},{6,0},{7,1},{8,10},{9,11},{10,... | collective-permute-start | bytes 98312 | tf_op jit(solution)/shard_map/ppermute | solution.py:350
  12.6 5.2 %collective-permute-start.5 = (bf16[4,32,128]{2,1,0:T(8,128)(2,1)S(1)}, bf16[4,32,128]{2,1,0:T(8,128)(2,1)S(1)}, u32[]{:S(2)}, u32[]{:S(2)}) collective-permute-start(bf16[4,32,128]{2,1,0:T(8,128)(2,1)S(1)} %constant_dynamic-update-slice_fusion.refs_5_), channel_id=1, source_target_pairs={{0,4},{1,5},{2,6},{3,7},{4,0},{5,1},{6,2},{7,3},{8,12},{9,13},{10,... | collective-permute-start | bytes 98312 | tf_op jit(solution)/shard_map/ppermute | solution.py:350
  14.1 3.9 %collective-permute-start.6 = (bf16[4,32,128]{2,1,0:T(8,128)(2,1)S(1)}, bf16[4,32,128]{2,1,0:T(8,128)(2,1)S(1)}, u32[]{:S(2)}, u32[]{:S(2)}) collective-permute-start(bf16[4,32,128]{2,1,0:T(8,128)(2,1)S(1)} %constant_dynamic-update-slice_fusion.refs_5_), channel_id=1, source_target_pairs={{0,6},{1,7},{2,0},{3,1},{4,2},{5,3},{6,4},{7,5},{8,14},{9,15},{10,... | collective-permute-start | bytes 98312 | tf_op jit(solution)/shard_map/ppermute | solution.py:350
  15.6 4.5 %copy-start.1 = (bf16[8,64,256]{2,1,0:T(8,128)(2,1)S(1)}, bf16[8,64,256]{2,1,0:T(8,128)(2,1)}, u32[]{:S(2)}) copy-start(bf16[8,64,256]{2,1,0:T(8,128)(2,1)} %basis.1) | copy-start | bytes 786436
  18.3 1.8 %collective-permute-start.7 = (bf16[3,32,128]{2,1,0:T(8,128)(2,1)S(1)}, bf16[3,32,128]{2,1,0:T(8,128)(2,1)S(1)}, u32[]{:S(2)}, u32[]{:S(2)}) collective-permute-start(bf16[3,32,128]{2,1,0:T(8,128)(2,1)S(1)} %get-tuple-element.39.blocks), channel_id=1, source_target_pairs={{0,1},{1,0},{2,3},{3,2},{4,5},{5,4},{6,7},{7,6},{8,9},{9,8},{10,11... | collective-permute-start | bytes 73736 | tf_op jit(solution)/shard_map/ppermute | solution.py:350

commit v7 on v6

--- a/solution.py
+++ b/solution.py
@@ -296,9 +296,15 @@
     doubled = dot(jnp.concatenate([high_low(pair), high_low(mine)], axis=1), spread[...], NT)
     half = boxes * rank
     rounded = (doubled[:, :half] + doubled[:, half:] + local[...]).astype(BF16)
-    for b in range(boxes):
-        far = dot(rounded[:, b * rank : (b + 1) * rank], basis[b])
-        field[:, b * points : (b + 1) * points] = near[b] + far
+    columns = near.shape[1]
+    lane = lax.broadcasted_iota(jnp.int32, (columns, 2 * rank), 1)
+    for b in range(0, boxes, 2):
+        both = rounded[:, b * rank : (b + 2) * rank]
+        zeros = jnp.zeros_like(both)
+        apart = [jnp.where(lane < rank, both, zeros), jnp.where(lane < rank, zeros, both)]
+        far = dot(jnp.concatenate(apart, axis=0), basis[b : b + 2].reshape(2 * rank, points))
+        field[:, b * points : (b + 1) * points] = near[b] + far[:columns]
+        field[:, (b + 1) * points : (b + 2) * points] = near[b + 1] + far[columns:]
 
 
 SPACES = {"v": pltpu.VMEM, "s": pltpu.SMEM, "h": pl.ANY}

time: 21.7 us -> 21.6 us (level)
  no operation moved by 1% of the time
where the time goes in v7:
time: 21.6 us; the launch traced here: 21.4 us
  starting transfers between devices  13.7 us (63%)
  Pallas kernels  6.55 us (30%)
  between operations  0.8 us (4%)
  waiting for transfers between devices  0.24 us (1%)
    ppermute x9, starting transfers between devices, send(): return lax.ppermute(x, AXES, [(i, target(i)) for i in range(count)])  13.7 us
    pallas_call x6, Pallas kernels, call(): pl.pallas_call(kernel, name=name, out_shape=[jax.ShapeDtypeStruct(shape,...  6.55 us
  transfers between devices with their start and end apart: 9, of which 1 were waited for; matrix products, arithmetic and copies ran while one was open for 0% of the time, Pallas kernels for 25%

profile of v7, /device:TPU:0, one launch (start us, length us, event | category | flops | bytes accessed | tf_op | source)
XLA Modules:
  0.0 21.4 jit_solution(14467558601488973521)
XLA Ops:
  0.0 0.0 copy-start
  0.0 0.5 %collective-permute-start = (bf16[32,2048]{1,0:T(8,128)(2,1)}, bf16[32,2048]{1,0:T(8,128)(2,1)S(1)}, u32[]{:S(2)}, u32[]{:S(2)}) collective-permute-start(bf16[32,2048]{1,0:T(8,128)(2,1)} %vectors_hbm.1), channel_id=1, source_target_pairs={{0,1},{1,2},{2,3},{3,4},{4,5},{5,6},{6,7},{7,8},{8,9},{9,10},{10,1... | collective-permute-start | bytes 393224 | tf_op jit(solution)/shard_map/ppermute | solution.py:356
  0.5 1.8 %leaf.1 = (f32[2,64,64]{2,1,0:T(8,128)S(1)}, bf16[32,2048]{1,0:T(8,128)(2,1)S(1)}, f32[2,64,64]{2,1,0:T(8,128)S(1)}, bf16[1,32,128]{2,1,0:T(8,128)(2,1)S(1)}, f3...) custom-call(f32[2,64,64]{2,1,0:T(8,128)} %transfer_hbm.1, ...), custom_call_target="tpu_custom_call" | custom-call | bytes 458752 | tf_op jit(solution)/shard_map/leaf/pallas_call | solution.py:322
  2.3 2.6 %collective-permute-start.1 = (bf16[1,32,128]{2,1,0:T(8,128)(2,1)S(1)}, bf16[1,32,128]{2,1,0:T(8,128)(2,1)S(1)}, u32[]{:S(2)}, u32[]{:S(2)}) collective-permute-start(bf16[1,32,128]{2,1,0:T(8,128)(2,1)S(1)} %get-tuple-element.28.coeffs), channel_id=1, source_target_pairs={{0,8},{1,9},{2,10},{3,11},{4,12},{5,13},{6,14},{7,15},{8,16},{9,17... | collective-permute-start | bytes 24584 | tf_op jit(solution)/shard_map/ppermute | solution.py:356
  4.9 2.6 %collective-permute-start.2 = (bf16[1,32,128]{2,1,0:T(8,128)(2,1)S(1)}, bf16[1,32,128]{2,1,0:T(8,128)(2,1)S(1)}, u32[]{:S(2)}, u32[]{:S(2)}) collective-permute-start(bf16[1,32,128]{2,1,0:T(8,128)(2,1)S(1)} %get-tuple-element.28.coeffs), channel_id=1, source_target_pairs={{0,16},{1,17},{2,18},{3,19},{4,20},{5,21},{6,22},{7,23},{8,24},{9,... | collective-permute-start | bytes 24584 | tf_op jit(solution)/shard_map/ppermute | solution.py:356
  7.5 1.3 %collective-permute-start.3 = (bf16[1,32,128]{2,1,0:T(8,128)(2,1)S(1)}, bf16[1,32,128]{2,1,0:T(8,128)(2,1)S(1)}, u32[]{:S(2)}, u32[]{:S(2)}) collective-permute-start(bf16[1,32,128]{2,1,0:T(8,128)(2,1)S(1)} %get-tuple-element.28.coeffs), channel_id=1, source_target_pairs={{0,24},{1,25},{2,26},{3,27},{4,28},{5,29},{6,30},{7,31},{8,0},{9,1... | collective-permute-start | bytes 24584 | tf_op jit(solution)/shard_map/ppermute | solution.py:356
  8.8 2.6 %collective-permute-start.8 = (bf16[32,2048]{1,0:T(8,128)(2,1)S(1)}, bf16[32,2048]{1,0:T(8,128)(2,1)S(1)}, u32[]{:S(2)}, u32[]{:S(2)}) collective-permute-start(bf16[32,2048]{1,0:T(8,128)(2,1)S(1)} %get-tuple-element.29.own), channel_id=1, source_target_pairs={{0,31},{1,0},{2,1},{3,2},{4,3},{5,4},{6,5},{7,6},{8,7},{9,8},{10,9... | collective-permute-start | bytes 393224 | tf_op jit(solution)/shard_map/ppermute | solution.py:356
  11.4 0.0 collective-permute-done.before
  11.4 0.0 collective-permute-done.1
  11.4 0.0 collective-permute-done.2
  11.4 0.0 collective-permute-done.3
  11.5 1.2 %collective-permute-start.4 = (bf16[4,32,128]{2,1,0:T(8,128)(2,1)S(1)}, bf16[4,32,128]{2,1,0:T(8,128)(2,1)S(1)}, u32[]{:S(2)}, u32[]{:S(2)}) collective-permute-start(bf16[4,32,128]{2,1,0:T(8,128)(2,1)S(1)} %constant_dynamic-update-slice_fusion.refs_5_), channel_id=1, source_target_pairs={{0,2},{1,3},{2,4},{3,5},{4,6},{5,7},{6,0},{7,1},{8,10},{9,11},{10,... | collective-permute-start | bytes 98312 | tf_op jit(solution)/shard_map/ppermute | solution.py:356
  12.6 1.5 %collective-permute-start.5 = (bf16[4,32,128]{2,1,0:T(8,128)(2,1)S(1)}, bf16[4,32,128]{2,1,0:T(8,128)(2,1)S(1)}, u32[]{:S(2)}, u32[]{:S(2)}) collective-permute-start(bf16[4,32,128]{2,1,0:T(8,128)(2,1)S(1)} %constant_dynamic-update-slice_fusion.refs_5_), channel_id=1, source_target_pairs={{0,4},{1,5},{2,6},{3,7},{4,0},{5,1},{6,2},{7,3},{8,12},{9,13},{10,... | collective-permute-start | bytes 98312 | tf_op jit(solution)/shard_map/ppermute | solution.py:356
  14.1 1.4 %collective-permute-start.6 = (bf16[4,32,128]{2,1,0:T(8,128)(2,1)S(1)}, bf16[4,32,128]{2,1,0:T(8,128)(2,1)S(1)}, u32[]{:S(2)}, u32[]{:S(2)}) collective-permute-start(bf16[4,32,128]{2,1,0:T(8,128)(2,1)S(1)} %constant_dynamic-update-slice_fusion.refs_5_), channel_id=1, source_target_pairs={{0,6},{1,7},{2,0},{3,1},{4,2},{5,3},{6,4},{7,5},{8,14},{9,15},{10,... | collective-permute-start | bytes 98312 | tf_op jit(solution)/shard_map/ppermute | solution.py:356
  15.6 0.0 copy-start.1
  15.6 2.2 %maps.1 = (bf16[2048,128]{1,0:T(8,128)(2,1)S(1)}, bf16[512,128]{1,0:T(8,128)(2,1)S(1)}, s32[3,8,128]{2,1,0:T(8,128)S(1)}, s32[3,32,128]{2,1,0:T(8,128)S(1)}, bf1...) custom-call(s32[1]{0:T(128)} %bitcast.device, ...), custom_call_target="tpu_custom_call" | custom-call | bytes 753820 | tf_op jit(solution)/shard_map/maps/pallas_call | solution.py:322
  17.8 0.0 collective-permute-done.4
  17.8 0.0 collective-permute-done.5
  17.8 0.2 %collective-permute-done.6 = bf16[4,32,128]{2,1,0:T(8,128)(2,1)S(1)} collective-permute-done((bf16[4,32,128]{2,1,0:T(8,128)(2,1)S(1)}, bf16[4,32,128]{2,1,0:T(8,128)(2,1)S(1)}, u32[]{:S(2)}, u32[]{:S(2)}) %collective-permute-start.6) | collective-permute-done | bytes 32800 | tf_op jit(solution)/shard_map/ppermute | solution.py:356
  18.1 0.3 %half.1 = (bf16[3,32,128]{2,1,0:T(8,128)(2,1)S(1)}, f32[32,128]{1,0:T(8,128)S(1)}) custom-call(s32[1]{0:T(128)} %bitcast.device, bf16[16,32,128]{2,1,0:T(8,128)(2,1)S(1)} %constant_dynamic-update-slice_fusion.4.gathered, bf16[2048,128]{1,0:T(8,128)(2,1)S(1)} %get-tuple-element.38.maps), custom_call_target="tpu_custom_call" | custom-call | bytes 655364 | tf_op jit(solution)/shard_map/half/pallas_call | solution.py:322
  18.3 0.1 collective-permute-start.7
  19.1 0.0 collective-permute-done.8.after
  19.1 0.0 copy-done
  19.1 1.0 %near.1 = (f32[8,32,256]{2,1,0:T(8,128)S(1)}, bf16[3,32,128]{2,1,0:T(8,128)(2,1)S(1)}) custom-call(s32[1]{0:T(128)S(6)} %copy.18.live, s32[16]{0:T(128)S(1)} %get-tuple-element.40.targets, s32[16]{0:T(128)S(1)} %get-tuple-element.41.sources, bf16[16,32,256]{2,1,0:T(8,128)(2,1)S(1)} %get-tuple-element.42.window, ...), custom_call_target="tpu_custom_call" | custom-call | bytes 2658436 | tf_op jit(solution)/shard_map/near/pallas_call | solution.py:322
  20.1 0.0 collective-permute-done.7.other
  20.1 0.0 copy-done.1
  20.1 1.3 %field.1 = f32[32,2048]{1,0:T(8,128)} custom-call(bf16[3,32,128]{2,1,0:T(8,128)(2,1)S(1)} %collective-permute-done.7.other, bf16[3,32,128]{2,1,0:T(8,128)(2,1)S(1)} %get-tuple-element.44.links, s32[3,32,128]{2,1,0:T(8,128)S(1)} %get-tuple-element.45.codes, bf16[512,128]{1,0:T(8,128)(2,1)S(1)} %get-tuple-element.46.rest, ...), custom_call_target="tpu_custom_call" | custom-call | bytes 1359872 | tf_op jit(solution)/shard_map/field/pallas_call | solution.py:322
  (9 shorter events, 0.1 us)
Async XLA Ops:
  0.0 19.1 %copy-start = (bf16[16,256,256]{2,1,0:T(8,128)(2,1)S(1)}, bf16[16,256,256]{2,1,0:T(8,128)(2,1)}, u32[]{:S(2)}) copy-start(bf16[16,256,256]{2,1,0:T(8,128)(2,1)} %tiles.1) | copy-start | bytes 6291460
  0.0 11.4 %collective-permute-start = (bf16[32,2048]{1,0:T(8,128)(2,1)}, bf16[32,2048]{1,0:T(8,128)(2,1)S(1)}, u32[]{:S(2)}, u32[]{:S(2)}) collective-permute-start(bf16[32,2048]{1,0:T(8,128)(2,1)} %vectors_hbm.1), channel_id=1, source_target_pairs={{0,1},{1,2},{2,3},{3,4},{4,5},{5,6},{6,7},{7,8},{8,9},{9,10},{10,1... | collective-permute-start | bytes 393224 | tf_op jit(solution)/shard_map/ppermute | solution.py:356
  2.3 9.1 %collective-permute-start.1 = (bf16[1,32,128]{2,1,0:T(8,128)(2,1)S(1)}, bf16[1,32,128]{2,1,0:T(8,128)(2,1)S(1)}, u32[]{:S(2)}, u32[]{:S(2)}) collective-permute-start(bf16[1,32,128]{2,1,0:T(8,128)(2,1)S(1)} %get-tuple-element.28.coeffs), channel_id=1, source_target_pairs={{0,8},{1,9},{2,10},{3,11},{4,12},{5,13},{6,14},{7,15},{8,16},{9,17... | collective-permute-start | bytes 24584 | tf_op jit(solution)/shard_map/ppermute | solution.py:356
  4.9 6.6 %collective-permute-start.2 = (bf16[1,32,128]{2,1,0:T(8,128)(2,1)S(1)}, bf16[1,32,128]{2,1,0:T(8,128)(2,1)S(1)}, u32[]{:S(2)}, u32[]{:S(2)}) collective-permute-start(bf16[1,32,128]{2,1,0:T(8,128)(2,1)S(1)} %get-tuple-element.28.coeffs), channel_id=1, source_target_pairs={{0,16},{1,17},{2,18},{3,19},{4,20},{5,21},{6,22},{7,23},{8,24},{9,... | collective-permute-start | bytes 24584 | tf_op jit(solution)/shard_map/ppermute | solution.py:356
  7.5 4.0 %collective-permute-start.3 = (bf16[1,32,128]{2,1,0:T(8,128)(2,1)S(1)}, bf16[1,32,128]{2,1,0:T(8,128)(2,1)S(1)}, u32[]{:S(2)}, u32[]{:S(2)}) collective-permute-start(bf16[1,32,128]{2,1,0:T(8,128)(2,1)S(1)} %get-tuple-element.28.coeffs), channel_id=1, source_target_pairs={{0,24},{1,25},{2,26},{3,27},{4,28},{5,29},{6,30},{7,31},{8,0},{9,1... | collective-permute-start | bytes 24584 | tf_op jit(solution)/shard_map/ppermute | solution.py:356
  8.8 10.3 %collective-permute-start.8 = (bf16[32,2048]{1,0:T(8,128)(2,1)S(1)}, bf16[32,2048]{1,0:T(8,128)(2,1)S(1)}, u32[]{:S(2)}, u32[]{:S(2)}) collective-permute-start(bf16[32,2048]{1,0:T(8,128)(2,1)S(1)} %get-tuple-element.29.own), channel_id=1, source_target_pairs={{0,31},{1,0},{2,1},{3,2},{4,3},{5,4},{6,5},{7,6},{8,7},{9,8},{10,9... | collective-permute-start | bytes 393224 | tf_op jit(solution)/shard_map/ppermute | solution.py:356
  11.5 6.3 %collective-permute-start.4 = (bf16[4,32,128]{2,1,0:T(8,128)(2,1)S(1)}, bf16[4,32,128]{2,1,0:T(8,128)(2,1)S(1)}, u32[]{:S(2)}, u32[]{:S(2)}) collective-permute-start(bf16[4,32,128]{2,1,0:T(8,128)(2,1)S(1)} %constant_dynamic-update-slice_fusion.refs_5_), channel_id=1, source_target_pairs={{0,2},{1,3},{2,4},{3,5},{4,6},{5,7},{6,0},{7,1},{8,10},{9,11},{10,... | collective-permute-start | bytes 98312 | tf_op jit(solution)/shard_map/ppermute | solution.py:356
  12.6 5.2 %collective-permute-start.5 = (bf16[4,32,128]{2,1,0:T(8,128)(2,1)S(1)}, bf16[4,32,128]{2,1,0:T(8,128)(2,1)S(1)}, u32[]{:S(2)}, u32[]{:S(2)}) collective-permute-start(bf16[4,32,128]{2,1,0:T(8,128)(2,1)S(1)} %constant_dynamic-update-slice_fusion.refs_5_), channel_id=1, source_target_pairs={{0,4},{1,5},{2,6},{3,7},{4,0},{5,1},{6,2},{7,3},{8,12},{9,13},{10,... | collective-permute-start | bytes 98312 | tf_op jit(solution)/shard_map/ppermute | solution.py:356
  14.1 3.9 %collective-permute-start.6 = (bf16[4,32,128]{2,1,0:T(8,128)(2,1)S(1)}, bf16[4,32,128]{2,1,0:T(8,128)(2,1)S(1)}, u32[]{:S(2)}, u32[]{:S(2)}) collective-permute-start(bf16[4,32,128]{2,1,0:T(8,128)(2,1)S(1)} %constant_dynamic-update-slice_fusion.refs_5_), channel_id=1, source_target_pairs={{0,6},{1,7},{2,0},{3,1},{4,2},{5,3},{6,4},{7,5},{8,14},{9,15},{10,... | collective-permute-start | bytes 98312 | tf_op jit(solution)/shard_map/ppermute | solution.py:356
  15.6 4.5 %copy-start.1 = (bf16[8,64,256]{2,1,0:T(8,128)(2,1)S(1)}, bf16[8,64,256]{2,1,0:T(8,128)(2,1)}, u32[]{:S(2)}) copy-start(bf16[8,64,256]{2,1,0:T(8,128)(2,1)} %basis.1) | copy-start | bytes 786436
  18.3 1.8 %collective-permute-start.7 = (bf16[3,32,128]{2,1,0:T(8,128)(2,1)S(1)}, bf16[3,32,128]{2,1,0:T(8,128)(2,1)S(1)}, u32[]{:S(2)}, u32[]{:S(2)}) collective-permute-start(bf16[3,32,128]{2,1,0:T(8,128)(2,1)S(1)} %get-tuple-element.39.blocks), channel_id=1, source_target_pairs={{0,1},{1,0},{2,3},{3,2},{4,5},{5,4},{6,7},{7,6},{8,9},{9,8},{10,11... | collective-permute-start | bytes 73736 | tf_op jit(solution)/shard_map/ppermute | solution.py:356

commit v8 on v7

--- a/solution.py
+++ b/solution.py
@@ -93,7 +93,9 @@
     *paths, basis, sems = refs
     boxes, rank, points = basis.shape
     steps = boxes.bit_length() - 1
-    pairs = ((transfer_hbm, transfer), (vectors_hbm, vectors), (basis_hbm, basis), (sibling_hbm, sibling))
+    first, second = pl.ds(0, boxes // 2), pl.ds(boxes // 2, boxes // 2)
+    pairs = [(transfer_hbm, transfer), (vectors_hbm, vectors), (basis_hbm.at[first], basis.at[first])]
+    pairs += [(sibling_hbm, sibling), (basis_hbm.at[second], basis.at[second])]
     copies = start_copies(pairs, sems)
     copies[0].wait()
     t0, t1 = twice(transfer[0]), twice(transfer[1])
@@ -103,6 +105,7 @@
         if height == steps:
             copies[1].wait()
             copies[2].wait()
+            copies[4].wait()
             high, low = [], []
             for b in range(boxes):
                 coeffs = dot(vectors[:, b * points : (b + 1) * points], basis[b], NT)
@@ -374,7 +377,7 @@
             ("v", (boxes, columns, rank), F32),
             *(("v", shape, F32) for shape in path_shapes),
         ),
-        scratch=(pltpu.VMEM(leaf_basis.shape, BF16), dma((4,))),
+        scratch=(pltpu.VMEM(leaf_basis.shape, BF16), dma((5,))),
     )
     device = lax.axis_index(AXES).astype(ints).reshape(1)
     window, passed = call(

time: 21.6 us -> 21.6 us (level)
  no operation moved by 1% of the time
where the time goes in v8:
time: 21.6 us; the launch traced here: 21.4 us
  starting transfers between devices  13.7 us (63%)
  Pallas kernels  6.56 us (30%)
  between operations  0.8 us (4%)
  waiting for transfers between devices  0.24 us (1%)
    ppermute x9, starting transfers between devices, send(): return lax.ppermute(x, AXES, [(i, target(i)) for i in range(count)])  13.7 us
    pallas_call x6, Pallas kernels, call(): pl.pallas_call(kernel, name=name, out_shape=[jax.ShapeDtypeStruct(shape,...  6.56 us
  transfers between devices with their start and end apart: 9, of which 1 were waited for; matrix products, arithmetic and copies ran while one was open for 0% of the time, Pallas kernels for 25%

profile of v8, /device:TPU:0, one launch (start us, length us, event | category | flops | bytes accessed | tf_op | source)
XLA Modules:
  0.0 21.4 jit_solution(4874920127062260961)
XLA Ops:
  0.0 0.0 copy-start
  0.0 0.5 %collective-permute-start = (bf16[32,2048]{1,0:T(8,128)(2,1)}, bf16[32,2048]{1,0:T(8,128)(2,1)S(1)}, u32[]{:S(2)}, u32[]{:S(2)}) collective-permute-start(bf16[32,2048]{1,0:T(8,128)(2,1)} %vectors_hbm.1), channel_id=1, source_target_pairs={{0,1},{1,2},{2,3},{3,4},{4,5},{5,6},{6,7},{7,8},{8,9},{9,10},{10,1... | collective-permute-start | bytes 393224 | tf_op jit(solution)/shard_map/ppermute | solution.py:359
  0.5 1.8 %leaf.1 = (f32[2,64,64]{2,1,0:T(8,128)S(1)}, bf16[32,2048]{1,0:T(8,128)(2,1)S(1)}, f32[2,64,64]{2,1,0:T(8,128)S(1)}, bf16[1,32,128]{2,1,0:T(8,128)(2,1)S(1)}, f3...) custom-call(f32[2,64,64]{2,1,0:T(8,128)} %transfer_hbm.1, ...), custom_call_target="tpu_custom_call" | custom-call | bytes 458752 | tf_op jit(solution)/shard_map/leaf/pallas_call | solution.py:325
  2.3 2.6 %collective-permute-start.1 = (bf16[1,32,128]{2,1,0:T(8,128)(2,1)S(1)}, bf16[1,32,128]{2,1,0:T(8,128)(2,1)S(1)}, u32[]{:S(2)}, u32[]{:S(2)}) collective-permute-start(bf16[1,32,128]{2,1,0:T(8,128)(2,1)S(1)} %get-tuple-element.28.coeffs), channel_id=1, source_target_pairs={{0,8},{1,9},{2,10},{3,11},{4,12},{5,13},{6,14},{7,15},{8,16},{9,17... | collective-permute-start | bytes 24584 | tf_op jit(solution)/shard_map/ppermute | solution.py:359
  4.9 2.6 %collective-permute-start.2 = (bf16[1,32,128]{2,1,0:T(8,128)(2,1)S(1)}, bf16[1,32,128]{2,1,0:T(8,128)(2,1)S(1)}, u32[]{:S(2)}, u32[]{:S(2)}) collective-permute-start(bf16[1,32,128]{2,1,0:T(8,128)(2,1)S(1)} %get-tuple-element.28.coeffs), channel_id=1, source_target_pairs={{0,16},{1,17},{2,18},{3,19},{4,20},{5,21},{6,22},{7,23},{8,24},{9,... | collective-permute-start | bytes 24584 | tf_op jit(solution)/shard_map/ppermute | solution.py:359
  7.5 1.3 %collective-permute-start.3 = (bf16[1,32,128]{2,1,0:T(8,128)(2,1)S(1)}, bf16[1,32,128]{2,1,0:T(8,128)(2,1)S(1)}, u32[]{:S(2)}, u32[]{:S(2)}) collective-permute-start(bf16[1,32,128]{2,1,0:T(8,128)(2,1)S(1)} %get-tuple-element.28.coeffs), channel_id=1, source_target_pairs={{0,24},{1,25},{2,26},{3,27},{4,28},{5,29},{6,30},{7,31},{8,0},{9,1... | collective-permute-start | bytes 24584 | tf_op jit(solution)/shard_map/ppermute | solution.py:359
  8.8 2.6 %collective-permute-start.8 = (bf16[32,2048]{1,0:T(8,128)(2,1)S(1)}, bf16[32,2048]{1,0:T(8,128)(2,1)S(1)}, u32[]{:S(2)}, u32[]{:S(2)}) collective-permute-start(bf16[32,2048]{1,0:T(8,128)(2,1)S(1)} %get-tuple-element.29.own), channel_id=1, source_target_pairs={{0,31},{1,0},{2,1},{3,2},{4,3},{5,4},{6,5},{7,6},{8,7},{9,8},{10,9... | collective-permute-start | bytes 393224 | tf_op jit(solution)/shard_map/ppermute | solution.py:359
  11.4 0.0 collective-permute-done.before
  11.4 0.0 collective-permute-done.1
  11.4 0.0 collective-permute-done.2
  11.5 0.0 collective-permute-done.3
  11.5 1.2 %collective-permute-start.4 = (bf16[4,32,128]{2,1,0:T(8,128)(2,1)S(1)}, bf16[4,32,128]{2,1,0:T(8,128)(2,1)S(1)}, u32[]{:S(2)}, u32[]{:S(2)}) collective-permute-start(bf16[4,32,128]{2,1,0:T(8,128)(2,1)S(1)} %constant_dynamic-update-slice_fusion.refs_5_), channel_id=1, source_target_pairs={{0,2},{1,3},{2,4},{3,5},{4,6},{5,7},{6,0},{7,1},{8,10},{9,11},{10,... | collective-permute-start | bytes 98312 | tf_op jit(solution)/shard_map/ppermute | solution.py:359
  12.6 1.5 %collective-permute-start.5 = (bf16[4,32,128]{2,1,0:T(8,128)(2,1)S(1)}, bf16[4,32,128]{2,1,0:T(8,128)(2,1)S(1)}, u32[]{:S(2)}, u32[]{:S(2)}) collective-permute-start(bf16[4,32,128]{2,1,0:T(8,128)(2,1)S(1)} %constant_dynamic-update-slice_fusion.refs_5_), channel_id=1, source_target_pairs={{0,4},{1,5},{2,6},{3,7},{4,0},{5,1},{6,2},{7,3},{8,12},{9,13},{10,... | collective-permute-start | bytes 98312 | tf_op jit(solution)/shard_map/ppermute | solution.py:359
  14.1 1.4 %collective-permute-start.6 = (bf16[4,32,128]{2,1,0:T(8,128)(2,1)S(1)}, bf16[4,32,128]{2,1,0:T(8,128)(2,1)S(1)}, u32[]{:S(2)}, u32[]{:S(2)}) collective-permute-start(bf16[4,32,128]{2,1,0:T(8,128)(2,1)S(1)} %constant_dynamic-update-slice_fusion.refs_5_), channel_id=1, source_target_pairs={{0,6},{1,7},{2,0},{3,1},{4,2},{5,3},{6,4},{7,5},{8,14},{9,15},{10,... | collective-permute-start | bytes 98312 | tf_op jit(solution)/shard_map/ppermute | solution.py:359
  15.6 0.0 copy-start.1
  15.6 2.2 %maps.1 = (bf16[2048,128]{1,0:T(8,128)(2,1)S(1)}, bf16[512,128]{1,0:T(8,128)(2,1)S(1)}, s32[3,8,128]{2,1,0:T(8,128)S(1)}, s32[3,32,128]{2,1,0:T(8,128)S(1)}, bf1...) custom-call(s32[1]{0:T(128)} %bitcast.device, ...), custom_call_target="tpu_custom_call" | custom-call | bytes 753820 | tf_op jit(solution)/shard_map/maps/pallas_call | solution.py:325
  17.8 0.0 collective-permute-done.4
  17.8 0.0 collective-permute-done.5
  17.8 0.2 %collective-permute-done.6 = bf16[4,32,128]{2,1,0:T(8,128)(2,1)S(1)} collective-permute-done((bf16[4,32,128]{2,1,0:T(8,128)(2,1)S(1)}, bf16[4,32,128]{2,1,0:T(8,128)(2,1)S(1)}, u32[]{:S(2)}, u32[]{:S(2)}) %collective-permute-start.6) | collective-permute-done | bytes 32800 | tf_op jit(solution)/shard_map/ppermute | solution.py:359
  18.1 0.3 %half.1 = (bf16[3,32,128]{2,1,0:T(8,128)(2,1)S(1)}, f32[32,128]{1,0:T(8,128)S(1)}) custom-call(s32[1]{0:T(128)} %bitcast.device, bf16[16,32,128]{2,1,0:T(8,128)(2,1)S(1)} %constant_dynamic-update-slice_fusion.4.gathered, bf16[2048,128]{1,0:T(8,128)(2,1)S(1)} %get-tuple-element.38.maps), custom_call_target="tpu_custom_call" | custom-call | bytes 655364 | tf_op jit(solution)/shard_map/half/pallas_call | solution.py:325
  18.3 0.1 collective-permute-start.7
  19.1 0.0 collective-permute-done.8.after
  19.1 0.0 copy-done
  19.1 1.0 %near.1 = (f32[8,32,256]{2,1,0:T(8,128)S(1)}, bf16[3,32,128]{2,1,0:T(8,128)(2,1)S(1)}) custom-call(s32[1]{0:T(128)S(6)} %copy.18.live, s32[16]{0:T(128)S(1)} %get-tuple-element.40.targets, s32[16]{0:T(128)S(1)} %get-tuple-element.41.sources, bf16[16,32,256]{2,1,0:T(8,128)(2,1)S(1)} %get-tuple-element.42.window, ...), custom_call_target="tpu_custom_call" | custom-call | bytes 2658436 | tf_op jit(solution)/shard_map/near/pallas_call | solution.py:325
  20.1 0.0 collective-permute-done.7.other
  20.1 0.0 copy-done.1
  20.1 1.3 %field.1 = f32[32,2048]{1,0:T(8,128)} custom-call(bf16[3,32,128]{2,1,0:T(8,128)(2,1)S(1)} %collective-permute-done.7.other, bf16[3,32,128]{2,1,0:T(8,128)(2,1)S(1)} %get-tuple-element.44.links, s32[3,32,128]{2,1,0:T(8,128)S(1)} %get-tuple-element.45.codes, bf16[512,128]{1,0:T(8,128)(2,1)S(1)} %get-tuple-element.46.rest, ...), custom_call_target="tpu_custom_call" | custom-call | bytes 1359872 | tf_op jit(solution)/shard_map/field/pallas_call | solution.py:325
  (9 shorter events, 0.1 us)
Async XLA Ops:
  0.0 19.1 %copy-start = (bf16[16,256,256]{2,1,0:T(8,128)(2,1)S(1)}, bf16[16,256,256]{2,1,0:T(8,128)(2,1)}, u32[]{:S(2)}) copy-start(bf16[16,256,256]{2,1,0:T(8,128)(2,1)} %tiles.1) | copy-start | bytes 6291460
  0.0 11.4 %collective-permute-start = (bf16[32,2048]{1,0:T(8,128)(2,1)}, bf16[32,2048]{1,0:T(8,128)(2,1)S(1)}, u32[]{:S(2)}, u32[]{:S(2)}) collective-permute-start(bf16[32,2048]{1,0:T(8,128)(2,1)} %vectors_hbm.1), channel_id=1, source_target_pairs={{0,1},{1,2},{2,3},{3,4},{4,5},{5,6},{6,7},{7,8},{8,9},{9,10},{10,1... | collective-permute-start | bytes 393224 | tf_op jit(solution)/shard_map/ppermute | solution.py:359
  2.3 9.1 %collective-permute-start.1 = (bf16[1,32,128]{2,1,0:T(8,128)(2,1)S(1)}, bf16[1,32,128]{2,1,0:T(8,128)(2,1)S(1)}, u32[]{:S(2)}, u32[]{:S(2)}) collective-permute-start(bf16[1,32,128]{2,1,0:T(8,128)(2,1)S(1)} %get-tuple-element.28.coeffs), channel_id=1, source_target_pairs={{0,8},{1,9},{2,10},{3,11},{4,12},{5,13},{6,14},{7,15},{8,16},{9,17... | collective-permute-start | bytes 24584 | tf_op jit(solution)/shard_map/ppermute | solution.py:359
  4.9 6.6 %collective-permute-start.2 = (bf16[1,32,128]{2,1,0:T(8,128)(2,1)S(1)}, bf16[1,32,128]{2,1,0:T(8,128)(2,1)S(1)}, u32[]{:S(2)}, u32[]{:S(2)}) collective-permute-start(bf16[1,32,128]{2,1,0:T(8,128)(2,1)S(1)} %get-tuple-element.28.coeffs), channel_id=1, source_target_pairs={{0,16},{1,17},{2,18},{3,19},{4,20},{5,21},{6,22},{7,23},{8,24},{9,... | collective-permute-start | bytes 24584 | tf_op jit(solution)/shard_map/ppermute | solution.py:359
  7.5 4.0 %collective-permute-start.3 = (bf16[1,32,128]{2,1,0:T(8,128)(2,1)S(1)}, bf16[1,32,128]{2,1,0:T(8,128)(2,1)S(1)}, u32[]{:S(2)}, u32[]{:S(2)}) collective-permute-start(bf16[1,32,128]{2,1,0:T(8,128)(2,1)S(1)} %get-tuple-element.28.coeffs), channel_id=1, source_target_pairs={{0,24},{1,25},{2,26},{3,27},{4,28},{5,29},{6,30},{7,31},{8,0},{9,1... | collective-permute-start | bytes 24584 | tf_op jit(solution)/shard_map/ppermute | solution.py:359
  8.8 10.3 %collective-permute-start.8 = (bf16[32,2048]{1,0:T(8,128)(2,1)S(1)}, bf16[32,2048]{1,0:T(8,128)(2,1)S(1)}, u32[]{:S(2)}, u32[]{:S(2)}) collective-permute-start(bf16[32,2048]{1,0:T(8,128)(2,1)S(1)} %get-tuple-element.29.own), channel_id=1, source_target_pairs={{0,31},{1,0},{2,1},{3,2},{4,3},{5,4},{6,5},{7,6},{8,7},{9,8},{10,9... | collective-permute-start | bytes 393224 | tf_op jit(solution)/shard_map/ppermute | solution.py:359
  11.5 6.3 %collective-permute-start.4 = (bf16[4,32,128]{2,1,0:T(8,128)(2,1)S(1)}, bf16[4,32,128]{2,1,0:T(8,128)(2,1)S(1)}, u32[]{:S(2)}, u32[]{:S(2)}) collective-permute-start(bf16[4,32,128]{2,1,0:T(8,128)(2,1)S(1)} %constant_dynamic-update-slice_fusion.refs_5_), channel_id=1, source_target_pairs={{0,2},{1,3},{2,4},{3,5},{4,6},{5,7},{6,0},{7,1},{8,10},{9,11},{10,... | collective-permute-start | bytes 98312 | tf_op jit(solution)/shard_map/ppermute | solution.py:359
  12.6 5.2 %collective-permute-start.5 = (bf16[4,32,128]{2,1,0:T(8,128)(2,1)S(1)}, bf16[4,32,128]{2,1,0:T(8,128)(2,1)S(1)}, u32[]{:S(2)}, u32[]{:S(2)}) collective-permute-start(bf16[4,32,128]{2,1,0:T(8,128)(2,1)S(1)} %constant_dynamic-update-slice_fusion.refs_5_), channel_id=1, source_target_pairs={{0,4},{1,5},{2,6},{3,7},{4,0},{5,1},{6,2},{7,3},{8,12},{9,13},{10,... | collective-permute-start | bytes 98312 | tf_op jit(solution)/shard_map/ppermute | solution.py:359
  14.1 3.9 %collective-permute-start.6 = (bf16[4,32,128]{2,1,0:T(8,128)(2,1)S(1)}, bf16[4,32,128]{2,1,0:T(8,128)(2,1)S(1)}, u32[]{:S(2)}, u32[]{:S(2)}) collective-permute-start(bf16[4,32,128]{2,1,0:T(8,128)(2,1)S(1)} %constant_dynamic-update-slice_fusion.refs_5_), channel_id=1, source_target_pairs={{0,6},{1,7},{2,0},{3,1},{4,2},{5,3},{6,4},{7,5},{8,14},{9,15},{10,... | collective-permute-start | bytes 98312 | tf_op jit(solution)/shard_map/ppermute | solution.py:359
  15.6 4.5 %copy-start.1 = (bf16[8,64,256]{2,1,0:T(8,128)(2,1)S(1)}, bf16[8,64,256]{2,1,0:T(8,128)(2,1)}, u32[]{:S(2)}) copy-start(bf16[8,64,256]{2,1,0:T(8,128)(2,1)} %basis.1) | copy-start | bytes 786436
  18.3 1.8 %collective-permute-start.7 = (bf16[3,32,128]{2,1,0:T(8,128)(2,1)S(1)}, bf16[3,32,128]{2,1,0:T(8,128)(2,1)S(1)}, u32[]{:S(2)}, u32[]{:S(2)}) collective-permute-start(bf16[3,32,128]{2,1,0:T(8,128)(2,1)S(1)} %get-tuple-element.39.blocks), channel_id=1, source_target_pairs={{0,1},{1,0},{2,3},{3,2},{4,5},{5,4},{6,7},{7,6},{8,9},{9,8},{10,11... | collective-permute-start | bytes 73736 | tf_op jit(solution)/shard_map/ppermute | solution.py:359
